TPU v7x, 32 devices: a whole 2x2x4 slice. The times are simulated.
32 devices in a mesh: rep: 8 (over z, x), shard: 4 (over y, core).
Axes of the slice: x: 2, y: 2, z: 4, core: 2. Of those that a mesh axis runs over, the one named last changes fastest.
Arguments:
- grads: float32 [8, 8, 8, 5120], P('rep', 'shard'), may hold values from -1000 to 1000
- weight: float32 [8, 8, 5120], P('shard'), may hold values from -6 to 6
- moment_one: float32 [8, 8, 5120], P('shard', 'rep'), may hold values from -6 to 6
- moment_two: float32 [8, 8, 5120], P('shard', 'rep'), may hold values from 0.1 to 3
Outputs:
- new_weight: float32 [8, 8, 5120], P('shard')
- new_moment_one: float32 [8, 8, 5120], P('shard', 'rep')
- new_moment_two: float32 [8, 8, 5120], P('shard', 'rep')
All inputs are finite; a program needn't handle non-finite values.
Results may differ from a plain program's by a relative error of at most 0.0003.
Values sent between devices are 32-bit elements; how exact they have to be, the bound alone decides.
No kernel may reach another device: no remote copies, remote signals or barrier semaphores. Data moves between devices by JAX's collectives and lax.ppermute only.
A program may use at most 64 MiB of HBM per device.

v0:
```python
import jax
import jax.numpy as jnp
from jax import lax
from jax.sharding import PartitionSpec as P

STEP = 100


def trimmed_block(block, trim_count):
    count = block.shape[0]
    order = jnp.arange(count, dtype=jnp.int32)
    lower = block[None, :, :] < block[:, None, :]
    equal = (block[None, :, :] == block[:, None, :]) & (order[None, :, None] < order[:, None, None])
    rank = jnp.sum((lower | equal).astype(jnp.int32), axis=1)
    keep = (rank >= trim_count) & (rank < count - trim_count)
    kept = jnp.sum(jnp.where(keep, block, jnp.zeros_like(block)), axis=0)
    return kept / (count - 2 * trim_count)


def trimmed_mean(values, trim_count):
    count, total = values.shape
    width = 512
    blocks = values.reshape(count, total // width, width).transpose(1, 0, 2)
    result = lax.map(lambda item: trimmed_block(item, trim_count), blocks)
    return result.reshape(total)


def trimmed_rows(received):
    count = received.shape[0]
    flat = received.reshape(count, -1)
    return trimmed_mean(flat, count // 8).reshape(received.shape[1:])


def on_device(grads, weight, moment_one, moment_two):
    params = weight.shape[0] * lax.axis_size("shard") * weight.shape[1] * weight.shape[2]
    received = lax.all_to_all(grads, "rep", split_axis=2, concat_axis=0, tiled=True)
    trimmed = trimmed_rows(received)
    squares = jnp.sum(trimmed * trimmed)
    total = lax.psum(squares, ("rep", "shard"))
    factor = jnp.minimum(1.0, 1.0 / jnp.sqrt(total / params + 1e-12))
    clipped = factor * trimmed
    new_one = 0.9 * moment_one + 0.1 * clipped
    new_two = 0.95 * moment_two + 0.05 * clipped * clipped
    update = new_one / (1.0 - 0.9**STEP) / (jnp.sqrt(new_two / (1.0 - 0.95**STEP)) + 1e-08)
    owned = lax.dynamic_slice_in_dim(
        weight, lax.axis_index("rep") * moment_one.shape[1], moment_one.shape[1], 1
    )
    owned_new = owned - 0.05 * (update + 0.1 * owned)
    new_weight = lax.all_gather(owned_new, "rep", axis=1, tiled=True)
    return (new_weight, new_one, new_two)


def solution(mesh):
    return jax.shard_map(
        on_device,
        mesh=mesh,
        in_specs=(
            P("rep", "shard", None, None),
            P("shard", None, None),
            P("shard", "rep", None),
            P("shard", "rep", None),
        ),
        out_specs=(P("shard", None, None), P("shard", "rep", None), P("shard", "rep", None)),
        check_vma=False,
    )
```

profile of v0, /device:TPU:0, one launch (start us, length us, event | category | flops | bytes accessed | tf_op | source)
XLA Modules:
  0.0 100.5 jit_solution(9916965587327509337)
XLA Ops:
  0.6 0.0 copy-start
  0.6 2.0 %copy.25 = f32[1,2,8,5120]{3,1,0,2:T(2,128)} copy(f32[1,2,8,5120]{3,2,1,0:T(8,128)} %param.6) | data formatting | bytes 655360 | tf_op args[0]
  2.6 7.3 %all-to-all-start = ((f32[1,2,8,5120]{3,1,0,2:T(2,128)}), f32[1,2,8,5120]{3,1,0,2:T(2,128)S(1)}, u32[]{:S(2)}, u32[]{:S(2)}) async-start(f32[1,2,8,5120]{3,1,0,2:T(2,128)} %copy.25), calls=%async_computation | async-start | bytes 655360 | tf_op jit(solution)/shard_map/all_to_all | solution.py:36
  9.9 10.3 %all-to-all-done = f32[1,2,8,5120]{3,1,0,2:T(2,128)S(1)} async-done(((f32[1,2,8,5120]{3,1,0,2:T(2,128)}), f32[1,2,8,5120]{3,1,0,2:T(2,128)S(1)}, u32[]{:S(2)}, u32[]{:S(2)}) %all-to-all-start) | async-done | bytes 327712 | tf_op jit(solution)/shard_map/all_to_all | solution.py:36
  20.2 0.3 reshape_reshape.4
  20.5 5.7 %while.10 = (s32[]{:T(128)}, f32[20,512]{1,0:T(8,128)S(1)}, f32[20,8,512]{2,0,1:T(8,128)S(1)}, s32[]{:T(128)}, s32[]{:T(128)}) while((s32[]{:T(128)}, f32[20,512]{1,0:T(8,128)S(1)}, f32[20,8,512]{2,0,1:T(8,128)S(1)}, s32[]{:T(128)}, s32[]{:T(128)}) %tuple.32), condition=%wide.region_3.4_spmd, body=%wide.region_0.3_spmd.sunk | while | flops 213058 | bytes 141509 | solution.py:24
  20.5 0.1 convert_reduce_fusion.2
  20.7 0.1 dynamic_update_slice.5
  20.8 0.1 convert_reduce_fusion.2
  21.0 0.1 dynamic_update_slice.5
  21.1 0.1 convert_reduce_fusion.2
  21.3 0.1 dynamic_update_slice.5
  21.4 0.1 convert_reduce_fusion.2
  21.6 0.1 dynamic_update_slice.5
  21.7 0.1 convert_reduce_fusion.2
  21.8 0.1 dynamic_update_slice.5
  22.0 0.1 convert_reduce_fusion.2
  22.1 0.1 dynamic_update_slice.5
  22.3 0.1 convert_reduce_fusion.2
  22.4 0.1 dynamic_update_slice.5
  22.6 0.1 convert_reduce_fusion.2
  22.7 0.1 dynamic_update_slice.5
  22.8 0.1 convert_reduce_fusion.2
  23.0 0.1 dynamic_update_slice.5
  23.1 0.1 convert_reduce_fusion.2
  23.3 0.1 dynamic_update_slice.5
  23.4 0.1 convert_reduce_fusion.2
  23.6 0.1 dynamic_update_slice.5
  23.7 0.1 convert_reduce_fusion.2
  23.8 0.1 dynamic_update_slice.5
  24.0 0.1 convert_reduce_fusion.2
  24.1 0.1 dynamic_update_slice.5
  24.3 0.1 convert_reduce_fusion.2
  24.4 0.1 dynamic_update_slice.5
  24.6 0.1 convert_reduce_fusion.2
  24.7 0.1 dynamic_update_slice.5
  24.8 0.1 convert_reduce_fusion.2
  25.0 0.1 dynamic_update_slice.5
  25.1 0.1 convert_reduce_fusion.2
  25.3 0.1 dynamic_update_slice.5
  25.4 0.1 convert_reduce_fusion.2
  25.6 0.1 dynamic_update_slice.5
  25.7 0.1 convert_reduce_fusion.2
  25.9 0.1 dynamic_update_slice.5
  26.0 0.1 convert_reduce_fusion.2
  26.1 0.1 dynamic_update_slice.5
  26.2 0.6 multiply_reduce_fusion
  26.8 0.0 copy-done
  26.9 38.9 %psum.7 = f32[]{:T(128)} all-reduce(f32[]{:T(128)} %multiply_reduce_fusion), channel_id=1, replica_groups=mesh['rep'=8,'shard'=4] {'rep','shard'}, use_global_device_ids=true, to_apply=%region_5.6 | all-reduce | flops 1 | bytes 8 | tf_op jit(solution)/shard_map/psum | solution.py:39
  66.5 0.0 copy-start.1
  66.5 0.0 copy-start.2
  66.6 0.7 copy-done.1
  67.3 0.0 copy-done.2
  67.3 0.2 multiply_subtract_fusion
  67.5 30.9 %all_gather.3 = f32[2,8,5120]{2,0,1:T(2,128)S(1)} all-gather(f32[2,1,5120]{2,0,1:T(2,128)S(1)} %get-tuple-element.42), channel_id=1, replica_groups=mesh['rep'=8,'shard'=4] {'rep'}, dimensions={1}, use_global_device_ids=true | all-gather | bytes 368640 | tf_op jit(solution)/shard_map/all_gather | solution.py:49
  98.4 0.8 copy.28
  99.2 0.7 copy.29
  99.8 0.7 copy.30
  (104 shorter events, 1.2 us)
Async XLA Ops:
  0.6 26.2 %copy-start = (f32[2,8,5120]{2,1,0:T(8,128)S(1)}, f32[2,8,5120]{2,1,0:T(8,128)}, u32[]{:S(2)}) copy-start(f32[2,8,5120]{2,1,0:T(8,128)} %param.7) | copy-start | bytes 983044
  2.6 17.6 %all-to-all-start = ((f32[1,2,8,5120]{3,1,0,2:T(2,128)}), f32[1,2,8,5120]{3,1,0,2:T(2,128)S(1)}, u32[]{:S(2)}, u32[]{:S(2)}) async-start(f32[1,2,8,5120]{3,1,0,2:T(2,128)} %copy.25), calls=%async_computation | async-start | bytes 655360 | tf_op jit(solution)/shard_map/all_to_all | solution.py:36
  66.5 0.8 copy-start.1
  66.5 0.8 copy-start.2
where the time goes:
time: 101 us
  blocking collectives  69.8 us (69%)
  waiting for transfers between devices  10.3 us (10%)
  starting transfers between devices  7.25 us (7%)
  local copies, waits for them, and re-layouts  6.93 us (7%)
  other arithmetic  3.69 us (4%)
  between operations  1.38 us (1%)
  loops' own time  1.1 us (1%)
    psum x1, blocking collectives, on_device(): total = lax.psum(squares, ('rep', 'shard'))  38.9 us
    all_gather x1, blocking collectives, on_device(): new_weight = lax.all_gather(owned_new, 'rep', axis=1, tiled=True)  30.9 us
    all_to_all x1, waiting for transfers between devices, on_device(): lax.all_to_all(grads, 'rep', split_axis=2, concat_axis=0, tiled=True)  10.3 us
    all_to_all x1, starting transfers between devices, on_device(): lax.all_to_all(grads, 'rep', split_axis=2, concat_axis=0, tiled=True)  7.25 us
    unnamed x10, local copies, waits for them, and re-layouts  4.9 us
    reduce_sum x20, other arithmetic, trimmed_block(): rank = jnp.sum((lower | equal).astype(jnp.int32), axis=1)  2.25 us
  transfers between devices with their start and end apart: 1, of which 1 were waited for; matrix products, arithmetic and copies ran while one was open for 0% of the time, Pallas kernels for 0%

commit v1 on v0

v1 whole, which is shorter than its diff:
```python
import functools

import jax
import jax.numpy as jnp
from jax import lax
from jax.experimental import pallas as pl
from jax.experimental.pallas import tpu as pltpu
from jax.sharding import PartitionSpec as P

STEP = 100
LANES = 128
SUB = 8
VMEM = pl.BlockSpec(memory_space=pltpu.VMEM)


def f32(*shape):
    return jax.ShapeDtypeStruct(shape, jnp.float32)


def call(kernel, outs, args, scratch=()):
    return pl.pallas_call(
        kernel,
        out_shape=outs,
        in_specs=[VMEM] * len(args),
        out_specs=jax.tree.map(lambda _: VMEM, outs),
        scratch_shapes=scratch,
        compiler_params=pltpu.CompilerParams(vmem_limit_bytes=32 << 20),
    )(*args)


def middle_sum(values, trim):
    low, high, total = [], [], None
    for value in values:
        for place in reversed(range(len(low))):
            low[place], value = jnp.minimum(low[place], value), jnp.maximum(low[place], value)
        if len(low) < trim:
            low.append(value)
            continue
        for place in range(len(high)):
            value, high[place] = jnp.minimum(high[place], value), jnp.maximum(high[place], value)
        if len(high) < trim:
            high.insert(0, value)
            continue
        total = value if total is None else total + value
    return total


def pack_kernel(block_ref, out_ref):
    blocks, rows, cols = block_ref.shape
    tiles = cols // LANES
    run = blocks * tiles
    for b in range(blocks):
        for r in range(0, rows, SUB):
            for j in range(tiles):
                tile = block_ref[b, r : r + SUB, j * LANES : (j + 1) * LANES]
                out_ref[pl.ds(r * run + b * tiles + j, SUB, stride=run), :] = tile


def unpack_kernel(dense_ref, out_ref):
    blocks, rows, cols = out_ref.shape
    tiles = cols // LANES
    run = blocks * tiles
    for b in range(blocks):
        for r in range(0, rows, SUB):
            for j in range(tiles):
                out_ref[b, r : r + SUB, j * LANES : (j + 1) * LANES] = dense_ref[
                    pl.ds(r * run + b * tiles + j, SUB, stride=run), :
                ]


def trim_kernel(count, trim, received_ref, trimmed_ref, squares_ref):
    run = trimmed_ref.shape[0]
    squares = jnp.zeros((SUB, LANES), jnp.float32)
    for at in range(0, run, SUB):
        values = [received_ref[i * run + at : i * run + at + SUB, :] for i in range(count)]
        mean = middle_sum(values, trim) / (count - 2 * trim)
        trimmed_ref[at : at + SUB, :] = mean
        squares += mean * mean
    for at in range(0, squares_ref.shape[0], SUB):
        squares_ref[at : at + SUB, :] = squares


def clip_factor(squares_ref, params):
    squares = squares_ref[0:SUB, :]
    for at in range(SUB, squares_ref.shape[0], SUB):
        squares += squares_ref[at : at + SUB, :]
    total = jnp.sum(squares, keepdims=True)
    return jnp.minimum(1.0, 1.0 / jnp.sqrt(total / params + 1e-12))


def adam(factor, trimmed, one, two, weight):
    clipped = factor * trimmed
    new_one = 0.9 * one + 0.1 * clipped
    new_two = 0.95 * two + 0.05 * clipped * clipped
    update = new_one / (1.0 - 0.9**STEP) / (jnp.sqrt(new_two / (1.0 - 0.95**STEP)) + 1e-08)
    return weight - 0.05 * (update + 0.1 * weight), new_one, new_two


def adam_kernel(params, squares_ref, trimmed_ref, one_ref, two_ref, weight_ref, new_ref, new_one_ref, new_two_ref):
    factor = clip_factor(squares_ref, params)
    weight, one, two = adam(factor, trimmed_ref[...], one_ref[...], two_ref[...], weight_ref[...])
    new_one_ref[...] = one
    new_two_ref[...] = two
    run = trimmed_ref.shape[0]
    for at in range(0, new_ref.shape[0], run):
        new_ref[at : at + run, :] = weight


def on_device(grads, weight, moment_one, moment_two):
    count, shards = lax.axis_size("rep"), lax.axis_size("shard")
    blocks, rows, cols = weight.shape
    params = blocks * shards * rows * cols
    run = blocks * (rows // count) * cols // LANES
    everyone = count * shards

    packed = call(pack_kernel, f32(count * run, LANES), (grads[0],))
    received = lax.all_to_all(packed, "rep", 0, 0, tiled=True)
    trimmed, squares = call(
        functools.partial(trim_kernel, count, count // 8),
        (f32(run, LANES), f32(everyone * SUB, LANES)),
        (received,),
    )
    squares = lax.all_to_all(squares, ("rep", "shard"), 0, 0, tiled=True)
    owned = lax.dynamic_slice_in_dim(weight, lax.axis_index("rep") * moment_one.shape[1], moment_one.shape[1], 1)
    new, one, two = call(
        functools.partial(adam_kernel, params),
        (f32(count * run, LANES), f32(run, LANES), f32(run, LANES)),
        (squares, trimmed, moment_one.reshape(run, LANES), moment_two.reshape(run, LANES), owned.reshape(run, LANES)),
    )
    gathered = lax.all_to_all(new, "rep", 0, 0, tiled=True)
    new_weight = call(unpack_kernel, f32(*weight.shape), (gathered,))
    return new_weight, one.reshape(moment_one.shape), two.reshape(moment_two.shape)


def solution(mesh):
    return jax.shard_map(
        on_device,
        mesh=mesh,
        in_specs=(
            P("rep", "shard", None, None),
            P("shard", None, None),
            P("shard", "rep", None),
            P("shard", "rep", None),
        ),
        out_specs=(P("shard", None, None), P("shard", "rep", None), P("shard", "rep", None)),
        check_vma=False,
    )
```

time: 101 us -> 48.5 us (0.48)
  blocking collectives: 69.8 us -> 13.9 us
  waiting for transfers between devices: 10.3 us -> 18.5 us
  local copies, waits for them, and re-layouts: 6.93 us -> 1.07 us
  other arithmetic: 3.69 us -> 0 us
  starting transfers between devices: 7.25 us -> 10.9 us
  Pallas kernels: 0 us -> 3.17 us
  loops' own time: 1.1 us -> 0 us
    psum x1 -> x0, blocking collectives: 38.9 us -> none  [on_device(): total = lax.psum(squares, ('rep', 'shard'))]
    all_gather x1 -> x0, blocking collectives: 30.9 us -> none  [on_device(): new_weight = lax.all_gather(owned_new, 'rep', axis=1, tiled=True)]
    all_to_all x0 -> x1, blocking collectives: none -> 13.9 us  [on_device(): gathered = lax.all_to_all(new, 'rep', 0, 0, tiled=True)]
    all_to_all x1 -> x2, waiting for transfers between devices: 10.3 us -> 18.5 us  [the longest x1 10.3 us: on_device(): received = lax.all_to_all(packed, 'rep', 0, 0, tiled=True)]
    unnamed x10 -> x8, local copies, waits for them, and re-layouts: 4.9 us -> 1.03 us
    all_to_all x1 -> x2, starting transfers between devices: 7.25 us -> 10.9 us  [the longest x1 7.25 us: on_device(): received = lax.all_to_all(packed, 'rep', 0, 0, tiled=True)]
    reduce_sum x41 -> x0, other arithmetic: 3.29 us -> none  [the longest x20 2.25 us: trimmed_block(): rank = jnp.sum((lower | equal).astype(jnp.int32), axis=1)]
    pallas_call x0 -> x4, Pallas kernels: none -> 3.17 us  [call(): pl.pallas_call(kernel, out_shape=outs, in_specs=[VMEM] * len(args), out_s...]
  transfers between devices with their start and end apart: 1 -> 2, of which waited for: 1 -> 2; matrix products, arithmetic and copies ran while one was open for 0% -> 0% of each run, Pallas kernels for 0% -> 0%
where the time goes in v1:
time: 48.5 us; the launch traced here: 48.2 us
  waiting for transfers between devices  18.5 us (38%)
  blocking collectives  13.9 us (29%)
  starting transfers between devices  10.9 us (22%)
  Pallas kernels  3.17 us (7%)
  local copies, waits for them, and re-layouts  1.07 us (2%)
  between operations  0.69 us (1%)
    all_to_all x1, blocking collectives, on_device(): gathered = lax.all_to_all(new, 'rep', 0, 0, tiled=True)  13.9 us
    all_to_all x1, waiting for transfers between devices, on_device(): received = lax.all_to_all(packed, 'rep', 0, 0, tiled=True)  10.3 us
    all_to_all x1, waiting for transfers between devices, on_device(): squares = lax.all_to_all(squares, ('rep', 'shard'), 0, 0, tiled=True)  8.15 us
    all_to_all x1, starting transfers between devices, on_device(): received = lax.all_to_all(packed, 'rep', 0, 0, tiled=True)  7.25 us
    all_to_all x1, starting transfers between devices, on_device(): squares = lax.all_to_all(squares, ('rep', 'shard'), 0, 0, tiled=True)  3.63 us
    pallas_call x4, Pallas kernels, call(): pl.pallas_call(kernel, out_shape=outs, in_specs=[VMEM] * len(args), out_s...  3.17 us
    unnamed x8, local copies, waits for them, and re-layouts  1.03 us
  transfers between devices with their start and end apart: 2, of which 2 were waited for; matrix products, arithmetic and copies ran while one was open for 0% of the time, Pallas kernels for 0%

profile of v1, /device:TPU:0, one launch (start us, length us, event | category | flops | bytes accessed | tf_op | source)
XLA Modules:
  0.0 48.2 jit_solution(5369681758109123440)
XLA Ops:
  0.6 0.0 copy-start
  0.6 0.0 copy-start.1
  0.7 1.0 %copy-done.1 = f32[1,2,8,5120]{3,2,1,0:T(8,128)S(1)} copy-done((f32[1,2,8,5120]{3,2,1,0:T(8,128)S(1)}, f32[1,2,8,5120]{3,2,1,0:T(8,128)}, u32[]{:S(2)}) %copy-start.1) | copy-done | bytes 327704
  1.7 0.8 %shard_map.67 = f32[640,128]{1,0:T(8,128)} custom-call(f32[2,8,5120]{2,1,0:T(8,128)S(1)} %bitcast.15), custom_call_target="tpu_custom_call" | custom-call | tf_op jit(solution)/shard_map/pallas_call | solution.py:21
  2.5 7.3 %all-to-all-start = ((f32[8,80,128]{2,1,0:T(8,128)}), f32[8,80,128]{2,1,0:T(8,128)S(1)}, u32[]{:S(2)}, u32[]{:S(2)}) async-start(f32[8,80,128]{2,1,0:T(8,128)} %bitcast.1), calls=%async_computation | async-start | bytes 655360 | tf_op jit(solution)/shard_map/all_to_all | solution.py:117
  9.7 10.3 %all-to-all-done = f32[8,80,128]{2,1,0:T(8,128)S(1)} async-done(((f32[8,80,128]{2,1,0:T(8,128)}), f32[8,80,128]{2,1,0:T(8,128)S(1)}, u32[]{:S(2)}, u32[]{:S(2)}) %all-to-all-start) | async-done | bytes 327712 | tf_op jit(solution)/shard_map/all_to_all | solution.py:117
  20.1 0.7 %shard_map.68 = (f32[80,128]{1,0:T(8,128)S(1)}, f32[256,128]{1,0:T(8,128)}) custom-call(f32[640,128]{1,0:T(8,128)S(1)} %bitcast.12), custom_call_target="tpu_custom_call" | custom-call | tf_op jit(solution)/shard_map/pallas_call | solution.py:21
  20.8 3.6 %all-to-all-start.1 = ((f32[32,8,128]{2,1,0:T(8,128)}), f32[32,8,128]{2,1,0:T(8,128)S(1)}, u32[]{:S(2)}, u32[]{:S(2)}) async-start(f32[32,8,128]{2,1,0:T(8,128)} %bitcast.3), calls=%async_computation.1 | async-start | bytes 262144 | tf_op jit(solution)/shard_map/all_to_all | solution.py:123
  24.4 0.0 copy-done
  24.4 0.0 copy-start.2
  24.4 0.0 copy-start.3
  24.5 8.2 %all-to-all-done.1 = f32[32,8,128]{2,1,0:T(8,128)S(1)} async-done(((f32[32,8,128]{2,1,0:T(8,128)}), f32[32,8,128]{2,1,0:T(8,128)S(1)}, u32[]{:S(2)}, u32[]{:S(2)}) %all-to-all-start.1) | async-done | bytes 131104 | tf_op jit(solution)/shard_map/all_to_all | solution.py:123
  32.6 0.0 copy-done.2
  32.6 0.0 copy-done.3
  32.6 0.8 %shard_map.69 = (f32[640,128]{1,0:T(8,128)S(1)}, f32[80,128]{1,0:T(8,128)}, f32[80,128]{1,0:T(8,128)}) custom-call(f32[256,128]{1,0:T(8,128)S(1)} %bitcast.14, f32[80,128]{1,0:T(8,128)S(1)} %get-tuple-element.9.trimmed_ref, f32[80,128]{1,0:T(8,128)S(1)} %bitcast.18, f32[80,128]{1,0:T(8,128)S(1)} %bitcast.19, f32[80,128]{1,0:T(8,128)S(1)} %bitcast.17), custom_call_target="tpu_custom_call" | custom-call | tf_op jit(solution)/shard_map/pallas_call | solution.py:21
  33.5 13.9 %all_to_all.33 = f32[8,80,128]{2,1,0:T(8,128)S(1)} all-to-all(f32[8,80,128]{2,1,0:T(8,128)S(1)} %bitcast.16), channel_id=1, replica_groups=mesh['rep'=8,'shard'=4] {'rep'}, dimensions={0} | all-to-all | bytes 655360 | tf_op jit(solution)/shard_map/all_to_all | solution.py:130
  47.4 0.8 %shard_map.70 = f32[2,8,5120]{2,1,0:T(8,128)} custom-call(f32[640,128]{1,0:T(8,128)S(1)} %bitcast.13), custom_call_target="tpu_custom_call" | custom-call | tf_op jit(solution)/shard_map/pallas_call | solution.py:21
  (1 shorter events, 0.0 us)
Async XLA Ops:
  0.6 23.8 %copy-start = (f32[2,8,5120]{2,1,0:T(8,128)S(1)}, f32[2,8,5120]{2,1,0:T(8,128)}, u32[]{:S(2)}) copy-start(f32[2,8,5120]{2,1,0:T(8,128)} %param.5) | copy-start | bytes 983044
  0.6 1.0 %copy-start.1 = (f32[1,2,8,5120]{3,2,1,0:T(8,128)S(1)}, f32[1,2,8,5120]{3,2,1,0:T(8,128)}, u32[]{:S(2)}) copy-start(f32[1,2,8,5120]{3,2,1,0:T(8,128)} %param.4) | copy-start | bytes 983044
  2.5 17.6 %all-to-all-start = ((f32[8,80,128]{2,1,0:T(8,128)}), f32[8,80,128]{2,1,0:T(8,128)S(1)}, u32[]{:S(2)}, u32[]{:S(2)}) async-start(f32[8,80,128]{2,1,0:T(8,128)} %bitcast.1), calls=%async_computation | async-start | bytes 655360 | tf_op jit(solution)/shard_map/all_to_all | solution.py:117
  20.8 11.9 %all-to-all-start.1 = ((f32[32,8,128]{2,1,0:T(8,128)}), f32[32,8,128]{2,1,0:T(8,128)S(1)}, u32[]{:S(2)}, u32[]{:S(2)}) async-start(f32[32,8,128]{2,1,0:T(8,128)} %bitcast.3), calls=%async_computation.1 | async-start | bytes 262144 | tf_op jit(solution)/shard_map/all_to_all | solution.py:123
  24.4 8.2 %copy-start.2 = (f32[2,1,5120]{2,1,0:T(1,128)S(1)}, f32[2,1,5120]{2,1,0:T(1,128)}, u32[]{:S(2)}) copy-start(f32[2,1,5120]{2,1,0:T(1,128)} %param.6) | copy-start | bytes 122884
  24.4 8.2 %copy-start.3 = (f32[2,1,5120]{2,1,0:T(1,128)S(1)}, f32[2,1,5120]{2,1,0:T(1,128)}, u32[]{:S(2)}) copy-start(f32[2,1,5120]{2,1,0:T(1,128)} %param.7) | copy-start | bytes 122884

commit v2 on v1

v2 whole, which is shorter than its diff:
```python
import functools

import jax
import jax.numpy as jnp
from jax import lax
from jax.experimental import pallas as pl
from jax.experimental.pallas import tpu as pltpu
from jax.sharding import PartitionSpec as P

STEP = 100
LANES = 128
SUB = 8
VMEM = pl.BlockSpec(memory_space=pltpu.VMEM)
SMEM = pl.BlockSpec(memory_space=pltpu.SMEM)
PARAMS = pltpu.CompilerParams(vmem_limit_bytes=32 << 20)


def f32(*shape):
    return jax.ShapeDtypeStruct(shape, jnp.float32)


def middle_sum(values, trim):
    low, high, total = [], [], None
    for value in values:
        for place in reversed(range(len(low))):
            low[place], value = jnp.minimum(low[place], value), jnp.maximum(low[place], value)
        if len(low) < trim:
            low.append(value)
            continue
        for place in range(len(high)):
            value, high[place] = jnp.minimum(high[place], value), jnp.maximum(high[place], value)
        if len(high) < trim:
            high.insert(0, value)
            continue
        total = value if total is None else total + value
    return total


def trim_kernel(trim, received_ref, trimmed_ref):
    count, tiles = received_ref.shape[:2]
    for tile in range(tiles):
        values = [received_ref[i, tile] for i in range(count)]
        mean = middle_sum(values, trim) / (count - 2 * trim)
        for i in range(count):
            trimmed_ref[i, tile] = mean


def square_kernel(trimmed_ref, squares_ref):
    squares = jnp.zeros((SUB, LANES), jnp.float32)
    for owner in range(trimmed_ref.shape[0]):
        for tile in range(trimmed_ref.shape[1]):
            squares += trimmed_ref[owner, tile] * trimmed_ref[owner, tile]
    squares_ref[...] = squares


def adam(factor, trimmed, one, two, weight):
    clipped = factor * trimmed
    new_one = 0.9 * one + 0.1 * clipped
    new_two = 0.95 * two + 0.05 * clipped * clipped
    update = new_one / (1.0 - 0.9**STEP) / (jnp.sqrt(new_two / (1.0 - 0.95**STEP)) + 1e-08)
    return weight - 0.05 * (update + 0.1 * weight), new_one, new_two


def adam_kernel(params, orders, me_ref, squares_ref, trimmed_ref, weight_ref, *refs):
    moment_refs, (new_ref, new_one_ref, new_two_ref, moments) = refs[: len(orders)], refs[len(orders) :]
    total = jnp.sum(squares_ref[...], keepdims=True)
    factor = jnp.minimum(1.0, 1.0 / jnp.sqrt(total / params + 1e-12))
    blocks, rows, cols = weight_ref.shape
    across = cols // LANES
    run = blocks * across
    me = me_ref[0]
    for order, ref in zip(orders, moment_refs):
        for part, place in enumerate(order):
            row = pl.multiple_of((me ^ place) * 2 * run, 2 * run)
            moments[pl.ds(row, 2 * run), :] = ref[part * 2 * run : (part + 1) * 2 * run, :]
    start = (me // SUB) * across * SUB + me % SUB
    own = moment_refs[0]
    for b in range(blocks):
        base = b * (rows // SUB) * across * SUB
        mine = trimmed_ref[pl.ds(base + start, across, stride=SUB), :]
        here, there = slice(b * across, (b + 1) * across), slice(run + b * across, run + (b + 1) * across)
        _, new_one_ref[here, :], new_two_ref[here, :] = adam(factor, mine, own[here, :], own[there, :], mine)
    tile = 0
    for b in range(blocks):
        for r in range(0, rows, SUB):
            for j in range(across):
                at = b * across + j
                trimmed = trimmed_ref[tile * SUB : (tile + 1) * SUB, :]
                one = moments[pl.ds(2 * r * run + at, SUB, stride=2 * run), :]
                two = moments[pl.ds((2 * r + 1) * run + at, SUB, stride=2 * run), :]
                lanes = slice(j * LANES, (j + 1) * LANES)
                new_ref[b, r : r + SUB, lanes], _, _ = adam(factor, trimmed, one, two, weight_ref[b, r : r + SUB, lanes])
                tile += 1


def on_device(grads, weight, moment_one, moment_two):
    count, shards = lax.axis_size("rep"), lax.axis_size("shard")
    blocks, rows, cols = weight.shape
    params = blocks * shards * rows * cols
    run = blocks * cols // LANES
    tiles = blocks * rows * cols // (SUB * LANES) // count

    def swap(value, axis, mask):
        return lax.ppermute(value, axis, [(i, i ^ mask) for i in range(lax.axis_size(axis))])

    tiled = grads.reshape(blocks, rows // SUB, SUB, cols // LANES, LANES).transpose(0, 1, 3, 2, 4)
    received = lax.all_to_all(tiled.reshape(count, tiles, SUB, LANES), "rep", 0, 0, tiled=True)

    moments = [jnp.concatenate([moment_one.reshape(run, LANES), moment_two.reshape(run, LANES)])]
    orders = [[0]]
    masks = [1, 4, 2]

    def spread(mask):
        held = moments[0] if len(moments) == 1 else jnp.concatenate(moments)
        orders.append([place ^ mask for order in orders for place in order])
        moments.append(swap(held, "rep", mask))

    spread(masks[0])
    received, moments[-1] = lax.optimization_barrier((received, moments[-1]))
    spread(masks[1])
    spread(masks[2])
    trimmed = pl.pallas_call(
        functools.partial(trim_kernel, count // 8),
        out_shape=f32(count, tiles, SUB, LANES),
        in_specs=[VMEM],
        out_specs=VMEM,
        compiler_params=PARAMS,
    )(received)
    trimmed = lax.all_to_all(trimmed, "rep", 0, 0, tiled=True)
    squares = pl.pallas_call(
        square_kernel, out_shape=f32(SUB, LANES), in_specs=[VMEM], out_specs=VMEM, compiler_params=PARAMS
    )(trimmed)
    mask = 1
    while mask < shards:
        squares += swap(squares, "shard", mask)
        mask *= 2
    args = (lax.axis_index("rep").reshape(1), squares, trimmed.reshape(-1, LANES), weight, *moments)
    new_weight, one, two = pl.pallas_call(
        functools.partial(adam_kernel, params, orders),
        out_shape=(f32(*weight.shape), f32(run, LANES), f32(run, LANES)),
        in_specs=[SMEM] + [VMEM] * (len(args) - 1),
        out_specs=(VMEM, VMEM, VMEM),
        scratch_shapes=[pltpu.VMEM((count * 2 * run, LANES), jnp.float32)],
        compiler_params=PARAMS,
    )(*args)
    return new_weight, one.reshape(moment_one.shape), two.reshape(moment_two.shape)


def solution(mesh):
    return jax.shard_map(
        on_device,
        mesh=mesh,
        in_specs=(
            P("rep", "shard", None, None),
            P("shard", None, None),
            P("shard", "rep", None),
            P("shard", "rep", None),
        ),
        out_specs=(P("shard", None, None), P("shard", "rep", None), P("shard", "rep", None)),
        check_vma=False,
    )
```

time: 48.5 us -> 41.9 us (0.86)
  blocking collectives: 13.9 us -> 0 us
  starting transfers between devices: 10.9 us -> 19.9 us
  local copies, waits for them, and re-layouts: 1.07 us -> 0.01 us
  Pallas kernels: 3.17 us -> 2.24 us
    all_to_all x1 -> x0, blocking collectives: 13.9 us -> none  [on_device(): gathered = lax.all_to_all(new, 'rep', 0, 0, tiled=True)]
    ppermute x0 -> x5, waiting for transfers between devices: none -> 10.3 us  [swap(): lax.ppermute(value, axis, [(i, i ^ mask) for i in range(lax.axis_size(axi...]
    all_to_all x2, waiting for transfers between devices: 18.5 us -> 8.29 us  [the longest x1 4.52 us: on_device(): trimmed = lax.all_to_all(trimmed, 'rep', 0, 0, tiled=True)]
    ppermute x0 -> x5, starting transfers between devices: none -> 8.45 us  [swap(): lax.ppermute(value, axis, [(i, i ^ mask) for i in range(lax.axis_size(axi...]
    unnamed x8 -> x6, local copies, waits for them, and re-layouts: 1.03 us -> 0.01 us
    pallas_call x4 -> x3, Pallas kernels: 3.17 us -> 2.24 us  [the longest x1 1.38 us: on_device(): pl.pallas_call(functools.partial(adam_kernel, params, orders), out_shape=...]
    all_to_all x2, starting transfers between devices: 10.9 us -> 11.5 us  [the longest x1 7.4 us: on_device(): lax.all_to_all(tiled.reshape(count, tiles, SUB, LANES), 'rep', 0, 0, tile...]
  transfers between devices with their start and end apart: 2 -> 7, of which waited for: 2 -> 6; matrix products, arithmetic and copies ran while one was open for 0% -> 0% of each run, Pallas kernels for 0% -> 2%
where the time goes in v2:
time: 41.9 us; the launch traced here: 41.5 us
  starting transfers between devices  19.9 us (47%)
  waiting for transfers between devices  18.6 us (44%)
  Pallas kernels  2.24 us (5%)
  between operations  0.7 us (2%)
    ppermute x5, waiting for transfers between devices, swap(): lax.ppermute(value, axis, [(i, i ^ mask) for i in range(lax.axis_size(axi...  10.3 us
    ppermute x5, starting transfers between devices, swap(): lax.ppermute(value, axis, [(i, i ^ mask) for i in range(lax.axis_size(axi...  8.45 us
    all_to_all x1, starting transfers between devices, on_device(): lax.all_to_all(tiled.reshape(count, tiles, SUB, LANES), 'rep', 0, 0, tile...  7.4 us
    all_to_all x1, waiting for transfers between devices, on_device(): trimmed = lax.all_to_all(trimmed, 'rep', 0, 0, tiled=True)  4.52 us
    all_to_all x1, starting transfers between devices, on_device(): trimmed = lax.all_to_all(trimmed, 'rep', 0, 0, tiled=True)  4.08 us
    all_to_all x1, waiting for transfers between devices, on_device(): lax.all_to_all(tiled.reshape(count, tiles, SUB, LANES), 'rep', 0, 0, tile...  3.77 us
    pallas_call x1, Pallas kernels, on_device(): pl.pallas_call(functools.partial(adam_kernel, params, orders), out_shape=...  1.38 us
  transfers between devices with their start and end apart: 7, of which 6 were waited for; matrix products, arithmetic and copies ran while one was open for 0% of the time, Pallas kernels for 2%

profile of v2, /device:TPU:0, one launch (start us, length us, event | category | flops | bytes accessed | tf_op | source)
XLA Modules:
  0.0 41.5 jit_solution(17442381526108820658)
XLA Ops:
  0.6 0.0 copy-start.1
  0.6 0.0 copy-start.2
  0.7 7.4 %all-to-all-start = ((f32[8,10,8,128]{3,2,1,0:T(8,128)}), f32[8,10,8,128]{3,2,1,0:T(8,128)S(1)}, u32[]{:S(2)}, u32[]{:S(2)}) async-start(f32[8,10,8,128]{3,2,1,0:T(8,128)} %bitcast.18), calls=%async_computation | async-start | bytes 655360 | tf_op jit(solution)/shard_map/all_to_all | solution.py:107
  8.0 0.0 copy-done.1
  8.1 0.0 copy-done.2
  8.1 2.1 %collective-permute-start = (f32[160,128]{1,0:T(8,128)S(1)}, f32[160,128]{1,0:T(8,128)S(1)}, u32[]{:S(2)}, u32[]{:S(2)}) collective-permute-start(f32[160,128]{1,0:T(8,128)S(1)} %pad_maximum_fusion.2.refs_0_), channel_id=1, source_target_pairs={{0,4},{4,0},{8,12},{12,8},{16,20},{20,16},{24,28},{28,24},{1,5},{5... | collective-permute-start | bytes 245768 | tf_op jit(solution)/shard_map/ppermute | solution.py:104
  10.2 4.4 %collective-permute-done.refs_1_ = f32[160,128]{1,0:T(8,128)S(1)} collective-permute-done((f32[160,128]{1,0:T(8,128)S(1)}, f32[160,128]{1,0:T(8,128)S(1)}, u32[]{:S(2)}, u32[]{:S(2)}) %collective-permute-start) | collective-permute-done | bytes 81952 | tf_op jit(solution)/shard_map/ppermute | solution.py:104
  14.6 3.8 %all-to-all-done.received_ref = f32[8,10,8,128]{3,2,1,0:T(8,128)S(1)} async-done(((f32[8,10,8,128]{3,2,1,0:T(8,128)}), f32[8,10,8,128]{3,2,1,0:T(8,128)S(1)}, u32[]{:S(2)}, u32[]{:S(2)}) %all-to-all-start) | async-done | bytes 327712 | tf_op jit(solution)/shard_map/all_to_all | solution.py:107
  18.4 1.0 %collective-permute-start.3 = (f32[320,128]{1,0:T(8,128)S(1)}, f32[320,128]{1,0:T(8,128)S(1)}, u32[]{:S(2)}, u32[]{:S(2)}) collective-permute-start(f32[320,128]{1,0:T(8,128)S(1)} %pad_maximum_fusion.1), channel_id=1, source_target_pairs={{0,16},{4,20},{8,24},{12,28},{16,0},{20,4},{24,8},{28,12},{1,17},{... | collective-permute-start | bytes 491528 | tf_op jit(solution)/shard_map/ppermute | solution.py:104
  19.4 0.8 %shard_map.67 = f32[8,10,8,128]{3,2,1,0:T(8,128)} custom-call(f32[8,10,8,128]{3,2,1,0:T(8,128)S(1)} %all-to-all-done.received_ref), custom_call_target="tpu_custom_call" | custom-call | tf_op jit(solution)/shard_map/pallas_call | solution.py:122
  20.2 4.1 %all-to-all-start.1 = ((f32[8,10,8,128]{3,2,1,0:T(8,128)}), f32[8,10,8,128]{3,2,1,0:T(8,128)S(1)}, u32[]{:S(2)}, u32[]{:S(2)}) async-start(f32[8,10,8,128]{3,2,1,0:T(8,128)} %shard_map.67), calls=%async_computation.1 | async-start | bytes 655360 | tf_op jit(solution)/shard_map/all_to_all | solution.py:129
  24.3 2.6 %collective-permute-done.3.refs_2_ = f32[320,128]{1,0:T(8,128)S(1)} collective-permute-done((f32[320,128]{1,0:T(8,128)S(1)}, f32[320,128]{1,0:T(8,128)S(1)}, u32[]{:S(2)}, u32[]{:S(2)}) %collective-permute-start.3) | collective-permute-done | bytes 163872 | tf_op jit(solution)/shard_map/ppermute | solution.py:104
  26.9 0.0 copy-start
  26.9 3.7 %collective-permute-start.4 = (f32[640,128]{1,0:T(8,128)S(1)}, f32[640,128]{1,0:T(8,128)S(1)}, u32[]{:S(2)}, u32[]{:S(2)}) collective-permute-start(f32[640,128]{1,0:T(8,128)S(1)} %pad_maximum_fusion), channel_id=1, source_target_pairs={{0,8},{4,12},{8,0},{12,4},{16,24},{20,28},{24,16},{28,20},{1,9},{5... | collective-permute-start | bytes 983048 | tf_op jit(solution)/shard_map/ppermute | solution.py:104
  30.7 4.5 %all-to-all-done.1.trimmed_ref = f32[8,10,8,128]{3,2,1,0:T(8,128)S(1)} async-done(((f32[8,10,8,128]{3,2,1,0:T(8,128)}), f32[8,10,8,128]{3,2,1,0:T(8,128)S(1)}, u32[]{:S(2)}, u32[]{:S(2)}) %all-to-all-start.1) | async-done | bytes 327712 | tf_op jit(solution)/shard_map/all_to_all | solution.py:129
  35.2 0.1 shard_map.68
  35.3 0.1 collective-permute-start.1
  35.4 1.2 %collective-permute-done.1 = f32[8,128]{1,0:T(8,128)S(1)} collective-permute-done((f32[8,128]{1,0:T(8,128)S(1)}, f32[8,128]{1,0:T(8,128)S(1)}, u32[]{:S(2)}, u32[]{:S(2)}) %collective-permute-start.1) | collective-permute-done | bytes 4128 | tf_op jit(solution)/shard_map/ppermute | solution.py:104
  36.5 1.5 %collective-permute-start.2 = (f32[8,128]{1,0:T(8,128)S(1)}, f32[8,128]{1,0:T(8,128)S(1)}, u32[]{:S(2)}, u32[]{:S(2)}) collective-permute-start(f32[8,128]{1,0:T(8,128)S(1)} %add.6), channel_id=1, source_target_pairs={{0,2},{1,3},{2,0},{3,1},{4,6},{5,7},{6,4},{7,5},{8,10},{9,11},{10,... | collective-permute-start | bytes 12296 | tf_op jit(solution)/shard_map/ppermute | solution.py:104
  38.0 2.1 %collective-permute-done.2 = f32[8,128]{1,0:T(8,128)S(1)} collective-permute-done((f32[8,128]{1,0:T(8,128)S(1)}, f32[8,128]{1,0:T(8,128)S(1)}, u32[]{:S(2)}, u32[]{:S(2)}) %collective-permute-start.2) | collective-permute-done | bytes 4128 | tf_op jit(solution)/shard_map/ppermute | solution.py:104
  40.1 0.0 collective-permute-done.4.refs_3_
  40.1 0.0 copy-done
  40.1 1.4 %shard_map.69 = (f32[2,8,5120]{2,1,0:T(8,128)}, f32[80,128]{1,0:T(8,128)}, f32[80,128]{1,0:T(8,128)}) custom-call(s32[1]{0:T(128)} %bitcast.me_ref, f32[8,128]{1,0:T(8,128)S(1)} %add.7.squares_ref, f32[640,128]{1,0:T(8,128)S(1)} %bitcast.11, f32[2,8,5120]{2,1,0:T(8,128)S(1)} %copy-done, f32[160,128]{1,0:T(8,128)S(1)} %pad_maximum_fusion.2.refs_0_, ...), custom_call_target="tpu_custom_call" | custom-call | tf_op jit(solution)/shard_map/pallas_call | solution.py:138
  (5 shorter events, 0.0 us)
Async XLA Ops:
  0.6 7.4 %copy-start.1 = (f32[2,1,5120]{2,1,0:T(1,128)S(1)}, f32[2,1,5120]{2,1,0:T(1,128)}, u32[]{:S(2)}) copy-start(f32[2,1,5120]{2,1,0:T(1,128)} %param.7) | copy-start | bytes 122884
  0.6 7.4 %copy-start.2 = (f32[2,1,5120]{2,1,0:T(1,128)S(1)}, f32[2,1,5120]{2,1,0:T(1,128)}, u32[]{:S(2)}) copy-start(f32[2,1,5120]{2,1,0:T(1,128)} %param.6) | copy-start | bytes 122884
  0.7 17.7 %all-to-all-start = ((f32[8,10,8,128]{3,2,1,0:T(8,128)}), f32[8,10,8,128]{3,2,1,0:T(8,128)S(1)}, u32[]{:S(2)}, u32[]{:S(2)}) async-start(f32[8,10,8,128]{3,2,1,0:T(8,128)} %bitcast.18), calls=%async_computation | async-start | bytes 655360 | tf_op jit(solution)/shard_map/all_to_all | solution.py:107
  8.1 6.5 %collective-permute-start = (f32[160,128]{1,0:T(8,128)S(1)}, f32[160,128]{1,0:T(8,128)S(1)}, u32[]{:S(2)}, u32[]{:S(2)}) collective-permute-start(f32[160,128]{1,0:T(8,128)S(1)} %pad_maximum_fusion.2.refs_0_), channel_id=1, source_target_pairs={{0,4},{4,0},{8,12},{12,8},{16,20},{20,16},{24,28},{28,24},{1,5},{5... | collective-permute-start | bytes 245768 | tf_op jit(solution)/shard_map/ppermute | solution.py:104
  18.4 8.5 %collective-permute-start.3 = (f32[320,128]{1,0:T(8,128)S(1)}, f32[320,128]{1,0:T(8,128)S(1)}, u32[]{:S(2)}, u32[]{:S(2)}) collective-permute-start(f32[320,128]{1,0:T(8,128)S(1)} %pad_maximum_fusion.1), channel_id=1, source_target_pairs={{0,16},{4,20},{8,24},{12,28},{16,0},{20,4},{24,8},{28,12},{1,17},{... | collective-permute-start | bytes 491528 | tf_op jit(solution)/shard_map/ppermute | solution.py:104
  20.2 15.0 %all-to-all-start.1 = ((f32[8,10,8,128]{3,2,1,0:T(8,128)}), f32[8,10,8,128]{3,2,1,0:T(8,128)S(1)}, u32[]{:S(2)}, u32[]{:S(2)}) async-start(f32[8,10,8,128]{3,2,1,0:T(8,128)} %shard_map.67), calls=%async_computation.1 | async-start | bytes 655360 | tf_op jit(solution)/shard_map/all_to_all | solution.py:129
  26.9 13.2 %copy-start = (f32[2,8,5120]{2,1,0:T(8,128)S(1)}, f32[2,8,5120]{2,1,0:T(8,128)}, u32[]{:S(2)}) copy-start(f32[2,8,5120]{2,1,0:T(8,128)} %weight_ref.1) | copy-start | bytes 983044
  26.9 13.2 %collective-permute-start.4 = (f32[640,128]{1,0:T(8,128)S(1)}, f32[640,128]{1,0:T(8,128)S(1)}, u32[]{:S(2)}, u32[]{:S(2)}) collective-permute-start(f32[640,128]{1,0:T(8,128)S(1)} %pad_maximum_fusion), channel_id=1, source_target_pairs={{0,8},{4,12},{8,0},{12,4},{16,24},{20,28},{24,16},{28,20},{1,9},{5... | collective-permute-start | bytes 983048 | tf_op jit(solution)/shard_map/ppermute | solution.py:104
  35.3 1.2 %collective-permute-start.1 = (f32[8,128]{1,0:T(8,128)S(1)}, f32[8,128]{1,0:T(8,128)S(1)}, u32[]{:S(2)}, u32[]{:S(2)}) collective-permute-start(f32[8,128]{1,0:T(8,128)S(1)} %shard_map.68), channel_id=1, source_target_pairs={{0,1},{1,0},{2,3},{3,2},{4,5},{5,4},{6,7},{7,6},{8,9},{9,8},{10,11... | collective-permute-start | bytes 12296 | tf_op jit(solution)/shard_map/ppermute | solution.py:104
  36.5 3.6 %collective-permute-start.2 = (f32[8,128]{1,0:T(8,128)S(1)}, f32[8,128]{1,0:T(8,128)S(1)}, u32[]{:S(2)}, u32[]{:S(2)}) collective-permute-start(f32[8,128]{1,0:T(8,128)S(1)} %add.6), channel_id=1, source_target_pairs={{0,2},{1,3},{2,0},{3,1},{4,6},{5,7},{6,4},{7,5},{8,10},{9,11},{10,... | collective-permute-start | bytes 12296 | tf_op jit(solution)/shard_map/ppermute | solution.py:104

commit v3 on v2

--- a/solution.py
+++ b/solution.py
@@ -108,17 +108,15 @@
 
     moments = [jnp.concatenate([moment_one.reshape(run, LANES), moment_two.reshape(run, LANES)])]
     orders = [[0]]
-    masks = [1, 4, 2]
+    masks = [1 << bit for bit in range(1, (count - 1).bit_length())] + [1]
 
     def spread(mask):
         held = moments[0] if len(moments) == 1 else jnp.concatenate(moments)
         orders.append([place ^ mask for order in orders for place in order])
         moments.append(swap(held, "rep", mask))
 
-    spread(masks[0])
-    received, moments[-1] = lax.optimization_barrier((received, moments[-1]))
-    spread(masks[1])
-    spread(masks[2])
+    for mask in masks[:]:
+        spread(mask)
     trimmed = pl.pallas_call(
         functools.partial(trim_kernel, count // 8),
         out_shape=f32(count, tiles, SUB, LANES),

time: 41.9 us -> 40.1 us (0.957)
  waiting for transfers between devices: 18.6 us -> 17.4 us
  starting transfers between devices: 19.9 us -> 19.3 us
    all_to_all x1, waiting for transfers between devices: 3.77 us -> 0.01 us  [on_device(): lax.all_to_all(tiled.reshape(count, tiles, SUB, LANES), 'rep', 0, 0, tile...]
    ppermute x5, waiting for transfers between devices: 10.3 us -> 11.7 us  [swap(): lax.ppermute(value, axis, [(i, i ^ mask) for i in range(lax.axis_size(axi...]
    all_to_all x1, waiting for transfers between devices: 4.52 us -> 5.65 us  [on_device(): trimmed = lax.all_to_all(trimmed, 'rep', 0, 0, tiled=True)]
    all_to_all x1, starting transfers between devices: 4.08 us -> 3.43 us  [on_device(): trimmed = lax.all_to_all(trimmed, 'rep', 0, 0, tiled=True)]
  transfers between devices with their start and end apart: 7 -> 7, of which waited for: 6 -> 5; matrix products, arithmetic and copies ran while one was open for 0% -> 0% of each run, Pallas kernels for 2% -> 2%
where the time goes in v3:
time: 40.1 us; the launch traced here: 39.7 us
  starting transfers between devices  19.3 us (48%)
  waiting for transfers between devices  17.4 us (43%)
  Pallas kernels  2.24 us (6%)
  between operations  0.71 us (2%)
    ppermute x5, waiting for transfers between devices, swap(): lax.ppermute(value, axis, [(i, i ^ mask) for i in range(lax.axis_size(axi...  11.7 us
    ppermute x5, starting transfers between devices, swap(): lax.ppermute(value, axis, [(i, i ^ mask) for i in range(lax.axis_size(axi...  8.49 us
    all_to_all x1, starting transfers between devices, on_device(): lax.all_to_all(tiled.reshape(count, tiles, SUB, LANES), 'rep', 0, 0, tile...  7.4 us
    all_to_all x1, waiting for transfers between devices, on_device(): trimmed = lax.all_to_all(trimmed, 'rep', 0, 0, tiled=True)  5.65 us
    all_to_all x1, starting transfers between devices, on_device(): trimmed = lax.all_to_all(trimmed, 'rep', 0, 0, tiled=True)  3.43 us
    pallas_call x1, Pallas kernels, on_device(): pl.pallas_call(functools.partial(adam_kernel, params, orders), out_shape=...  1.38 us
  transfers between devices with their start and end apart: 7, of which 5 were waited for; matrix products, arithmetic and copies ran while one was open for 0% of the time, Pallas kernels for 2%

profile of v3, /device:TPU:0, one launch (start us, length us, event | category | flops | bytes accessed | tf_op | source)
XLA Modules:
  0.0 39.7 jit_solution(424925947183273610)
XLA Ops:
  0.6 0.0 copy-start.1
  0.6 0.0 copy-start.2
  0.7 7.4 %all-to-all-start = ((f32[8,10,8,128]{3,2,1,0:T(8,128)}), f32[8,10,8,128]{3,2,1,0:T(8,128)S(1)}, u32[]{:S(2)}, u32[]{:S(2)}) async-start(f32[8,10,8,128]{3,2,1,0:T(8,128)} %bitcast.18), calls=%async_computation | async-start | bytes 655360 | tf_op jit(solution)/shard_map/all_to_all | solution.py:107
  8.0 0.0 copy-done.1
  8.1 0.0 copy-done.2
  8.1 2.1 %collective-permute-start.2 = (f32[160,128]{1,0:T(8,128)S(1)}, f32[160,128]{1,0:T(8,128)S(1)}, u32[]{:S(2)}, u32[]{:S(2)}) collective-permute-start(f32[160,128]{1,0:T(8,128)S(1)} %pad_maximum_fusion.2.refs_0_), channel_id=1, source_target_pairs={{0,8},{4,12},{8,0},{12,4},{16,24},{20,28},{24,16},{28,20},{1,9},{5... | collective-permute-start | bytes 245768 | tf_op jit(solution)/shard_map/ppermute | solution.py:104
  10.2 5.9 %collective-permute-done.2.refs_1_ = f32[160,128]{1,0:T(8,128)S(1)} collective-permute-done((f32[160,128]{1,0:T(8,128)S(1)}, f32[160,128]{1,0:T(8,128)S(1)}, u32[]{:S(2)}, u32[]{:S(2)}) %collective-permute-start.2) | collective-permute-done | bytes 81952 | tf_op jit(solution)/shard_map/ppermute | solution.py:104
  16.1 3.7 %collective-permute-start.3 = (f32[320,128]{1,0:T(8,128)S(1)}, f32[320,128]{1,0:T(8,128)S(1)}, u32[]{:S(2)}, u32[]{:S(2)}) collective-permute-start(f32[320,128]{1,0:T(8,128)S(1)} %pad_maximum_fusion.1), channel_id=1, source_target_pairs={{0,16},{4,20},{8,24},{12,28},{16,0},{20,4},{24,8},{28,12},{1,17},{... | collective-permute-start | bytes 491528 | tf_op jit(solution)/shard_map/ppermute | solution.py:104
  19.9 0.0 all-to-all-done.received_ref
  19.9 0.8 %shard_map.67 = f32[8,10,8,128]{3,2,1,0:T(8,128)} custom-call(f32[8,10,8,128]{3,2,1,0:T(8,128)S(1)} %all-to-all-done.received_ref), custom_call_target="tpu_custom_call" | custom-call | tf_op jit(solution)/shard_map/pallas_call | solution.py:120
  20.6 3.4 %all-to-all-start.1 = ((f32[8,10,8,128]{3,2,1,0:T(8,128)}), f32[8,10,8,128]{3,2,1,0:T(8,128)S(1)}, u32[]{:S(2)}, u32[]{:S(2)}) async-start(f32[8,10,8,128]{3,2,1,0:T(8,128)} %shard_map.67), calls=%async_computation.1 | async-start | bytes 655360 | tf_op jit(solution)/shard_map/all_to_all | solution.py:127
  24.1 2.6 %collective-permute-done.3.refs_2_ = f32[320,128]{1,0:T(8,128)S(1)} collective-permute-done((f32[320,128]{1,0:T(8,128)S(1)}, f32[320,128]{1,0:T(8,128)S(1)}, u32[]{:S(2)}, u32[]{:S(2)}) %collective-permute-start.3) | collective-permute-done | bytes 163872 | tf_op jit(solution)/shard_map/ppermute | solution.py:104
  26.7 0.0 copy-start
  26.7 1.1 %collective-permute-start.4 = (f32[640,128]{1,0:T(8,128)S(1)}, f32[640,128]{1,0:T(8,128)S(1)}, u32[]{:S(2)}, u32[]{:S(2)}) collective-permute-start(f32[640,128]{1,0:T(8,128)S(1)} %pad_maximum_fusion), channel_id=1, source_target_pairs={{0,4},{4,0},{8,12},{12,8},{16,20},{20,16},{24,28},{28,24},{1,5},{5... | collective-permute-start | bytes 983048 | tf_op jit(solution)/shard_map/ppermute | solution.py:104
  27.8 5.7 %all-to-all-done.1.trimmed_ref = f32[8,10,8,128]{3,2,1,0:T(8,128)S(1)} async-done(((f32[8,10,8,128]{3,2,1,0:T(8,128)}), f32[8,10,8,128]{3,2,1,0:T(8,128)S(1)}, u32[]{:S(2)}, u32[]{:S(2)}) %all-to-all-start.1) | async-done | bytes 327712 | tf_op jit(solution)/shard_map/all_to_all | solution.py:127
  33.4 0.1 shard_map.68
  33.5 0.1 collective-permute-start
  33.6 1.2 %collective-permute-done = f32[8,128]{1,0:T(8,128)S(1)} collective-permute-done((f32[8,128]{1,0:T(8,128)S(1)}, f32[8,128]{1,0:T(8,128)S(1)}, u32[]{:S(2)}, u32[]{:S(2)}) %collective-permute-start) | collective-permute-done | bytes 4128 | tf_op jit(solution)/shard_map/ppermute | solution.py:104
  34.7 1.5 %collective-permute-start.1 = (f32[8,128]{1,0:T(8,128)S(1)}, f32[8,128]{1,0:T(8,128)S(1)}, u32[]{:S(2)}, u32[]{:S(2)}) collective-permute-start(f32[8,128]{1,0:T(8,128)S(1)} %add.6), channel_id=1, source_target_pairs={{0,2},{1,3},{2,0},{3,1},{4,6},{5,7},{6,4},{7,5},{8,10},{9,11},{10,... | collective-permute-start | bytes 12296 | tf_op jit(solution)/shard_map/ppermute | solution.py:104
  36.2 2.1 %collective-permute-done.1 = f32[8,128]{1,0:T(8,128)S(1)} collective-permute-done((f32[8,128]{1,0:T(8,128)S(1)}, f32[8,128]{1,0:T(8,128)S(1)}, u32[]{:S(2)}, u32[]{:S(2)}) %collective-permute-start.1) | collective-permute-done | bytes 4128 | tf_op jit(solution)/shard_map/ppermute | solution.py:104
  38.3 0.0 collective-permute-done.4.refs_3_
  38.3 0.0 copy-done
  38.3 1.4 %shard_map.69 = (f32[2,8,5120]{2,1,0:T(8,128)}, f32[80,128]{1,0:T(8,128)}, f32[80,128]{1,0:T(8,128)}) custom-call(s32[1]{0:T(128)} %bitcast.me_ref, f32[8,128]{1,0:T(8,128)S(1)} %add.7.squares_ref, f32[640,128]{1,0:T(8,128)S(1)} %bitcast.11, f32[2,8,5120]{2,1,0:T(8,128)S(1)} %copy-done, f32[160,128]{1,0:T(8,128)S(1)} %pad_maximum_fusion.2.refs_0_, ...), custom_call_target="tpu_custom_call" | custom-call | tf_op jit(solution)/shard_map/pallas_call | solution.py:136
  (5 shorter events, 0.0 us)
Async XLA Ops:
  0.6 7.4 %copy-start.1 = (f32[2,1,5120]{2,1,0:T(1,128)S(1)}, f32[2,1,5120]{2,1,0:T(1,128)}, u32[]{:S(2)}) copy-start(f32[2,1,5120]{2,1,0:T(1,128)} %param.7) | copy-start | bytes 122884
  0.6 7.4 %copy-start.2 = (f32[2,1,5120]{2,1,0:T(1,128)S(1)}, f32[2,1,5120]{2,1,0:T(1,128)}, u32[]{:S(2)}) copy-start(f32[2,1,5120]{2,1,0:T(1,128)} %param.6) | copy-start | bytes 122884
  0.7 19.2 %all-to-all-start = ((f32[8,10,8,128]{3,2,1,0:T(8,128)}), f32[8,10,8,128]{3,2,1,0:T(8,128)S(1)}, u32[]{:S(2)}, u32[]{:S(2)}) async-start(f32[8,10,8,128]{3,2,1,0:T(8,128)} %bitcast.18), calls=%async_computation | async-start | bytes 655360 | tf_op jit(solution)/shard_map/all_to_all | solution.py:107
  8.1 8.0 %collective-permute-start.2 = (f32[160,128]{1,0:T(8,128)S(1)}, f32[160,128]{1,0:T(8,128)S(1)}, u32[]{:S(2)}, u32[]{:S(2)}) collective-permute-start(f32[160,128]{1,0:T(8,128)S(1)} %pad_maximum_fusion.2.refs_0_), channel_id=1, source_target_pairs={{0,8},{4,12},{8,0},{12,4},{16,24},{20,28},{24,16},{28,20},{1,9},{5... | collective-permute-start | bytes 245768 | tf_op jit(solution)/shard_map/ppermute | solution.py:104
  16.1 10.5 %collective-permute-start.3 = (f32[320,128]{1,0:T(8,128)S(1)}, f32[320,128]{1,0:T(8,128)S(1)}, u32[]{:S(2)}, u32[]{:S(2)}) collective-permute-start(f32[320,128]{1,0:T(8,128)S(1)} %pad_maximum_fusion.1), channel_id=1, source_target_pairs={{0,16},{4,20},{8,24},{12,28},{16,0},{20,4},{24,8},{28,12},{1,17},{... | collective-permute-start | bytes 491528 | tf_op jit(solution)/shard_map/ppermute | solution.py:104
  20.6 12.8 %all-to-all-start.1 = ((f32[8,10,8,128]{3,2,1,0:T(8,128)}), f32[8,10,8,128]{3,2,1,0:T(8,128)S(1)}, u32[]{:S(2)}, u32[]{:S(2)}) async-start(f32[8,10,8,128]{3,2,1,0:T(8,128)} %shard_map.67), calls=%async_computation.1 | async-start | bytes 655360 | tf_op jit(solution)/shard_map/all_to_all | solution.py:127
  26.7 11.7 %copy-start = (f32[2,8,5120]{2,1,0:T(8,128)S(1)}, f32[2,8,5120]{2,1,0:T(8,128)}, u32[]{:S(2)}) copy-start(f32[2,8,5120]{2,1,0:T(8,128)} %weight_ref.1) | copy-start | bytes 983044
  26.7 11.7 %collective-permute-start.4 = (f32[640,128]{1,0:T(8,128)S(1)}, f32[640,128]{1,0:T(8,128)S(1)}, u32[]{:S(2)}, u32[]{:S(2)}) collective-permute-start(f32[640,128]{1,0:T(8,128)S(1)} %pad_maximum_fusion), channel_id=1, source_target_pairs={{0,4},{4,0},{8,12},{12,8},{16,20},{20,16},{24,28},{28,24},{1,5},{5... | collective-permute-start | bytes 983048 | tf_op jit(solution)/shard_map/ppermute | solution.py:104
  33.5 1.2 %collective-permute-start = (f32[8,128]{1,0:T(8,128)S(1)}, f32[8,128]{1,0:T(8,128)S(1)}, u32[]{:S(2)}, u32[]{:S(2)}) collective-permute-start(f32[8,128]{1,0:T(8,128)S(1)} %shard_map.68), channel_id=1, source_target_pairs={{0,1},{1,0},{2,3},{3,2},{4,5},{5,4},{6,7},{7,6},{8,9},{9,8},{10,11... | collective-permute-start | bytes 12296 | tf_op jit(solution)/shard_map/ppermute | solution.py:104
  34.7 3.6 %collective-permute-start.1 = (f32[8,128]{1,0:T(8,128)S(1)}, f32[8,128]{1,0:T(8,128)S(1)}, u32[]{:S(2)}, u32[]{:S(2)}) collective-permute-start(f32[8,128]{1,0:T(8,128)S(1)} %add.6), channel_id=1, source_target_pairs={{0,2},{1,3},{2,0},{3,1},{4,6},{5,7},{6,4},{7,5},{8,10},{9,11},{10,... | collective-permute-start | bytes 12296 | tf_op jit(solution)/shard_map/ppermute | solution.py:104

commit v4 on v3

--- a/solution.py
+++ b/solution.py
@@ -53,18 +53,8 @@
     squares_ref[...] = squares
 
 
-def adam(factor, trimmed, one, two, weight):
-    clipped = factor * trimmed
-    new_one = 0.9 * one + 0.1 * clipped
-    new_two = 0.95 * two + 0.05 * clipped * clipped
-    update = new_one / (1.0 - 0.9**STEP) / (jnp.sqrt(new_two / (1.0 - 0.95**STEP)) + 1e-08)
-    return weight - 0.05 * (update + 0.1 * weight), new_one, new_two
-
-
-def adam_kernel(params, orders, me_ref, squares_ref, trimmed_ref, weight_ref, *refs):
-    moment_refs, (new_ref, new_one_ref, new_two_ref, moments) = refs[: len(orders)], refs[len(orders) :]
-    total = jnp.sum(squares_ref[...], keepdims=True)
-    factor = jnp.minimum(1.0, 1.0 / jnp.sqrt(total / params + 1e-12))
+def spread_kernel(orders, me_ref, weight_ref, *refs):
+    moment_refs, (one_ref, two_ref, kept_ref, moments) = refs[: len(orders)], refs[len(orders) :]
     blocks, rows, cols = weight_ref.shape
     across = cols // LANES
     run = blocks * across
@@ -73,24 +63,44 @@
         for part, place in enumerate(order):
             row = pl.multiple_of((me ^ place) * 2 * run, 2 * run)
             moments[pl.ds(row, 2 * run), :] = ref[part * 2 * run : (part + 1) * 2 * run, :]
-    start = (me // SUB) * across * SUB + me % SUB
-    own = moment_refs[0]
-    for b in range(blocks):
-        base = b * (rows // SUB) * across * SUB
-        mine = trimmed_ref[pl.ds(base + start, across, stride=SUB), :]
-        here, there = slice(b * across, (b + 1) * across), slice(run + b * across, run + (b + 1) * across)
-        _, new_one_ref[here, :], new_two_ref[here, :] = adam(factor, mine, own[here, :], own[there, :], mine)
-    tile = 0
+    at = 0
     for b in range(blocks):
         for r in range(0, rows, SUB):
             for j in range(across):
-                at = b * across + j
-                trimmed = trimmed_ref[tile * SUB : (tile + 1) * SUB, :]
-                one = moments[pl.ds(2 * r * run + at, SUB, stride=2 * run), :]
-                two = moments[pl.ds((2 * r + 1) * run + at, SUB, stride=2 * run), :]
-                lanes = slice(j * LANES, (j + 1) * LANES)
-                new_ref[b, r : r + SUB, lanes], _, _ = adam(factor, trimmed, one, two, weight_ref[b, r : r + SUB, lanes])
-                tile += 1
+                col = b * across + j
+                one_ref[at : at + SUB, :] = 0.9 * moments[pl.ds(2 * r * run + col, SUB, stride=2 * run), :]
+                two_ref[at : at + SUB, :] = 0.95 * moments[pl.ds((2 * r + 1) * run + col, SUB, stride=2 * run), :]
+                weight = weight_ref[b, r : r + SUB, j * LANES : (j + 1) * LANES]
+                kept_ref[at : at + SUB, :] = weight - 0.05 * (0.1 * weight)
+                at += SUB
+
+
+def adam_kernel(params, me_ref, squares_ref, trimmed_ref, ones_ref, twos_ref, kept_ref, own_ref, new_ref, new_one_ref, new_two_ref):
+    total = jnp.sum(squares_ref[...], keepdims=True)
+    factor = jnp.minimum(1.0, 1.0 / jnp.sqrt(total / params + 1e-12))
+    blocks, rows, cols = new_ref.shape
+    across = cols // LANES
+    run = blocks * across
+    me = me_ref[0]
+    start = (me // SUB) * across * SUB + me % SUB
+    for b in range(blocks):
+        base = b * (rows // SUB) * across * SUB
+        clipped = factor * trimmed_ref[pl.ds(base + start, across, stride=SUB), :]
+        here = slice(b * across, (b + 1) * across)
+        new_one_ref[here, :] = 0.9 * own_ref[here, :] + 0.1 * clipped
+        there = slice(run + b * across, run + (b + 1) * across)
+        new_two_ref[here, :] = 0.95 * own_ref[there, :] + 0.05 * clipped * clipped
+    at = 0
+    for b in range(blocks):
+        for r in range(0, rows, SUB):
+            for j in range(across):
+                tile = slice(at, at + SUB)
+                clipped = factor * trimmed_ref[tile, :]
+                one = ones_ref[tile, :] + 0.1 * clipped
+                two = twos_ref[tile, :] + 0.05 * clipped * clipped
+                update = one / (1.0 - 0.9**STEP) / (jnp.sqrt(two / (1.0 - 0.95**STEP)) + 1e-08)
+                new_ref[b, r : r + SUB, j * LANES : (j + 1) * LANES] = kept_ref[tile, :] - 0.05 * update
+                at += SUB
 
 
 def on_device(grads, weight, moment_one, moment_two):
@@ -108,14 +118,14 @@
 
     moments = [jnp.concatenate([moment_one.reshape(run, LANES), moment_two.reshape(run, LANES)])]
     orders = [[0]]
-    masks = [1 << bit for bit in range(1, (count - 1).bit_length())] + [1]
+    masks = [2] + [3 << bit for bit in range(1, (count - 1).bit_length() - 1)] + [1]
 
     def spread(mask):
         held = moments[0] if len(moments) == 1 else jnp.concatenate(moments)
         orders.append([place ^ mask for order in orders for place in order])
         moments.append(swap(held, "rep", mask))
 
-    for mask in masks[:]:
+    for mask in masks:
         spread(mask)
     trimmed = pl.pallas_call(
         functools.partial(trim_kernel, count // 8),
@@ -128,19 +138,25 @@
     squares = pl.pallas_call(
         square_kernel, out_shape=f32(SUB, LANES), in_specs=[VMEM], out_specs=VMEM, compiler_params=PARAMS
     )(trimmed)
-    mask = 1
-    while mask < shards:
+    for mask in [1] + [(1 << bit) + 1 for bit in range(1, (shards - 1).bit_length())]:
         squares += swap(squares, "shard", mask)
-        mask *= 2
-    args = (lax.axis_index("rep").reshape(1), squares, trimmed.reshape(-1, LANES), weight, *moments)
-    new_weight, one, two = pl.pallas_call(
-        functools.partial(adam_kernel, params, orders),
-        out_shape=(f32(*weight.shape), f32(run, LANES), f32(run, LANES)),
-        in_specs=[SMEM] + [VMEM] * (len(args) - 1),
+    me = lax.axis_index("rep").reshape(1)
+    ready = f32(weight.size // LANES, LANES)
+    decayed = pl.pallas_call(
+        functools.partial(spread_kernel, orders),
+        out_shape=(ready, ready, ready),
+        in_specs=[SMEM] + [VMEM] * (1 + len(moments)),
         out_specs=(VMEM, VMEM, VMEM),
         scratch_shapes=[pltpu.VMEM((count * 2 * run, LANES), jnp.float32)],
         compiler_params=PARAMS,
-    )(*args)
+    )(me, weight, *moments)
+    new_weight, one, two = pl.pallas_call(
+        functools.partial(adam_kernel, params),
+        out_shape=(f32(*weight.shape), f32(run, LANES), f32(run, LANES)),
+        in_specs=[SMEM] + [VMEM] * 6,
+        out_specs=(VMEM, VMEM, VMEM),
+        compiler_params=PARAMS,
+    )(me, squares, trimmed.reshape(-1, LANES), *decayed, moments[0])
     return new_weight, one.reshape(moment_one.shape), two.reshape(moment_two.shape)
 
 

time: 40.1 us -> 38.9 us (0.970)
  waiting for transfers between devices: 17.4 us -> 16 us
    ppermute x5, waiting for transfers between devices: 11.7 us -> 8.35 us  [swap(): lax.ppermute(value, axis, [(i, i ^ mask) for i in range(lax.axis_size(axi...]
    all_to_all x1, waiting for transfers between devices: 5.65 us -> 7.61 us  [on_device(): trimmed = lax.all_to_all(trimmed, 'rep', 0, 0, tiled=True)]
    pallas_call x1 -> x2, Pallas kernels: 1.38 us -> 1.57 us  [the longest x1 1.09 us: on_device(): pl.pallas_call(functools.partial(adam_kernel, params), out_shape=(f32(*we...]
  transfers between devices with their start and end apart: 7 -> 7, of which waited for: 5 -> 4; matrix products, arithmetic and copies ran while one was open for 0% -> 0% of each run, Pallas kernels for 2% -> 3%
where the time goes in v4:
time: 38.9 us; the launch traced here: 38.6 us
  starting transfers between devices  19.4 us (50%)
  waiting for transfers between devices  16 us (41%)
  Pallas kernels  2.44 us (6%)
  between operations  0.72 us (2%)
    ppermute x5, starting transfers between devices, swap(): lax.ppermute(value, axis, [(i, i ^ mask) for i in range(lax.axis_size(axi...  8.57 us
    ppermute x5, waiting for transfers between devices, swap(): lax.ppermute(value, axis, [(i, i ^ mask) for i in range(lax.axis_size(axi...  8.35 us
    all_to_all x1, waiting for transfers between devices, on_device(): trimmed = lax.all_to_all(trimmed, 'rep', 0, 0, tiled=True)  7.61 us
    all_to_all x1, starting transfers between devices, on_device(): lax.all_to_all(tiled.reshape(count, tiles, SUB, LANES), 'rep', 0, 0, tile...  7.4 us
    all_to_all x1, starting transfers between devices, on_device(): trimmed = lax.all_to_all(trimmed, 'rep', 0, 0, tiled=True)  3.43 us
    pallas_call x1, Pallas kernels, on_device(): pl.pallas_call(functools.partial(adam_kernel, params), out_shape=(f32(*we...  1.09 us
  transfers between devices with their start and end apart: 7, of which 4 were waited for; matrix products, arithmetic and copies ran while one was open for 0% of the time, Pallas kernels for 3%

profile of v4, /device:TPU:0, one launch (start us, length us, event | category | flops | bytes accessed | tf_op | source)
XLA Modules:
  0.0 38.6 jit_solution(10372912181019078000)
XLA Ops:
  0.6 0.0 copy-start.1
  0.6 0.0 copy-start.2
  0.7 7.4 %all-to-all-start = ((f32[8,10,8,128]{3,2,1,0:T(8,128)}), f32[8,10,8,128]{3,2,1,0:T(8,128)S(1)}, u32[]{:S(2)}, u32[]{:S(2)}) async-start(f32[8,10,8,128]{3,2,1,0:T(8,128)} %bitcast.18), calls=%async_computation | async-start | bytes 655360 | tf_op jit(solution)/shard_map/all_to_all | solution.py:117
  8.0 0.0 copy-done.1
  8.1 0.0 copy-done.2
  8.1 2.1 %collective-permute-start.2 = (f32[160,128]{1,0:T(8,128)S(1)}, f32[160,128]{1,0:T(8,128)S(1)}, u32[]{:S(2)}, u32[]{:S(2)}) collective-permute-start(f32[160,128]{1,0:T(8,128)S(1)} %pad_maximum_fusion.2.refs_0_.own_ref), channel_id=1, source_target_pairs={{0,8},{4,12},{8,0},{12,4},{16,24},{20,28},{24,16},{28,20},{1,9},{5... | collective-permute-start | bytes 245768 | tf_op jit(solution)/shard_map/ppermute | solution.py:114
  10.2 5.9 %collective-permute-done.2.refs_1_ = f32[160,128]{1,0:T(8,128)S(1)} collective-permute-done((f32[160,128]{1,0:T(8,128)S(1)}, f32[160,128]{1,0:T(8,128)S(1)}, u32[]{:S(2)}, u32[]{:S(2)}) %collective-permute-start.2) | collective-permute-done | bytes 81952 | tf_op jit(solution)/shard_map/ppermute | solution.py:114
  16.1 3.1 %collective-permute-start.3 = (f32[320,128]{1,0:T(8,128)S(1)}, f32[320,128]{1,0:T(8,128)S(1)}, u32[]{:S(2)}, u32[]{:S(2)}) collective-permute-start(f32[320,128]{1,0:T(8,128)S(1)} %pad_maximum_fusion.1), channel_id=1, source_target_pairs={{0,24},{4,28},{8,16},{12,20},{16,8},{20,12},{24,0},{28,4},{1,25},{... | collective-permute-start | bytes 491528 | tf_op jit(solution)/shard_map/ppermute | solution.py:114
  19.2 0.0 all-to-all-done.received_ref
  19.2 0.8 %shard_map.67 = f32[8,10,8,128]{3,2,1,0:T(8,128)} custom-call(f32[8,10,8,128]{3,2,1,0:T(8,128)S(1)} %all-to-all-done.received_ref), custom_call_target="tpu_custom_call" | custom-call | tf_op jit(solution)/shard_map/pallas_call | solution.py:130
  20.0 3.4 %all-to-all-start.1 = ((f32[8,10,8,128]{3,2,1,0:T(8,128)}), f32[8,10,8,128]{3,2,1,0:T(8,128)S(1)}, u32[]{:S(2)}, u32[]{:S(2)}) async-start(f32[8,10,8,128]{3,2,1,0:T(8,128)} %shard_map.67), calls=%async_computation.1 | async-start | bytes 655360 | tf_op jit(solution)/shard_map/all_to_all | solution.py:137
  23.5 0.0 collective-permute-done.3.refs_2_
  23.5 0.0 copy-start
  23.5 2.0 %collective-permute-start.4 = (f32[640,128]{1,0:T(8,128)S(1)}, f32[640,128]{1,0:T(8,128)S(1)}, u32[]{:S(2)}, u32[]{:S(2)}) collective-permute-start(f32[640,128]{1,0:T(8,128)S(1)} %pad_maximum_fusion), channel_id=1, source_target_pairs={{0,4},{4,0},{8,12},{12,8},{16,20},{20,16},{24,28},{28,24},{1,5},{5... | collective-permute-start | bytes 983048 | tf_op jit(solution)/shard_map/ppermute | solution.py:114
  25.5 7.6 %all-to-all-done.1.trimmed_ref = f32[8,10,8,128]{3,2,1,0:T(8,128)S(1)} async-done(((f32[8,10,8,128]{3,2,1,0:T(8,128)}), f32[8,10,8,128]{3,2,1,0:T(8,128)S(1)}, u32[]{:S(2)}, u32[]{:S(2)}) %all-to-all-start.1) | async-done | bytes 327712 | tf_op jit(solution)/shard_map/all_to_all | solution.py:137
  33.1 0.1 shard_map.68
  33.2 0.1 collective-permute-start
  33.3 1.2 %collective-permute-done = f32[8,128]{1,0:T(8,128)S(1)} collective-permute-done((f32[8,128]{1,0:T(8,128)S(1)}, f32[8,128]{1,0:T(8,128)S(1)}, u32[]{:S(2)}, u32[]{:S(2)}) %collective-permute-start) | collective-permute-done | bytes 4128 | tf_op jit(solution)/shard_map/ppermute | solution.py:114
  34.5 1.3 %collective-permute-start.1 = (f32[8,128]{1,0:T(8,128)S(1)}, f32[8,128]{1,0:T(8,128)S(1)}, u32[]{:S(2)}, u32[]{:S(2)}) collective-permute-start(f32[8,128]{1,0:T(8,128)S(1)} %add.6), channel_id=1, source_target_pairs={{0,3},{1,2},{2,1},{3,0},{4,7},{5,6},{6,5},{7,4},{8,11},{9,10},{10,... | collective-permute-start | bytes 12296 | tf_op jit(solution)/shard_map/ppermute | solution.py:114
  35.8 0.0 collective-permute-done.4.refs_3_
  35.8 0.0 copy-done
  35.8 0.5 %shard_map.69 = (f32[640,128]{1,0:T(8,128)S(1)}, f32[640,128]{1,0:T(8,128)S(1)}, f32[640,128]{1,0:T(8,128)S(1)}) custom-call(s32[1]{0:T(128)} %bitcast.me_ref, f32[2,8,5120]{2,1,0:T(8,128)S(1)} %copy-done, f32[160,128]{1,0:T(8,128)S(1)} %pad_maximum_fusion.2.refs_0_.own_ref, f32[160,128]{1,0:T(8,128)S(1)} %collective-permute-done.2.refs_1_, ...), custom_call_target="tpu_custom_call" | custom-call | tf_op jit(solution)/shard_map/pallas_call | solution.py:145
  36.2 1.3 %collective-permute-done.1 = f32[8,128]{1,0:T(8,128)S(1)} collective-permute-done((f32[8,128]{1,0:T(8,128)S(1)}, f32[8,128]{1,0:T(8,128)S(1)}, u32[]{:S(2)}, u32[]{:S(2)}) %collective-permute-start.1) | collective-permute-done | bytes 4128 | tf_op jit(solution)/shard_map/ppermute | solution.py:114
  37.5 1.1 %shard_map.70 = (f32[2,8,5120]{2,1,0:T(8,128)}, f32[80,128]{1,0:T(8,128)}, f32[80,128]{1,0:T(8,128)}) custom-call(s32[1]{0:T(128)} %bitcast.me_ref, f32[8,128]{1,0:T(8,128)S(1)} %add.7.squares_ref, f32[640,128]{1,0:T(8,128)S(1)} %bitcast.11, f32[640,128]{1,0:T(8,128)S(1)} %get-tuple-element.9.ones_ref, f32[640,128]{1,0:T(8,128)S(1)} %get-tuple-element.10.twos_ref, ...), custom_call_target="tpu_custom_call" | custom-call | tf_op jit(solution)/shard_map/pallas_call | solution.py:153
  (5 shorter events, 0.1 us)
Async XLA Ops:
  0.6 7.4 %copy-start.1 = (f32[2,1,5120]{2,1,0:T(1,128)S(1)}, f32[2,1,5120]{2,1,0:T(1,128)}, u32[]{:S(2)}) copy-start(f32[2,1,5120]{2,1,0:T(1,128)} %param.7) | copy-start | bytes 122884
  0.6 7.4 %copy-start.2 = (f32[2,1,5120]{2,1,0:T(1,128)S(1)}, f32[2,1,5120]{2,1,0:T(1,128)}, u32[]{:S(2)}) copy-start(f32[2,1,5120]{2,1,0:T(1,128)} %param.6) | copy-start | bytes 122884
  0.7 18.6 %all-to-all-start = ((f32[8,10,8,128]{3,2,1,0:T(8,128)}), f32[8,10,8,128]{3,2,1,0:T(8,128)S(1)}, u32[]{:S(2)}, u32[]{:S(2)}) async-start(f32[8,10,8,128]{3,2,1,0:T(8,128)} %bitcast.18), calls=%async_computation | async-start | bytes 655360 | tf_op jit(solution)/shard_map/all_to_all | solution.py:117
  8.1 8.0 %collective-permute-start.2 = (f32[160,128]{1,0:T(8,128)S(1)}, f32[160,128]{1,0:T(8,128)S(1)}, u32[]{:S(2)}, u32[]{:S(2)}) collective-permute-start(f32[160,128]{1,0:T(8,128)S(1)} %pad_maximum_fusion.2.refs_0_.own_ref), channel_id=1, source_target_pairs={{0,8},{4,12},{8,0},{12,4},{16,24},{20,28},{24,16},{28,20},{1,9},{5... | collective-permute-start | bytes 245768 | tf_op jit(solution)/shard_map/ppermute | solution.py:114
  16.1 7.3 %collective-permute-start.3 = (f32[320,128]{1,0:T(8,128)S(1)}, f32[320,128]{1,0:T(8,128)S(1)}, u32[]{:S(2)}, u32[]{:S(2)}) collective-permute-start(f32[320,128]{1,0:T(8,128)S(1)} %pad_maximum_fusion.1), channel_id=1, source_target_pairs={{0,24},{4,28},{8,16},{12,20},{16,8},{20,12},{24,0},{28,4},{1,25},{... | collective-permute-start | bytes 491528 | tf_op jit(solution)/shard_map/ppermute | solution.py:114
  20.0 13.1 %all-to-all-start.1 = ((f32[8,10,8,128]{3,2,1,0:T(8,128)}), f32[8,10,8,128]{3,2,1,0:T(8,128)S(1)}, u32[]{:S(2)}, u32[]{:S(2)}) async-start(f32[8,10,8,128]{3,2,1,0:T(8,128)} %shard_map.67), calls=%async_computation.1 | async-start | bytes 655360 | tf_op jit(solution)/shard_map/all_to_all | solution.py:137
  23.5 12.3 %copy-start = (f32[2,8,5120]{2,1,0:T(8,128)S(1)}, f32[2,8,5120]{2,1,0:T(8,128)}, u32[]{:S(2)}) copy-start(f32[2,8,5120]{2,1,0:T(8,128)} %weight_ref.1) | copy-start | bytes 983044
  23.5 12.2 %collective-permute-start.4 = (f32[640,128]{1,0:T(8,128)S(1)}, f32[640,128]{1,0:T(8,128)S(1)}, u32[]{:S(2)}, u32[]{:S(2)}) collective-permute-start(f32[640,128]{1,0:T(8,128)S(1)} %pad_maximum_fusion), channel_id=1, source_target_pairs={{0,4},{4,0},{8,12},{12,8},{16,20},{20,16},{24,28},{28,24},{1,5},{5... | collective-permute-start | bytes 983048 | tf_op jit(solution)/shard_map/ppermute | solution.py:114
  33.2 1.2 %collective-permute-start = (f32[8,128]{1,0:T(8,128)S(1)}, f32[8,128]{1,0:T(8,128)S(1)}, u32[]{:S(2)}, u32[]{:S(2)}) collective-permute-start(f32[8,128]{1,0:T(8,128)S(1)} %shard_map.68), channel_id=1, source_target_pairs={{0,1},{1,0},{2,3},{3,2},{4,5},{5,4},{6,7},{7,6},{8,9},{9,8},{10,11... | collective-permute-start | bytes 12296 | tf_op jit(solution)/shard_map/ppermute | solution.py:114
  34.5 3.0 %collective-permute-start.1 = (f32[8,128]{1,0:T(8,128)S(1)}, f32[8,128]{1,0:T(8,128)S(1)}, u32[]{:S(2)}, u32[]{:S(2)}) collective-permute-start(f32[8,128]{1,0:T(8,128)S(1)} %add.6), channel_id=1, source_target_pairs={{0,3},{1,2},{2,1},{3,0},{4,7},{5,6},{6,5},{7,4},{8,11},{9,10},{10,... | collective-permute-start | bytes 12296 | tf_op jit(solution)/shard_map/ppermute | solution.py:114

commit v5 on v4

--- a/solution.py
+++ b/solution.py
@@ -1,4 +1,5 @@
 import functools
+import operator
 
 import jax
 import jax.numpy as jnp
@@ -53,53 +54,57 @@
     squares_ref[...] = squares
 
 
-def spread_kernel(orders, me_ref, weight_ref, *refs):
-    moment_refs, (one_ref, two_ref, kept_ref, moments) = refs[: len(orders)], refs[len(orders) :]
+def ready_kernel(shards, orders, at_ref, weight_ref, trimmed_ref, *refs):
+    moment_refs, (kept_ref, one_ref, one_slope_ref, two_ref, two_slope_ref, own_ref, moments) = refs[: len(orders)], refs[len(orders) :]
     blocks, rows, cols = weight_ref.shape
     across = cols // LANES
     run = blocks * across
-    me = me_ref[0]
+    me, core = at_ref[0] // shards, at_ref[0] % 2
     for order, ref in zip(orders, moment_refs):
         for part, place in enumerate(order):
-            row = pl.multiple_of((me ^ place) * 2 * run, 2 * run)
+            away = jnp.where(core == 0, place[0], place[1])
+            row = pl.multiple_of((me ^ away) * 2 * run, 2 * run)
             moments[pl.ds(row, 2 * run), :] = ref[part * 2 * run : (part + 1) * 2 * run, :]
+    start = (me // SUB) * across * SUB + me % SUB
+    for b in range(blocks):
+        base = b * (rows // SUB) * across * SUB
+        own_ref[b * across : (b + 1) * across, :] = trimmed_ref[pl.ds(base + start, across, stride=SUB), :]
+    one_scale, two_scale = 0.05 / (1.0 - 0.9**STEP), 1.0 / (1.0 - 0.95**STEP)
     at = 0
     for b in range(blocks):
         for r in range(0, rows, SUB):
             for j in range(across):
                 col = b * across + j
-                one_ref[at : at + SUB, :] = 0.9 * moments[pl.ds(2 * r * run + col, SUB, stride=2 * run), :]
-                two_ref[at : at + SUB, :] = 0.95 * moments[pl.ds((2 * r + 1) * run + col, SUB, stride=2 * run), :]
+                tile = slice(at, at + SUB)
+                trimmed = trimmed_ref[tile, :]
+                one = moments[pl.ds(2 * r * run + col, SUB, stride=2 * run), :]
+                two = moments[pl.ds((2 * r + 1) * run + col, SUB, stride=2 * run), :]
                 weight = weight_ref[b, r : r + SUB, j * LANES : (j + 1) * LANES]
-                kept_ref[at : at + SUB, :] = weight - 0.05 * (0.1 * weight)
+                kept_ref[tile, :] = weight - 0.05 * (0.1 * weight)
+                one_ref[tile, :] = (0.9 * one_scale) * one
+                one_slope_ref[tile, :] = (0.1 * one_scale) * trimmed
+                two_ref[tile, :] = (0.95 * two_scale) * two
+                two_slope_ref[tile, :] = (0.05 * two_scale) * trimmed * trimmed
                 at += SUB
 
 
-def adam_kernel(params, me_ref, squares_ref, trimmed_ref, ones_ref, twos_ref, kept_ref, own_ref, new_ref, new_one_ref, new_two_ref):
+def adam_kernel(params, squares_ref, kept_ref, one_ref, one_slope_ref, two_ref, two_slope_ref, own_ref, own_moments_ref, new_ref, new_one_ref, new_two_ref):
     total = jnp.sum(squares_ref[...], keepdims=True)
     factor = jnp.minimum(1.0, 1.0 / jnp.sqrt(total / params + 1e-12))
+    square = factor * factor
+    run = own_ref.shape[0]
+    clipped = factor * own_ref[...]
+    new_one_ref[...] = 0.9 * own_moments_ref[0:run, :] + 0.1 * clipped
+    new_two_ref[...] = 0.95 * own_moments_ref[run : 2 * run, :] + 0.05 * clipped * clipped
     blocks, rows, cols = new_ref.shape
-    across = cols // LANES
-    run = blocks * across
-    me = me_ref[0]
-    start = (me // SUB) * across * SUB + me % SUB
-    for b in range(blocks):
-        base = b * (rows // SUB) * across * SUB
-        clipped = factor * trimmed_ref[pl.ds(base + start, across, stride=SUB), :]
-        here = slice(b * across, (b + 1) * across)
-        new_one_ref[here, :] = 0.9 * own_ref[here, :] + 0.1 * clipped
-        there = slice(run + b * across, run + (b + 1) * across)
-        new_two_ref[here, :] = 0.95 * own_ref[there, :] + 0.05 * clipped * clipped
     at = 0
     for b in range(blocks):
         for r in range(0, rows, SUB):
-            for j in range(across):
+            for j in range(cols // LANES):
                 tile = slice(at, at + SUB)
-                clipped = factor * trimmed_ref[tile, :]
-                one = ones_ref[tile, :] + 0.1 * clipped
-                two = twos_ref[tile, :] + 0.05 * clipped * clipped
-                update = one / (1.0 - 0.9**STEP) / (jnp.sqrt(two / (1.0 - 0.95**STEP)) + 1e-08)
-                new_ref[b, r : r + SUB, j * LANES : (j + 1) * LANES] = kept_ref[tile, :] - 0.05 * update
+                one = one_ref[tile, :] + factor * one_slope_ref[tile, :]
+                two = two_ref[tile, :] + square * two_slope_ref[tile, :]
+                new_ref[b, r : r + SUB, j * LANES : (j + 1) * LANES] = kept_ref[tile, :] - one / (jnp.sqrt(two) + 1e-08)
                 at += SUB
 
 
@@ -117,13 +122,14 @@
     received = lax.all_to_all(tiled.reshape(count, tiles, SUB, LANES), "rep", 0, 0, tiled=True)
 
     moments = [jnp.concatenate([moment_one.reshape(run, LANES), moment_two.reshape(run, LANES)])]
-    orders = [[0]]
-    masks = [2] + [3 << bit for bit in range(1, (count - 1).bit_length() - 1)] + [1]
+    orders = [[(0, 0)]]
+    masks = list(zip([1, 6, 2], [2, 6, 1]))
 
     def spread(mask):
         held = moments[0] if len(moments) == 1 else jnp.concatenate(moments)
-        orders.append([place ^ mask for order in orders for place in order])
-        moments.append(swap(held, "rep", mask))
+        orders.append([tuple(map(operator.xor, place, mask)) for order in orders for place in order])
+        pairs = [(r * shards + s, (r ^ mask[s % 2]) * shards + s) for r in range(count) for s in range(shards)]
+        moments.append(lax.ppermute(held, ("rep", "shard"), pairs))
 
     for mask in masks:
         spread(mask)
@@ -140,23 +146,23 @@
     )(trimmed)
     for mask in [1] + [(1 << bit) + 1 for bit in range(1, (shards - 1).bit_length())]:
         squares += swap(squares, "shard", mask)
-    me = lax.axis_index("rep").reshape(1)
-    ready = f32(weight.size // LANES, LANES)
-    decayed = pl.pallas_call(
-        functools.partial(spread_kernel, orders),
-        out_shape=(ready, ready, ready),
-        in_specs=[SMEM] + [VMEM] * (1 + len(moments)),
-        out_specs=(VMEM, VMEM, VMEM),
+    at = lax.axis_index(("rep", "shard")).reshape(1)
+    flat = f32(weight.size // LANES, LANES)
+    ready = pl.pallas_call(
+        functools.partial(ready_kernel, shards, orders),
+        out_shape=(flat,) * 5 + (f32(run, LANES),),
+        in_specs=[SMEM] + [VMEM] * (2 + len(moments)),
+        out_specs=(VMEM,) * 6,
         scratch_shapes=[pltpu.VMEM((count * 2 * run, LANES), jnp.float32)],
         compiler_params=PARAMS,
-    )(me, weight, *moments)
+    )(at, weight, trimmed.reshape(-1, LANES), *moments)
     new_weight, one, two = pl.pallas_call(
         functools.partial(adam_kernel, params),
         out_shape=(f32(*weight.shape), f32(run, LANES), f32(run, LANES)),
-        in_specs=[SMEM] + [VMEM] * 6,
-        out_specs=(VMEM, VMEM, VMEM),
+        in_specs=[VMEM] * 8,
+        out_specs=(VMEM,) * 3,
         compiler_params=PARAMS,
-    )(me, squares, trimmed.reshape(-1, LANES), *decayed, moments[0])
+    )(squares, *ready, moments[0])
     return new_weight, one.reshape(moment_one.shape), two.reshape(moment_two.shape)
 
 

time: 38.9 us -> 38.6 us (level)
  waiting for transfers between devices: 16 us -> 13.6 us
  starting transfers between devices: 19.4 us -> 21.4 us
    ppermute x0 -> x3, starting transfers between devices: none -> 9.23 us  [spread(): moments.append(lax.ppermute(held, ('rep', 'shard'), pairs))]
    ppermute x5 -> x2, starting transfers between devices: 8.57 us -> 1.36 us  [swap(): lax.ppermute(value, axis, [(i, i ^ mask) for i in range(lax.axis_size(axi...]
    ppermute x5 -> x2, waiting for transfers between devices: 8.35 us -> 2.35 us  [swap(): lax.ppermute(value, axis, [(i, i ^ mask) for i in range(lax.axis_size(axi...]
    ppermute x0 -> x3, waiting for transfers between devices: none -> 4.06 us  [spread(): moments.append(lax.ppermute(held, ('rep', 'shard'), pairs))]
    all_to_all x1, waiting for transfers between devices: 7.61 us -> 6.46 us  [on_device(): trimmed = lax.all_to_all(trimmed, 'rep', 0, 0, tiled=True)]
    all_to_all x1, waiting for transfers between devices: 0.01 us -> 0.69 us  [on_device(): lax.all_to_all(tiled.reshape(count, tiles, SUB, LANES), 'rep', 0, 0, tile...]
  transfers between devices with their start and end apart: 7 -> 7, of which waited for: 4 -> 5; matrix products, arithmetic and copies ran while one was open for 0% -> 0% of each run, Pallas kernels for 3% -> 4%
where the time goes in v5:
time: 38.6 us; the launch traced here: 38.2 us
  starting transfers between devices  21.4 us (55%)
  waiting for transfers between devices  13.6 us (35%)
  Pallas kernels  2.43 us (6%)
  between operations  0.72 us (2%)
    ppermute x3, starting transfers between devices, spread(): moments.append(lax.ppermute(held, ('rep', 'shard'), pairs))  9.23 us
    all_to_all x1, starting transfers between devices, on_device(): lax.all_to_all(tiled.reshape(count, tiles, SUB, LANES), 'rep', 0, 0, tile...  7.4 us
    all_to_all x1, waiting for transfers between devices, on_device(): trimmed = lax.all_to_all(trimmed, 'rep', 0, 0, tiled=True)  6.46 us
    ppermute x3, waiting for transfers between devices, spread(): moments.append(lax.ppermute(held, ('rep', 'shard'), pairs))  4.06 us
    all_to_all x1, starting transfers between devices, on_device(): trimmed = lax.all_to_all(trimmed, 'rep', 0, 0, tiled=True)  3.43 us
    ppermute x2, waiting for transfers between devices, swap(): lax.ppermute(value, axis, [(i, i ^ mask) for i in range(lax.axis_size(axi...  2.35 us
    ppermute x2, starting transfers between devices, swap(): lax.ppermute(value, axis, [(i, i ^ mask) for i in range(lax.axis_size(axi...  1.36 us
    pallas_call x1, Pallas kernels, on_device(): pl.pallas_call(functools.partial(adam_kernel, params), out_shape=(f32(*we...  1.04 us
  transfers between devices with their start and end apart: 7, of which 5 were waited for; matrix products, arithmetic and copies ran while one was open for 0% of the time, Pallas kernels for 4%

profile of v5, /device:TPU:0, one launch (start us, length us, event | category | flops | bytes accessed | tf_op | source)
XLA Modules:
  0.0 38.2 jit_solution(635712856366467795)
XLA Ops:
  0.6 0.0 copy-start.1
  0.6 0.0 copy-start.2
  0.7 7.4 %all-to-all-start = ((f32[8,10,8,128]{3,2,1,0:T(8,128)}), f32[8,10,8,128]{3,2,1,0:T(8,128)S(1)}, u32[]{:S(2)}, u32[]{:S(2)}) async-start(f32[8,10,8,128]{3,2,1,0:T(8,128)} %bitcast.18), calls=%async_computation | async-start | bytes 655360 | tf_op jit(solution)/shard_map/all_to_all | solution.py:122
  8.0 0.0 copy-done.1
  8.1 0.0 copy-done.2
  8.1 2.1 %collective-permute-start.2 = (f32[160,128]{1,0:T(8,128)S(1)}, f32[160,128]{1,0:T(8,128)S(1)}, u32[]{:S(2)}, u32[]{:S(2)}) collective-permute-start(f32[160,128]{1,0:T(8,128)S(1)} %pad_maximum_fusion.2.refs_0_.own_moments_ref), channel_id=1, source_target_pairs={{0,4},{1,9},{2,6},{3,11},{4,0},{5,13},{6,2},{7,15},{8,12},{9,1},{1... | collective-permute-start | bytes 245768 | tf_op jit(solution)/shard_map/ppermute | solution.py:132
  10.2 4.1 %collective-permute-done.2.refs_1_ = f32[160,128]{1,0:T(8,128)S(1)} collective-permute-done((f32[160,128]{1,0:T(8,128)S(1)}, f32[160,128]{1,0:T(8,128)S(1)}, u32[]{:S(2)}, u32[]{:S(2)}) %collective-permute-start.2) | collective-permute-done | bytes 81952 | tf_op jit(solution)/shard_map/ppermute | solution.py:132
  14.2 3.9 %collective-permute-start.3 = (f32[320,128]{1,0:T(8,128)S(1)}, f32[320,128]{1,0:T(8,128)S(1)}, u32[]{:S(2)}, u32[]{:S(2)}) collective-permute-start(f32[320,128]{1,0:T(8,128)S(1)} %pad_maximum_fusion.1), channel_id=1, source_target_pairs={{0,24},{1,25},{2,26},{3,27},{4,28},{5,29},{6,30},{7,31},{8,16},{9,... | collective-permute-start | bytes 491528 | tf_op jit(solution)/shard_map/ppermute | solution.py:132
  18.1 0.7 %all-to-all-done.received_ref = f32[8,10,8,128]{3,2,1,0:T(8,128)S(1)} async-done(((f32[8,10,8,128]{3,2,1,0:T(8,128)}), f32[8,10,8,128]{3,2,1,0:T(8,128)S(1)}, u32[]{:S(2)}, u32[]{:S(2)}) %all-to-all-start) | async-done | bytes 327712 | tf_op jit(solution)/shard_map/all_to_all | solution.py:122
  18.8 0.8 %shard_map.67 = f32[8,10,8,128]{3,2,1,0:T(8,128)} custom-call(f32[8,10,8,128]{3,2,1,0:T(8,128)S(1)} %all-to-all-done.received_ref), custom_call_target="tpu_custom_call" | custom-call | tf_op jit(solution)/shard_map/pallas_call | solution.py:136
  19.6 3.4 %all-to-all-start.1 = ((f32[8,10,8,128]{3,2,1,0:T(8,128)}), f32[8,10,8,128]{3,2,1,0:T(8,128)S(1)}, u32[]{:S(2)}, u32[]{:S(2)}) async-start(f32[8,10,8,128]{3,2,1,0:T(8,128)} %shard_map.67), calls=%async_computation.1 | async-start | bytes 655360 | tf_op jit(solution)/shard_map/all_to_all | solution.py:143
  23.0 0.0 collective-permute-done.3.refs_2_
  23.1 0.0 copy-start
  23.1 3.3 %collective-permute-start.4 = (f32[640,128]{1,0:T(8,128)S(1)}, f32[640,128]{1,0:T(8,128)S(1)}, u32[]{:S(2)}, u32[]{:S(2)}) collective-permute-start(f32[640,128]{1,0:T(8,128)S(1)} %pad_maximum_fusion), channel_id=1, source_target_pairs={{0,8},{1,5},{2,10},{3,7},{4,12},{5,1},{6,14},{7,3},{8,0},{9,13},{1... | collective-permute-start | bytes 983048 | tf_op jit(solution)/shard_map/ppermute | solution.py:132
  26.3 6.5 %all-to-all-done.1.trimmed_ref = f32[8,10,8,128]{3,2,1,0:T(8,128)S(1)} async-done(((f32[8,10,8,128]{3,2,1,0:T(8,128)}), f32[8,10,8,128]{3,2,1,0:T(8,128)S(1)}, u32[]{:S(2)}, u32[]{:S(2)}) %all-to-all-start.1) | async-done | bytes 327712 | tf_op jit(solution)/shard_map/all_to_all | solution.py:143
  32.8 0.1 shard_map.68
  32.9 0.1 collective-permute-start
  33.0 1.2 %collective-permute-done = f32[8,128]{1,0:T(8,128)S(1)} collective-permute-done((f32[8,128]{1,0:T(8,128)S(1)}, f32[8,128]{1,0:T(8,128)S(1)}, u32[]{:S(2)}, u32[]{:S(2)}) %collective-permute-start) | collective-permute-done | bytes 4128 | tf_op jit(solution)/shard_map/ppermute | solution.py:119
  34.1 1.3 %collective-permute-start.1 = (f32[8,128]{1,0:T(8,128)S(1)}, f32[8,128]{1,0:T(8,128)S(1)}, u32[]{:S(2)}, u32[]{:S(2)}) collective-permute-start(f32[8,128]{1,0:T(8,128)S(1)} %add.9), channel_id=1, source_target_pairs={{0,3},{1,2},{2,1},{3,0},{4,7},{5,6},{6,5},{7,4},{8,11},{9,10},{10,... | collective-permute-start | bytes 12296 | tf_op jit(solution)/shard_map/ppermute | solution.py:119
  35.4 0.0 collective-permute-done.4.refs_3_
  35.4 0.0 copy-done
  35.4 0.5 %shard_map.69 = (f32[640,128]{1,0:T(8,128)S(1)}, f32[640,128]{1,0:T(8,128)S(1)}, f32[640,128]{1,0:T(8,128)S(1)}, f32[640,128]{1,0:T(8,128)S(1)}, f32[640,128]{1,0:T(8,128)S(1)}, /*index=5*/f32[80,128]{1,0:T(8,128)S(1)}) custom-call(s32[1]{0:T(128)} %bitcast.3.at_ref, f32[2,8,5120]{2,1,0:T(8,128)S(1)} %copy-done, f32[640,128]{1,0:T(8,128)S(1)} %bitcast.11, ...), custom_call_target="tpu_custom_call" | custom-call | tf_op jit(solution)/shard_map/pallas_call | solution.py:151
  36.0 1.2 %collective-permute-done.1 = f32[8,128]{1,0:T(8,128)S(1)} collective-permute-done((f32[8,128]{1,0:T(8,128)S(1)}, f32[8,128]{1,0:T(8,128)S(1)}, u32[]{:S(2)}, u32[]{:S(2)}) %collective-permute-start.1) | collective-permute-done | bytes 4128 | tf_op jit(solution)/shard_map/ppermute | solution.py:119
  37.2 1.0 %shard_map.70 = (f32[2,8,5120]{2,1,0:T(8,128)}, f32[80,128]{1,0:T(8,128)}, f32[80,128]{1,0:T(8,128)}) custom-call(f32[8,128]{1,0:T(8,128)S(1)} %add.10.squares_ref, f32[640,128]{1,0:T(8,128)S(1)} %get-tuple-element.12.kept_ref, f32[640,128]{1,0:T(8,128)S(1)} %get-tuple-element.13.one_ref, f32[640,128]{1,0:T(8,128)S(1)} %get-tuple-element.14.one_slope_ref, ...), custom_call_target="tpu_custom_call" | custom-call | tf_op jit(solution)/shard_map/pallas_call | solution.py:159
  (5 shorter events, 0.1 us)
Async XLA Ops:
  0.6 7.4 %copy-start.1 = (f32[2,1,5120]{2,1,0:T(1,128)S(1)}, f32[2,1,5120]{2,1,0:T(1,128)}, u32[]{:S(2)}) copy-start(f32[2,1,5120]{2,1,0:T(1,128)} %param.7) | copy-start | bytes 122884
  0.6 7.4 %copy-start.2 = (f32[2,1,5120]{2,1,0:T(1,128)S(1)}, f32[2,1,5120]{2,1,0:T(1,128)}, u32[]{:S(2)}) copy-start(f32[2,1,5120]{2,1,0:T(1,128)} %param.6) | copy-start | bytes 122884
  0.7 18.2 %all-to-all-start = ((f32[8,10,8,128]{3,2,1,0:T(8,128)}), f32[8,10,8,128]{3,2,1,0:T(8,128)S(1)}, u32[]{:S(2)}, u32[]{:S(2)}) async-start(f32[8,10,8,128]{3,2,1,0:T(8,128)} %bitcast.18), calls=%async_computation | async-start | bytes 655360 | tf_op jit(solution)/shard_map/all_to_all | solution.py:122
  8.1 6.1 %collective-permute-start.2 = (f32[160,128]{1,0:T(8,128)S(1)}, f32[160,128]{1,0:T(8,128)S(1)}, u32[]{:S(2)}, u32[]{:S(2)}) collective-permute-start(f32[160,128]{1,0:T(8,128)S(1)} %pad_maximum_fusion.2.refs_0_.own_moments_ref), channel_id=1, source_target_pairs={{0,4},{1,9},{2,6},{3,11},{4,0},{5,13},{6,2},{7,15},{8,12},{9,1},{1... | collective-permute-start | bytes 245768 | tf_op jit(solution)/shard_map/ppermute | solution.py:132
  14.2 8.8 %collective-permute-start.3 = (f32[320,128]{1,0:T(8,128)S(1)}, f32[320,128]{1,0:T(8,128)S(1)}, u32[]{:S(2)}, u32[]{:S(2)}) collective-permute-start(f32[320,128]{1,0:T(8,128)S(1)} %pad_maximum_fusion.1), channel_id=1, source_target_pairs={{0,24},{1,25},{2,26},{3,27},{4,28},{5,29},{6,30},{7,31},{8,16},{9,... | collective-permute-start | bytes 491528 | tf_op jit(solution)/shard_map/ppermute | solution.py:132
  19.6 13.2 %all-to-all-start.1 = ((f32[8,10,8,128]{3,2,1,0:T(8,128)}), f32[8,10,8,128]{3,2,1,0:T(8,128)S(1)}, u32[]{:S(2)}, u32[]{:S(2)}) async-start(f32[8,10,8,128]{3,2,1,0:T(8,128)} %shard_map.67), calls=%async_computation.1 | async-start | bytes 655360 | tf_op jit(solution)/shard_map/all_to_all | solution.py:143
  23.1 12.4 %copy-start = (f32[2,8,5120]{2,1,0:T(8,128)S(1)}, f32[2,8,5120]{2,1,0:T(8,128)}, u32[]{:S(2)}) copy-start(f32[2,8,5120]{2,1,0:T(8,128)} %weight_ref.1) | copy-start | bytes 983044
  23.1 12.3 %collective-permute-start.4 = (f32[640,128]{1,0:T(8,128)S(1)}, f32[640,128]{1,0:T(8,128)S(1)}, u32[]{:S(2)}, u32[]{:S(2)}) collective-permute-start(f32[640,128]{1,0:T(8,128)S(1)} %pad_maximum_fusion), channel_id=1, source_target_pairs={{0,8},{1,5},{2,10},{3,7},{4,12},{5,1},{6,14},{7,3},{8,0},{9,13},{1... | collective-permute-start | bytes 983048 | tf_op jit(solution)/shard_map/ppermute | solution.py:132
  32.9 1.2 %collective-permute-start = (f32[8,128]{1,0:T(8,128)S(1)}, f32[8,128]{1,0:T(8,128)S(1)}, u32[]{:S(2)}, u32[]{:S(2)}) collective-permute-start(f32[8,128]{1,0:T(8,128)S(1)} %shard_map.68), channel_id=1, source_target_pairs={{0,1},{1,0},{2,3},{3,2},{4,5},{5,4},{6,7},{7,6},{8,9},{9,8},{10,11... | collective-permute-start | bytes 12296 | tf_op jit(solution)/shard_map/ppermute | solution.py:119
  34.1 3.0 %collective-permute-start.1 = (f32[8,128]{1,0:T(8,128)S(1)}, f32[8,128]{1,0:T(8,128)S(1)}, u32[]{:S(2)}, u32[]{:S(2)}) collective-permute-start(f32[8,128]{1,0:T(8,128)S(1)} %add.9), channel_id=1, source_target_pairs={{0,3},{1,2},{2,1},{3,0},{4,7},{5,6},{6,5},{7,4},{8,11},{9,10},{10,... | collective-permute-start | bytes 12296 | tf_op jit(solution)/shard_map/ppermute | solution.py:119

commit v6 on v5

--- a/solution.py
+++ b/solution.py
@@ -10,6 +10,7 @@
 
 STEP = 100
 LANES = 128
+PARTS = 4
 SUB = 8
 VMEM = pl.BlockSpec(memory_space=pltpu.VMEM)
 SMEM = pl.BlockSpec(memory_space=pltpu.SMEM)
@@ -88,24 +89,41 @@
                 at += SUB
 
 
-def adam_kernel(params, squares_ref, kept_ref, one_ref, one_slope_ref, two_ref, two_slope_ref, own_ref, own_moments_ref, new_ref, new_one_ref, new_two_ref):
+def adam_kernel(params, squares_ref, kept_ref, one_ref, one_slope_ref, two_ref, two_slope_ref, own_ref, own_moments_ref, *refs):
+    outs, stages, done = refs[:3], refs[3:6], refs[6]
+    new, new_one, new_two = stages
     total = jnp.sum(squares_ref[...], keepdims=True)
     factor = jnp.minimum(1.0, 1.0 / jnp.sqrt(total / params + 1e-12))
     square = factor * factor
     run = own_ref.shape[0]
     clipped = factor * own_ref[...]
-    new_one_ref[...] = 0.9 * own_moments_ref[0:run, :] + 0.1 * clipped
-    new_two_ref[...] = 0.95 * own_moments_ref[run : 2 * run, :] + 0.05 * clipped * clipped
-    blocks, rows, cols = new_ref.shape
+    new_one[...] = 0.9 * own_moments_ref[0:run, :] + 0.1 * clipped
+    new_two[...] = 0.95 * own_moments_ref[run : 2 * run, :] + 0.05 * clipped * clipped
+    copies = [pltpu.make_async_copy(new_one, outs[1], done.at[0]), pltpu.make_async_copy(new_two, outs[2], done.at[1])]
+    for copy in copies:
+        copy.start()
+    blocks, rows, cols = new.shape
+    across = cols // LANES
     at = 0
     for b in range(blocks):
         for r in range(0, rows, SUB):
-            for j in range(cols // LANES):
+            for j in range(across):
                 tile = slice(at, at + SUB)
                 one = one_ref[tile, :] + factor * one_slope_ref[tile, :]
                 two = two_ref[tile, :] + square * two_slope_ref[tile, :]
-                new_ref[b, r : r + SUB, j * LANES : (j + 1) * LANES] = kept_ref[tile, :] - one / (jnp.sqrt(two) + 1e-08)
+                new[b, r : r + SUB, j * LANES : (j + 1) * LANES] = kept_ref[tile, :] - one / (jnp.sqrt(two) + 1e-08)
                 at += SUB
+                if (j + 1) % (across // PARTS) == 0:
+                    part = slice((j + 1 - across // PARTS) * LANES, (j + 1) * LANES)
+                    place = (b, slice(r, r + SUB), part)
+                    copies.append(pltpu.make_async_copy(new.at[place], outs[0].at[place], done.at[len(copies)]))
+                    copies[-1].start()
+    for copy in copies:
+        copy.wait()
+
+
+def from_middle(count):
+    return sorted(range(count), key=lambda i: (i % 2, abs(40 * (i // 2) - 19 * (count // 2))))
 
 
 def on_device(grads, weight, moment_one, moment_two):
@@ -118,8 +136,9 @@
     def swap(value, axis, mask):
         return lax.ppermute(value, axis, [(i, i ^ mask) for i in range(lax.axis_size(axis))])
 
+    order = from_middle(count)
     tiled = grads.reshape(blocks, rows // SUB, SUB, cols // LANES, LANES).transpose(0, 1, 3, 2, 4)
-    received = lax.all_to_all(tiled.reshape(count, tiles, SUB, LANES), "rep", 0, 0, tiled=True)
+    received = lax.all_to_all(tiled.reshape(count, tiles, SUB, LANES), "rep", 0, 0, tiled=True, axis_index_groups=[order])
 
     moments = [jnp.concatenate([moment_one.reshape(run, LANES), moment_two.reshape(run, LANES)])]
     orders = [[(0, 0)]]
@@ -140,7 +159,7 @@
         out_specs=VMEM,
         compiler_params=PARAMS,
     )(received)
-    trimmed = lax.all_to_all(trimmed, "rep", 0, 0, tiled=True)
+    trimmed = lax.all_to_all(trimmed, "rep", 0, 0, tiled=True, axis_index_groups=[order])
     squares = pl.pallas_call(
         square_kernel, out_shape=f32(SUB, LANES), in_specs=[VMEM], out_specs=VMEM, compiler_params=PARAMS
     )(trimmed)
@@ -160,7 +179,13 @@
         functools.partial(adam_kernel, params),
         out_shape=(f32(*weight.shape), f32(run, LANES), f32(run, LANES)),
         in_specs=[VMEM] * 8,
-        out_specs=(VMEM,) * 3,
+        out_specs=(pl.BlockSpec(memory_space=pl.ANY),) * 3,
+        scratch_shapes=[
+            pltpu.VMEM(weight.shape, jnp.float32),
+            pltpu.VMEM((run, LANES), jnp.float32),
+            pltpu.VMEM((run, LANES), jnp.float32),
+            pltpu.SemaphoreType.DMA((2 + blocks * (rows // SUB) * PARTS,)),
+        ],
         compiler_params=PARAMS,
     )(squares, *ready, moments[0])
     return new_weight, one.reshape(moment_one.shape), two.reshape(moment_two.shape)

time: 38.6 us -> 36.3 us (0.940)
  waiting for transfers between devices: 13.6 us -> 11 us
    ppermute x3, starting transfers between devices: 9.23 us -> 6.52 us  [spread(): moments.append(lax.ppermute(held, ('rep', 'shard'), pairs))]
    all_to_all x1, waiting for transfers between devices: 6.46 us -> 3.83 us  [on_device(): lax.all_to_all(trimmed, 'rep', 0, 0, tiled=True, axis_index_groups=[order])]
    all_to_all x1, starting transfers between devices: 3.43 us -> 5.35 us  [on_device(): lax.all_to_all(trimmed, 'rep', 0, 0, tiled=True, axis_index_groups=[order])]
    ppermute x2, waiting for transfers between devices: 2.35 us -> 1.04 us  [swap(): lax.ppermute(value, axis, [(i, i ^ mask) for i in range(lax.axis_size(axi...]
    ppermute x3, waiting for transfers between devices: 4.06 us -> 5.08 us  [spread(): moments.append(lax.ppermute(held, ('rep', 'shard'), pairs))]
    all_to_all x1, starting transfers between devices: 7.4 us -> 7.96 us  [on_device(): lax.all_to_all(tiled.reshape(count, tiles, SUB, LANES), 'rep', 0, 0, tile...]
    ppermute x2, starting transfers between devices: 1.36 us -> 1.91 us  [swap(): lax.ppermute(value, axis, [(i, i ^ mask) for i in range(lax.axis_size(axi...]
  transfers between devices with their start and end apart: 7 -> 7, of which waited for: 5 -> 6; matrix products, arithmetic and copies ran while one was open for 0% -> 0% of each run, Pallas kernels for 4% -> 4%
where the time goes in v6:
time: 36.3 us; the launch traced here: 35.9 us
  starting transfers between devices  21.7 us (60%)
  waiting for transfers between devices  11 us (30%)
  Pallas kernels  2.41 us (7%)
  between operations  0.69 us (2%)
    all_to_all x1, starting transfers between devices, on_device(): lax.all_to_all(tiled.reshape(count, tiles, SUB, LANES), 'rep', 0, 0, tile...  7.96 us
    ppermute x3, starting transfers between devices, spread(): moments.append(lax.ppermute(held, ('rep', 'shard'), pairs))  6.52 us
    all_to_all x1, starting transfers between devices, on_device(): lax.all_to_all(trimmed, 'rep', 0, 0, tiled=True, axis_index_groups=[order])  5.35 us
    ppermute x3, waiting for transfers between devices, spread(): moments.append(lax.ppermute(held, ('rep', 'shard'), pairs))  5.08 us
    all_to_all x1, waiting for transfers between devices, on_device(): lax.all_to_all(trimmed, 'rep', 0, 0, tiled=True, axis_index_groups=[order])  3.83 us
    ppermute x2, starting transfers between devices, swap(): lax.ppermute(value, axis, [(i, i ^ mask) for i in range(lax.axis_size(axi...  1.91 us
    all_to_all x1, waiting for transfers between devices, on_device(): lax.all_to_all(tiled.reshape(count, tiles, SUB, LANES), 'rep', 0, 0, tile...  1.06 us
    ppermute x2, waiting for transfers between devices, swap(): lax.ppermute(value, axis, [(i, i ^ mask) for i in range(lax.axis_size(axi...  1.04 us
  transfers between devices with their start and end apart: 7, of which 6 were waited for; matrix products, arithmetic and copies ran while one was open for 0% of the time, Pallas kernels for 4%

profile of v6, /device:TPU:0, one launch (start us, length us, event | category | flops | bytes accessed | tf_op | source)
XLA Modules:
  0.0 35.9 jit_solution(6971300601441552111)
XLA Ops:
  0.6 0.0 copy-start.1
  0.6 0.0 copy-start.2
  0.7 8.0 %all-to-all-start = ((f32[8,10,8,128]{3,2,1,0:T(8,128)}), f32[8,10,8,128]{3,2,1,0:T(8,128)S(1)}, u32[]{:S(2)}, u32[]{:S(2)}) async-start(f32[8,10,8,128]{3,2,1,0:T(8,128)} %bitcast.18), calls=%async_computation | async-start | bytes 655360 | tf_op jit(solution)/shard_map/all_to_all | solution.py:141
  8.6 0.0 copy-done.1
  8.6 0.0 copy-done.2
  8.6 1.5 %collective-permute-start.2 = (f32[160,128]{1,0:T(8,128)S(1)}, f32[160,128]{1,0:T(8,128)S(1)}, u32[]{:S(2)}, u32[]{:S(2)}) collective-permute-start(f32[160,128]{1,0:T(8,128)S(1)} %pad_maximum_fusion.2.refs_0_.own_moments_ref), channel_id=1, source_target_pairs={{0,4},{1,9},{2,6},{3,11},{4,0},{5,13},{6,2},{7,15},{8,12},{9,1},{1... | collective-permute-start | bytes 245768 | tf_op jit(solution)/shard_map/ppermute | solution.py:151
  10.2 4.3 %collective-permute-done.2.refs_1_ = f32[160,128]{1,0:T(8,128)S(1)} collective-permute-done((f32[160,128]{1,0:T(8,128)S(1)}, f32[160,128]{1,0:T(8,128)S(1)}, u32[]{:S(2)}, u32[]{:S(2)}) %collective-permute-start.2) | collective-permute-done | bytes 81952 | tf_op jit(solution)/shard_map/ppermute | solution.py:151
  14.4 1.6 %collective-permute-start.3 = (f32[320,128]{1,0:T(8,128)S(1)}, f32[320,128]{1,0:T(8,128)S(1)}, u32[]{:S(2)}, u32[]{:S(2)}) collective-permute-start(f32[320,128]{1,0:T(8,128)S(1)} %pad_maximum_fusion.1), channel_id=1, source_target_pairs={{0,24},{1,25},{2,26},{3,27},{4,28},{5,29},{6,30},{7,31},{8,16},{9,... | collective-permute-start | bytes 491528 | tf_op jit(solution)/shard_map/ppermute | solution.py:151
  16.0 1.1 %all-to-all-done.received_ref = f32[8,10,8,128]{3,2,1,0:T(8,128)S(1)} async-done(((f32[8,10,8,128]{3,2,1,0:T(8,128)}), f32[8,10,8,128]{3,2,1,0:T(8,128)S(1)}, u32[]{:S(2)}, u32[]{:S(2)}) %all-to-all-start) | async-done | bytes 327712 | tf_op jit(solution)/shard_map/all_to_all | solution.py:141
  17.1 0.8 %shard_map.67 = f32[8,10,8,128]{3,2,1,0:T(8,128)} custom-call(f32[8,10,8,128]{3,2,1,0:T(8,128)S(1)} %all-to-all-done.received_ref), custom_call_target="tpu_custom_call" | custom-call | tf_op jit(solution)/shard_map/pallas_call | solution.py:155
  17.8 5.4 %all-to-all-start.1 = ((f32[8,10,8,128]{3,2,1,0:T(8,128)}), f32[8,10,8,128]{3,2,1,0:T(8,128)S(1)}, u32[]{:S(2)}, u32[]{:S(2)}) async-start(f32[8,10,8,128]{3,2,1,0:T(8,128)} %shard_map.67), calls=%async_computation.1 | async-start | bytes 655360 | tf_op jit(solution)/shard_map/all_to_all | solution.py:162
  23.2 0.0 collective-permute-done.3.refs_2_
  23.2 0.0 copy-start
  23.2 3.4 %collective-permute-start.4 = (f32[640,128]{1,0:T(8,128)S(1)}, f32[640,128]{1,0:T(8,128)S(1)}, u32[]{:S(2)}, u32[]{:S(2)}) collective-permute-start(f32[640,128]{1,0:T(8,128)S(1)} %pad_maximum_fusion), channel_id=1, source_target_pairs={{0,8},{1,5},{2,10},{3,7},{4,12},{5,1},{6,14},{7,3},{8,0},{9,13},{1... | collective-permute-start | bytes 983048 | tf_op jit(solution)/shard_map/ppermute | solution.py:151
  26.7 3.8 %all-to-all-done.1.trimmed_ref = f32[8,10,8,128]{3,2,1,0:T(8,128)S(1)} async-done(((f32[8,10,8,128]{3,2,1,0:T(8,128)}), f32[8,10,8,128]{3,2,1,0:T(8,128)S(1)}, u32[]{:S(2)}, u32[]{:S(2)}) %all-to-all-start.1) | async-done | bytes 327712 | tf_op jit(solution)/shard_map/all_to_all | solution.py:162
  30.5 0.1 shard_map.68
  30.6 0.4 %collective-permute-start = (f32[8,128]{1,0:T(8,128)S(1)}, f32[8,128]{1,0:T(8,128)S(1)}, u32[]{:S(2)}, u32[]{:S(2)}) collective-permute-start(f32[8,128]{1,0:T(8,128)S(1)} %shard_map.68), channel_id=1, source_target_pairs={{0,1},{1,0},{2,3},{3,2},{4,5},{5,4},{6,7},{7,6},{8,9},{9,8},{10,11... | collective-permute-start | bytes 12296 | tf_op jit(solution)/shard_map/ppermute | solution.py:137
  31.0 0.8 %collective-permute-done = f32[8,128]{1,0:T(8,128)S(1)} collective-permute-done((f32[8,128]{1,0:T(8,128)S(1)}, f32[8,128]{1,0:T(8,128)S(1)}, u32[]{:S(2)}, u32[]{:S(2)}) %collective-permute-start) | collective-permute-done | bytes 4128 | tf_op jit(solution)/shard_map/ppermute | solution.py:137
  31.8 1.5 %collective-permute-start.1 = (f32[8,128]{1,0:T(8,128)S(1)}, f32[8,128]{1,0:T(8,128)S(1)}, u32[]{:S(2)}, u32[]{:S(2)}) collective-permute-start(f32[8,128]{1,0:T(8,128)S(1)} %add.9), channel_id=1, source_target_pairs={{0,3},{1,2},{2,1},{3,0},{4,7},{5,6},{6,5},{7,4},{8,11},{9,10},{10,... | collective-permute-start | bytes 12296 | tf_op jit(solution)/shard_map/ppermute | solution.py:137
  33.3 0.8 %collective-permute-done.4.refs_3_ = f32[640,128]{1,0:T(8,128)S(1)} collective-permute-done((f32[640,128]{1,0:T(8,128)S(1)}, f32[640,128]{1,0:T(8,128)S(1)}, u32[]{:S(2)}, u32[]{:S(2)}) %collective-permute-start.4) | collective-permute-done | bytes 327712 | tf_op jit(solution)/shard_map/ppermute | solution.py:151
  34.1 0.0 copy-done
  34.1 0.5 %shard_map.69 = (f32[640,128]{1,0:T(8,128)S(1)}, f32[640,128]{1,0:T(8,128)S(1)}, f32[640,128]{1,0:T(8,128)S(1)}, f32[640,128]{1,0:T(8,128)S(1)}, f32[640,128]{1,0:T(8,128)S(1)}, /*index=5*/f32[80,128]{1,0:T(8,128)S(1)}) custom-call(s32[1]{0:T(128)} %bitcast.3.at_ref, f32[2,8,5120]{2,1,0:T(8,128)S(1)} %copy-done, f32[640,128]{1,0:T(8,128)S(1)} %bitcast.11, ...), custom_call_target="tpu_custom_call" | custom-call | tf_op jit(solution)/shard_map/pallas_call | solution.py:170
  34.7 0.2 collective-permute-done.1
  34.9 1.0 %shard_map.70 = (f32[2,8,5120]{2,1,0:T(8,128)}, f32[80,128]{1,0:T(8,128)}, f32[80,128]{1,0:T(8,128)}) custom-call(f32[8,128]{1,0:T(8,128)S(1)} %add.10.squares_ref, f32[640,128]{1,0:T(8,128)S(1)} %get-tuple-element.12.kept_ref, f32[640,128]{1,0:T(8,128)S(1)} %get-tuple-element.13.one_ref, f32[640,128]{1,0:T(8,128)S(1)} %get-tuple-element.14.one_slope_ref, ...), custom_call_target="tpu_custom_call" | custom-call | tf_op jit(solution)/shard_map/pallas_call | solution.py:178
  (5 shorter events, 0.0 us)
Async XLA Ops:
  0.6 8.0 %copy-start.1 = (f32[2,1,5120]{2,1,0:T(1,128)S(1)}, f32[2,1,5120]{2,1,0:T(1,128)}, u32[]{:S(2)}) copy-start(f32[2,1,5120]{2,1,0:T(1,128)} %param.7) | copy-start | bytes 122884
  0.6 8.0 %copy-start.2 = (f32[2,1,5120]{2,1,0:T(1,128)S(1)}, f32[2,1,5120]{2,1,0:T(1,128)}, u32[]{:S(2)}) copy-start(f32[2,1,5120]{2,1,0:T(1,128)} %param.6) | copy-start | bytes 122884
  0.7 16.4 %all-to-all-start = ((f32[8,10,8,128]{3,2,1,0:T(8,128)}), f32[8,10,8,128]{3,2,1,0:T(8,128)S(1)}, u32[]{:S(2)}, u32[]{:S(2)}) async-start(f32[8,10,8,128]{3,2,1,0:T(8,128)} %bitcast.18), calls=%async_computation | async-start | bytes 655360 | tf_op jit(solution)/shard_map/all_to_all | solution.py:141
  8.6 5.8 %collective-permute-start.2 = (f32[160,128]{1,0:T(8,128)S(1)}, f32[160,128]{1,0:T(8,128)S(1)}, u32[]{:S(2)}, u32[]{:S(2)}) collective-permute-start(f32[160,128]{1,0:T(8,128)S(1)} %pad_maximum_fusion.2.refs_0_.own_moments_ref), channel_id=1, source_target_pairs={{0,4},{1,9},{2,6},{3,11},{4,0},{5,13},{6,2},{7,15},{8,12},{9,1},{1... | collective-permute-start | bytes 245768 | tf_op jit(solution)/shard_map/ppermute | solution.py:151
  14.4 8.7 %collective-permute-start.3 = (f32[320,128]{1,0:T(8,128)S(1)}, f32[320,128]{1,0:T(8,128)S(1)}, u32[]{:S(2)}, u32[]{:S(2)}) collective-permute-start(f32[320,128]{1,0:T(8,128)S(1)} %pad_maximum_fusion.1), channel_id=1, source_target_pairs={{0,24},{1,25},{2,26},{3,27},{4,28},{5,29},{6,30},{7,31},{8,16},{9,... | collective-permute-start | bytes 491528 | tf_op jit(solution)/shard_map/ppermute | solution.py:151
  17.8 12.7 %all-to-all-start.1 = ((f32[8,10,8,128]{3,2,1,0:T(8,128)}), f32[8,10,8,128]{3,2,1,0:T(8,128)S(1)}, u32[]{:S(2)}, u32[]{:S(2)}) async-start(f32[8,10,8,128]{3,2,1,0:T(8,128)} %shard_map.67), calls=%async_computation.1 | async-start | bytes 655360 | tf_op jit(solution)/shard_map/all_to_all | solution.py:162
  23.2 10.9 %copy-start = (f32[2,8,5120]{2,1,0:T(8,128)S(1)}, f32[2,8,5120]{2,1,0:T(8,128)}, u32[]{:S(2)}) copy-start(f32[2,8,5120]{2,1,0:T(8,128)} %weight_ref.1) | copy-start | bytes 983044
  23.2 10.9 %collective-permute-start.4 = (f32[640,128]{1,0:T(8,128)S(1)}, f32[640,128]{1,0:T(8,128)S(1)}, u32[]{:S(2)}, u32[]{:S(2)}) collective-permute-start(f32[640,128]{1,0:T(8,128)S(1)} %pad_maximum_fusion), channel_id=1, source_target_pairs={{0,8},{1,5},{2,10},{3,7},{4,12},{5,1},{6,14},{7,3},{8,0},{9,13},{1... | collective-permute-start | bytes 983048 | tf_op jit(solution)/shard_map/ppermute | solution.py:151
  30.6 1.3 %collective-permute-start = (f32[8,128]{1,0:T(8,128)S(1)}, f32[8,128]{1,0:T(8,128)S(1)}, u32[]{:S(2)}, u32[]{:S(2)}) collective-permute-start(f32[8,128]{1,0:T(8,128)S(1)} %shard_map.68), channel_id=1, source_target_pairs={{0,1},{1,0},{2,3},{3,2},{4,5},{5,4},{6,7},{7,6},{8,9},{9,8},{10,11... | collective-permute-start | bytes 12296 | tf_op jit(solution)/shard_map/ppermute | solution.py:137
  31.8 3.0 %collective-permute-start.1 = (f32[8,128]{1,0:T(8,128)S(1)}, f32[8,128]{1,0:T(8,128)S(1)}, u32[]{:S(2)}, u32[]{:S(2)}) collective-permute-start(f32[8,128]{1,0:T(8,128)S(1)} %add.9), channel_id=1, source_target_pairs={{0,3},{1,2},{2,1},{3,0},{4,7},{5,6},{6,5},{7,4},{8,11},{9,10},{10,... | collective-permute-start | bytes 12296 | tf_op jit(solution)/shard_map/ppermute | solution.py:137

commit v7 on v6

--- a/solution.py
+++ b/solution.py
@@ -123,7 +123,7 @@
 
 
 def from_middle(count):
-    return sorted(range(count), key=lambda i: (i % 2, abs(40 * (i // 2) - 19 * (count // 2))))
+    return sorted(range(count), key=lambda i: (i % 2, abs(40 * (i // 2) - (19 + 2 * (i % 2)) * (count // 2))))
 
 
 def on_device(grads, weight, moment_one, moment_two):

time: 36.3 us -> 35.8 us (0.986)
  starting transfers between devices: 21.7 us -> 19.4 us
  waiting for transfers between devices: 11 us -> 12.9 us
    ppermute x3, starting transfers between devices: 6.52 us -> 3.83 us  [spread(): moments.append(lax.ppermute(held, ('rep', 'shard'), pairs))]
    all_to_all x1, waiting for transfers between devices: 3.83 us -> 6.08 us  [on_device(): lax.all_to_all(trimmed, 'rep', 0, 0, tiled=True, axis_index_groups=[order])]
    ppermute x2, waiting for transfers between devices: 1.04 us -> 2.1 us  [swap(): lax.ppermute(value, axis, [(i, i ^ mask) for i in range(lax.axis_size(axi...]
    all_to_all x1, waiting for transfers between devices: 1.06 us -> 0.15 us  [on_device(): lax.all_to_all(tiled.reshape(count, tiles, SUB, LANES), 'rep', 0, 0, tile...]
    all_to_all x1, starting transfers between devices: 5.35 us -> 6.26 us  [on_device(): lax.all_to_all(trimmed, 'rep', 0, 0, tiled=True, axis_index_groups=[order])]
    ppermute x3, waiting for transfers between devices: 5.08 us -> 4.52 us  [spread(): moments.append(lax.ppermute(held, ('rep', 'shard'), pairs))]
    ppermute x2, starting transfers between devices: 1.91 us -> 1.36 us  [swap(): lax.ppermute(value, axis, [(i, i ^ mask) for i in range(lax.axis_size(axi...]
where the time goes in v7:
time: 35.8 us; the launch traced here: 35.4 us
  starting transfers between devices  19.4 us (54%)
  waiting for transfers between devices  12.9 us (36%)
  Pallas kernels  2.41 us (7%)
  between operations  0.69 us (2%)
    all_to_all x1, starting transfers between devices, on_device(): lax.all_to_all(tiled.reshape(count, tiles, SUB, LANES), 'rep', 0, 0, tile...  7.96 us
    all_to_all x1, starting transfers between devices, on_device(): lax.all_to_all(trimmed, 'rep', 0, 0, tiled=True, axis_index_groups=[order])  6.26 us
    all_to_all x1, waiting for transfers between devices, on_device(): lax.all_to_all(trimmed, 'rep', 0, 0, tiled=True, axis_index_groups=[order])  6.08 us
    ppermute x3, waiting for transfers between devices, spread(): moments.append(lax.ppermute(held, ('rep', 'shard'), pairs))  4.52 us
    ppermute x3, starting transfers between devices, spread(): moments.append(lax.ppermute(held, ('rep', 'shard'), pairs))  3.83 us
    ppermute x2, waiting for transfers between devices, swap(): lax.ppermute(value, axis, [(i, i ^ mask) for i in range(lax.axis_size(axi...  2.1 us
    ppermute x2, starting transfers between devices, swap(): lax.ppermute(value, axis, [(i, i ^ mask) for i in range(lax.axis_size(axi...  1.36 us
    pallas_call x1, Pallas kernels, on_device(): pl.pallas_call(functools.partial(adam_kernel, params), out_shape=(f32(*we...  1.02 us
  transfers between devices with their start and end apart: 7, of which 6 were waited for; matrix products, arithmetic and copies ran while one was open for 0% of the time, Pallas kernels for 4%

profile of v7, /device:TPU:0, one launch (start us, length us, event | category | flops | bytes accessed | tf_op | source)
XLA Modules:
  0.0 35.4 jit_solution(14376510162672131892)
XLA Ops:
  0.6 0.0 copy-start.1
  0.6 0.0 copy-start.2
  0.7 8.0 %all-to-all-start = ((f32[8,10,8,128]{3,2,1,0:T(8,128)}), f32[8,10,8,128]{3,2,1,0:T(8,128)S(1)}, u32[]{:S(2)}, u32[]{:S(2)}) async-start(f32[8,10,8,128]{3,2,1,0:T(8,128)} %bitcast.18), calls=%async_computation | async-start | bytes 655360 | tf_op jit(solution)/shard_map/all_to_all | solution.py:141
  8.6 0.0 copy-done.1
  8.6 0.0 copy-done.2
  8.6 1.5 %collective-permute-start.2 = (f32[160,128]{1,0:T(8,128)S(1)}, f32[160,128]{1,0:T(8,128)S(1)}, u32[]{:S(2)}, u32[]{:S(2)}) collective-permute-start(f32[160,128]{1,0:T(8,128)S(1)} %pad_maximum_fusion.2.refs_0_.own_moments_ref), channel_id=1, source_target_pairs={{0,4},{1,9},{2,6},{3,11},{4,0},{5,13},{6,2},{7,15},{8,12},{9,1},{1... | collective-permute-start | bytes 245768 | tf_op jit(solution)/shard_map/ppermute | solution.py:151
  10.2 4.3 %collective-permute-done.2.refs_1_ = f32[160,128]{1,0:T(8,128)S(1)} collective-permute-done((f32[160,128]{1,0:T(8,128)S(1)}, f32[160,128]{1,0:T(8,128)S(1)}, u32[]{:S(2)}, u32[]{:S(2)}) %collective-permute-start.2) | collective-permute-done | bytes 81952 | tf_op jit(solution)/shard_map/ppermute | solution.py:151
  14.4 1.6 %collective-permute-start.3 = (f32[320,128]{1,0:T(8,128)S(1)}, f32[320,128]{1,0:T(8,128)S(1)}, u32[]{:S(2)}, u32[]{:S(2)}) collective-permute-start(f32[320,128]{1,0:T(8,128)S(1)} %pad_maximum_fusion.1), channel_id=1, source_target_pairs={{0,24},{1,25},{2,26},{3,27},{4,28},{5,29},{6,30},{7,31},{8,16},{9,... | collective-permute-start | bytes 491528 | tf_op jit(solution)/shard_map/ppermute | solution.py:151
  16.0 0.2 all-to-all-done.received_ref
  16.1 0.8 %shard_map.67 = f32[8,10,8,128]{3,2,1,0:T(8,128)} custom-call(f32[8,10,8,128]{3,2,1,0:T(8,128)S(1)} %all-to-all-done.received_ref), custom_call_target="tpu_custom_call" | custom-call | tf_op jit(solution)/shard_map/pallas_call | solution.py:155
  16.9 6.3 %all-to-all-start.1 = ((f32[8,10,8,128]{3,2,1,0:T(8,128)}), f32[8,10,8,128]{3,2,1,0:T(8,128)S(1)}, u32[]{:S(2)}, u32[]{:S(2)}) async-start(f32[8,10,8,128]{3,2,1,0:T(8,128)} %shard_map.67), calls=%async_computation.1 | async-start | bytes 655360 | tf_op jit(solution)/shard_map/all_to_all | solution.py:162
  23.2 0.0 collective-permute-done.3.refs_2_
  23.2 0.0 copy-start
  23.2 0.7 %collective-permute-start.4 = (f32[640,128]{1,0:T(8,128)S(1)}, f32[640,128]{1,0:T(8,128)S(1)}, u32[]{:S(2)}, u32[]{:S(2)}) collective-permute-start(f32[640,128]{1,0:T(8,128)S(1)} %pad_maximum_fusion), channel_id=1, source_target_pairs={{0,8},{1,5},{2,10},{3,7},{4,12},{5,1},{6,14},{7,3},{8,0},{9,13},{1... | collective-permute-start | bytes 983048 | tf_op jit(solution)/shard_map/ppermute | solution.py:151
  24.0 6.1 %all-to-all-done.1.trimmed_ref = f32[8,10,8,128]{3,2,1,0:T(8,128)S(1)} async-done(((f32[8,10,8,128]{3,2,1,0:T(8,128)}), f32[8,10,8,128]{3,2,1,0:T(8,128)S(1)}, u32[]{:S(2)}, u32[]{:S(2)}) %all-to-all-start.1) | async-done | bytes 327712 | tf_op jit(solution)/shard_map/all_to_all | solution.py:162
  30.1 0.1 shard_map.68
  30.1 0.1 collective-permute-start
  30.2 1.2 %collective-permute-done = f32[8,128]{1,0:T(8,128)S(1)} collective-permute-done((f32[8,128]{1,0:T(8,128)S(1)}, f32[8,128]{1,0:T(8,128)S(1)}, u32[]{:S(2)}, u32[]{:S(2)}) %collective-permute-start) | collective-permute-done | bytes 4128 | tf_op jit(solution)/shard_map/ppermute | solution.py:137
  31.4 1.3 %collective-permute-start.1 = (f32[8,128]{1,0:T(8,128)S(1)}, f32[8,128]{1,0:T(8,128)S(1)}, u32[]{:S(2)}, u32[]{:S(2)}) collective-permute-start(f32[8,128]{1,0:T(8,128)S(1)} %add.9), channel_id=1, source_target_pairs={{0,3},{1,2},{2,1},{3,0},{4,7},{5,6},{6,5},{7,4},{8,11},{9,10},{10,... | collective-permute-start | bytes 12296 | tf_op jit(solution)/shard_map/ppermute | solution.py:137
  32.7 0.2 collective-permute-done.4.refs_3_
  32.9 0.0 copy-done
  32.9 0.5 %shard_map.69 = (f32[640,128]{1,0:T(8,128)S(1)}, f32[640,128]{1,0:T(8,128)S(1)}, f32[640,128]{1,0:T(8,128)S(1)}, f32[640,128]{1,0:T(8,128)S(1)}, f32[640,128]{1,0:T(8,128)S(1)}, /*index=5*/f32[80,128]{1,0:T(8,128)S(1)}) custom-call(s32[1]{0:T(128)} %bitcast.3.at_ref, f32[2,8,5120]{2,1,0:T(8,128)S(1)} %copy-done, f32[640,128]{1,0:T(8,128)S(1)} %bitcast.11, ...), custom_call_target="tpu_custom_call" | custom-call | tf_op jit(solution)/shard_map/pallas_call | solution.py:170
  33.5 1.0 %collective-permute-done.1 = f32[8,128]{1,0:T(8,128)S(1)} collective-permute-done((f32[8,128]{1,0:T(8,128)S(1)}, f32[8,128]{1,0:T(8,128)S(1)}, u32[]{:S(2)}, u32[]{:S(2)}) %collective-permute-start.1) | collective-permute-done | bytes 4128 | tf_op jit(solution)/shard_map/ppermute | solution.py:137
  34.4 1.0 %shard_map.70 = (f32[2,8,5120]{2,1,0:T(8,128)}, f32[80,128]{1,0:T(8,128)}, f32[80,128]{1,0:T(8,128)}) custom-call(f32[8,128]{1,0:T(8,128)S(1)} %add.10.squares_ref, f32[640,128]{1,0:T(8,128)S(1)} %get-tuple-element.12.kept_ref, f32[640,128]{1,0:T(8,128)S(1)} %get-tuple-element.13.one_ref, f32[640,128]{1,0:T(8,128)S(1)} %get-tuple-element.14.one_slope_ref, ...), custom_call_target="tpu_custom_call" | custom-call | tf_op jit(solution)/shard_map/pallas_call | solution.py:178
  (5 shorter events, 0.0 us)
Async XLA Ops:
  0.6 8.0 %copy-start.1 = (f32[2,1,5120]{2,1,0:T(1,128)S(1)}, f32[2,1,5120]{2,1,0:T(1,128)}, u32[]{:S(2)}) copy-start(f32[2,1,5120]{2,1,0:T(1,128)} %param.7) | copy-start | bytes 122884
  0.6 8.0 %copy-start.2 = (f32[2,1,5120]{2,1,0:T(1,128)S(1)}, f32[2,1,5120]{2,1,0:T(1,128)}, u32[]{:S(2)}) copy-start(f32[2,1,5120]{2,1,0:T(1,128)} %param.6) | copy-start | bytes 122884
  0.7 15.5 %all-to-all-start = ((f32[8,10,8,128]{3,2,1,0:T(8,128)}), f32[8,10,8,128]{3,2,1,0:T(8,128)S(1)}, u32[]{:S(2)}, u32[]{:S(2)}) async-start(f32[8,10,8,128]{3,2,1,0:T(8,128)} %bitcast.18), calls=%async_computation | async-start | bytes 655360 | tf_op jit(solution)/shard_map/all_to_all | solution.py:141
  8.6 5.8 %collective-permute-start.2 = (f32[160,128]{1,0:T(8,128)S(1)}, f32[160,128]{1,0:T(8,128)S(1)}, u32[]{:S(2)}, u32[]{:S(2)}) collective-permute-start(f32[160,128]{1,0:T(8,128)S(1)} %pad_maximum_fusion.2.refs_0_.own_moments_ref), channel_id=1, source_target_pairs={{0,4},{1,9},{2,6},{3,11},{4,0},{5,13},{6,2},{7,15},{8,12},{9,1},{1... | collective-permute-start | bytes 245768 | tf_op jit(solution)/shard_map/ppermute | solution.py:151
  14.4 8.7 %collective-permute-start.3 = (f32[320,128]{1,0:T(8,128)S(1)}, f32[320,128]{1,0:T(8,128)S(1)}, u32[]{:S(2)}, u32[]{:S(2)}) collective-permute-start(f32[320,128]{1,0:T(8,128)S(1)} %pad_maximum_fusion.1), channel_id=1, source_target_pairs={{0,24},{1,25},{2,26},{3,27},{4,28},{5,29},{6,30},{7,31},{8,16},{9,... | collective-permute-start | bytes 491528 | tf_op jit(solution)/shard_map/ppermute | solution.py:151
  16.9 13.1 %all-to-all-start.1 = ((f32[8,10,8,128]{3,2,1,0:T(8,128)}), f32[8,10,8,128]{3,2,1,0:T(8,128)S(1)}, u32[]{:S(2)}, u32[]{:S(2)}) async-start(f32[8,10,8,128]{3,2,1,0:T(8,128)} %shard_map.67), calls=%async_computation.1 | async-start | bytes 655360 | tf_op jit(solution)/shard_map/all_to_all | solution.py:162
  23.2 9.7 %copy-start = (f32[2,8,5120]{2,1,0:T(8,128)S(1)}, f32[2,8,5120]{2,1,0:T(8,128)}, u32[]{:S(2)}) copy-start(f32[2,8,5120]{2,1,0:T(8,128)} %weight_ref.1) | copy-start | bytes 983044
  23.2 9.7 %collective-permute-start.4 = (f32[640,128]{1,0:T(8,128)S(1)}, f32[640,128]{1,0:T(8,128)S(1)}, u32[]{:S(2)}, u32[]{:S(2)}) collective-permute-start(f32[640,128]{1,0:T(8,128)S(1)} %pad_maximum_fusion), channel_id=1, source_target_pairs={{0,8},{1,5},{2,10},{3,7},{4,12},{5,1},{6,14},{7,3},{8,0},{9,13},{1... | collective-permute-start | bytes 983048 | tf_op jit(solution)/shard_map/ppermute | solution.py:151
  30.1 1.2 %collective-permute-start = (f32[8,128]{1,0:T(8,128)S(1)}, f32[8,128]{1,0:T(8,128)S(1)}, u32[]{:S(2)}, u32[]{:S(2)}) collective-permute-start(f32[8,128]{1,0:T(8,128)S(1)} %shard_map.68), channel_id=1, source_target_pairs={{0,1},{1,0},{2,3},{3,2},{4,5},{5,4},{6,7},{7,6},{8,9},{9,8},{10,11... | collective-permute-start | bytes 12296 | tf_op jit(solution)/shard_map/ppermute | solution.py:137
  31.4 3.0 %collective-permute-start.1 = (f32[8,128]{1,0:T(8,128)S(1)}, f32[8,128]{1,0:T(8,128)S(1)}, u32[]{:S(2)}, u32[]{:S(2)}) collective-permute-start(f32[8,128]{1,0:T(8,128)S(1)} %add.9), channel_id=1, source_target_pairs={{0,3},{1,2},{2,1},{3,0},{4,7},{5,6},{6,5},{7,4},{8,11},{9,10},{10,... | collective-permute-start | bytes 12296 | tf_op jit(solution)/shard_map/ppermute | solution.py:137

commit v8 on v7

--- a/solution.py
+++ b/solution.py
@@ -142,7 +142,8 @@
 
     moments = [jnp.concatenate([moment_one.reshape(run, LANES), moment_two.reshape(run, LANES)])]
     orders = [[(0, 0)]]
-    masks = list(zip([1, 6, 2], [2, 6, 1]))
+    middle = [3 << bit for bit in range(1, (count - 1).bit_length() - 1)]
+    masks = list(zip([1, *middle, 2], [2, *middle, 1]))
 
     def spread(mask):
         held = moments[0] if len(moments) == 1 else jnp.concatenate(moments)

time: 35.8 us -> 35.8 us (level)
  no operation moved by 1% of the time
where the time goes in v8:
time: 35.8 us; the launch traced here: 35.4 us
  starting transfers between devices  19.4 us (54%)
  waiting for transfers between devices  12.9 us (36%)
  Pallas kernels  2.41 us (7%)
  between operations  0.69 us (2%)
    all_to_all x1, starting transfers between devices, on_device(): lax.all_to_all(tiled.reshape(count, tiles, SUB, LANES), 'rep', 0, 0, tile...  7.96 us
    all_to_all x1, starting transfers between devices, on_device(): lax.all_to_all(trimmed, 'rep', 0, 0, tiled=True, axis_index_groups=[order])  6.26 us
    all_to_all x1, waiting for transfers between devices, on_device(): lax.all_to_all(trimmed, 'rep', 0, 0, tiled=True, axis_index_groups=[order])  6.08 us
    ppermute x3, waiting for transfers between devices, spread(): moments.append(lax.ppermute(held, ('rep', 'shard'), pairs))  4.52 us
    ppermute x3, starting transfers between devices, spread(): moments.append(lax.ppermute(held, ('rep', 'shard'), pairs))  3.83 us
    ppermute x2, waiting for transfers between devices, swap(): lax.ppermute(value, axis, [(i, i ^ mask) for i in range(lax.axis_size(axi...  2.1 us
    ppermute x2, starting transfers between devices, swap(): lax.ppermute(value, axis, [(i, i ^ mask) for i in range(lax.axis_size(axi...  1.36 us
    pallas_call x1, Pallas kernels, on_device(): pl.pallas_call(functools.partial(adam_kernel, params), out_shape=(f32(*we...  1.02 us
  transfers between devices with their start and end apart: 7, of which 6 were waited for; matrix products, arithmetic and copies ran while one was open for 0% of the time, Pallas kernels for 4%

profile of v8, /device:TPU:0, one launch (start us, length us, event | category | flops | bytes accessed | tf_op | source)
XLA Modules:
  0.0 35.4 jit_solution(14376510162672131892)
XLA Ops:
  0.6 0.0 copy-start.1
  0.6 0.0 copy-start.2
  0.7 8.0 %all-to-all-start = ((f32[8,10,8,128]{3,2,1,0:T(8,128)}), f32[8,10,8,128]{3,2,1,0:T(8,128)S(1)}, u32[]{:S(2)}, u32[]{:S(2)}) async-start(f32[8,10,8,128]{3,2,1,0:T(8,128)} %bitcast.18), calls=%async_computation | async-start | bytes 655360 | tf_op jit(solution)/shard_map/all_to_all | solution.py:141
  8.6 0.0 copy-done.1
  8.6 0.0 copy-done.2
  8.6 1.5 %collective-permute-start.2 = (f32[160,128]{1,0:T(8,128)S(1)}, f32[160,128]{1,0:T(8,128)S(1)}, u32[]{:S(2)}, u32[]{:S(2)}) collective-permute-start(f32[160,128]{1,0:T(8,128)S(1)} %pad_maximum_fusion.2.refs_0_.own_moments_ref), channel_id=1, source_target_pairs={{0,4},{1,9},{2,6},{3,11},{4,0},{5,13},{6,2},{7,15},{8,12},{9,1},{1... | collective-permute-start | bytes 245768 | tf_op jit(solution)/shard_map/ppermute | solution.py:152
  10.2 4.3 %collective-permute-done.2.refs_1_ = f32[160,128]{1,0:T(8,128)S(1)} collective-permute-done((f32[160,128]{1,0:T(8,128)S(1)}, f32[160,128]{1,0:T(8,128)S(1)}, u32[]{:S(2)}, u32[]{:S(2)}) %collective-permute-start.2) | collective-permute-done | bytes 81952 | tf_op jit(solution)/shard_map/ppermute | solution.py:152
  14.4 1.6 %collective-permute-start.3 = (f32[320,128]{1,0:T(8,128)S(1)}, f32[320,128]{1,0:T(8,128)S(1)}, u32[]{:S(2)}, u32[]{:S(2)}) collective-permute-start(f32[320,128]{1,0:T(8,128)S(1)} %pad_maximum_fusion.1), channel_id=1, source_target_pairs={{0,24},{1,25},{2,26},{3,27},{4,28},{5,29},{6,30},{7,31},{8,16},{9,... | collective-permute-start | bytes 491528 | tf_op jit(solution)/shard_map/ppermute | solution.py:152
  16.0 0.2 all-to-all-done.received_ref
  16.1 0.8 %shard_map.67 = f32[8,10,8,128]{3,2,1,0:T(8,128)} custom-call(f32[8,10,8,128]{3,2,1,0:T(8,128)S(1)} %all-to-all-done.received_ref), custom_call_target="tpu_custom_call" | custom-call | tf_op jit(solution)/shard_map/pallas_call | solution.py:156
  16.9 6.3 %all-to-all-start.1 = ((f32[8,10,8,128]{3,2,1,0:T(8,128)}), f32[8,10,8,128]{3,2,1,0:T(8,128)S(1)}, u32[]{:S(2)}, u32[]{:S(2)}) async-start(f32[8,10,8,128]{3,2,1,0:T(8,128)} %shard_map.67), calls=%async_computation.1 | async-start | bytes 655360 | tf_op jit(solution)/shard_map/all_to_all | solution.py:163
  23.2 0.0 collective-permute-done.3.refs_2_
  23.2 0.0 copy-start
  23.2 0.7 %collective-permute-start.4 = (f32[640,128]{1,0:T(8,128)S(1)}, f32[640,128]{1,0:T(8,128)S(1)}, u32[]{:S(2)}, u32[]{:S(2)}) collective-permute-start(f32[640,128]{1,0:T(8,128)S(1)} %pad_maximum_fusion), channel_id=1, source_target_pairs={{0,8},{1,5},{2,10},{3,7},{4,12},{5,1},{6,14},{7,3},{8,0},{9,13},{1... | collective-permute-start | bytes 983048 | tf_op jit(solution)/shard_map/ppermute | solution.py:152
  24.0 6.1 %all-to-all-done.1.trimmed_ref = f32[8,10,8,128]{3,2,1,0:T(8,128)S(1)} async-done(((f32[8,10,8,128]{3,2,1,0:T(8,128)}), f32[8,10,8,128]{3,2,1,0:T(8,128)S(1)}, u32[]{:S(2)}, u32[]{:S(2)}) %all-to-all-start.1) | async-done | bytes 327712 | tf_op jit(solution)/shard_map/all_to_all | solution.py:163
  30.1 0.1 shard_map.68
  30.1 0.1 collective-permute-start
  30.2 1.2 %collective-permute-done = f32[8,128]{1,0:T(8,128)S(1)} collective-permute-done((f32[8,128]{1,0:T(8,128)S(1)}, f32[8,128]{1,0:T(8,128)S(1)}, u32[]{:S(2)}, u32[]{:S(2)}) %collective-permute-start) | collective-permute-done | bytes 4128 | tf_op jit(solution)/shard_map/ppermute | solution.py:137
  31.4 1.3 %collective-permute-start.1 = (f32[8,128]{1,0:T(8,128)S(1)}, f32[8,128]{1,0:T(8,128)S(1)}, u32[]{:S(2)}, u32[]{:S(2)}) collective-permute-start(f32[8,128]{1,0:T(8,128)S(1)} %add.9), channel_id=1, source_target_pairs={{0,3},{1,2},{2,1},{3,0},{4,7},{5,6},{6,5},{7,4},{8,11},{9,10},{10,... | collective-permute-start | bytes 12296 | tf_op jit(solution)/shard_map/ppermute | solution.py:137
  32.7 0.2 collective-permute-done.4.refs_3_
  32.9 0.0 copy-done
  32.9 0.5 %shard_map.69 = (f32[640,128]{1,0:T(8,128)S(1)}, f32[640,128]{1,0:T(8,128)S(1)}, f32[640,128]{1,0:T(8,128)S(1)}, f32[640,128]{1,0:T(8,128)S(1)}, f32[640,128]{1,0:T(8,128)S(1)}, /*index=5*/f32[80,128]{1,0:T(8,128)S(1)}) custom-call(s32[1]{0:T(128)} %bitcast.3.at_ref, f32[2,8,5120]{2,1,0:T(8,128)S(1)} %copy-done, f32[640,128]{1,0:T(8,128)S(1)} %bitcast.11, ...), custom_call_target="tpu_custom_call" | custom-call | tf_op jit(solution)/shard_map/pallas_call | solution.py:171
  33.5 1.0 %collective-permute-done.1 = f32[8,128]{1,0:T(8,128)S(1)} collective-permute-done((f32[8,128]{1,0:T(8,128)S(1)}, f32[8,128]{1,0:T(8,128)S(1)}, u32[]{:S(2)}, u32[]{:S(2)}) %collective-permute-start.1) | collective-permute-done | bytes 4128 | tf_op jit(solution)/shard_map/ppermute | solution.py:137
  34.4 1.0 %shard_map.70 = (f32[2,8,5120]{2,1,0:T(8,128)}, f32[80,128]{1,0:T(8,128)}, f32[80,128]{1,0:T(8,128)}) custom-call(f32[8,128]{1,0:T(8,128)S(1)} %add.10.squares_ref, f32[640,128]{1,0:T(8,128)S(1)} %get-tuple-element.12.kept_ref, f32[640,128]{1,0:T(8,128)S(1)} %get-tuple-element.13.one_ref, f32[640,128]{1,0:T(8,128)S(1)} %get-tuple-element.14.one_slope_ref, ...), custom_call_target="tpu_custom_call" | custom-call | tf_op jit(solution)/shard_map/pallas_call | solution.py:179
  (5 shorter events, 0.0 us)
Async XLA Ops:
  0.6 8.0 %copy-start.1 = (f32[2,1,5120]{2,1,0:T(1,128)S(1)}, f32[2,1,5120]{2,1,0:T(1,128)}, u32[]{:S(2)}) copy-start(f32[2,1,5120]{2,1,0:T(1,128)} %param.7) | copy-start | bytes 122884
  0.6 8.0 %copy-start.2 = (f32[2,1,5120]{2,1,0:T(1,128)S(1)}, f32[2,1,5120]{2,1,0:T(1,128)}, u32[]{:S(2)}) copy-start(f32[2,1,5120]{2,1,0:T(1,128)} %param.6) | copy-start | bytes 122884
  0.7 15.5 %all-to-all-start = ((f32[8,10,8,128]{3,2,1,0:T(8,128)}), f32[8,10,8,128]{3,2,1,0:T(8,128)S(1)}, u32[]{:S(2)}, u32[]{:S(2)}) async-start(f32[8,10,8,128]{3,2,1,0:T(8,128)} %bitcast.18), calls=%async_computation | async-start | bytes 655360 | tf_op jit(solution)/shard_map/all_to_all | solution.py:141
  8.6 5.8 %collective-permute-start.2 = (f32[160,128]{1,0:T(8,128)S(1)}, f32[160,128]{1,0:T(8,128)S(1)}, u32[]{:S(2)}, u32[]{:S(2)}) collective-permute-start(f32[160,128]{1,0:T(8,128)S(1)} %pad_maximum_fusion.2.refs_0_.own_moments_ref), channel_id=1, source_target_pairs={{0,4},{1,9},{2,6},{3,11},{4,0},{5,13},{6,2},{7,15},{8,12},{9,1},{1... | collective-permute-start | bytes 245768 | tf_op jit(solution)/shard_map/ppermute | solution.py:152
  14.4 8.7 %collective-permute-start.3 = (f32[320,128]{1,0:T(8,128)S(1)}, f32[320,128]{1,0:T(8,128)S(1)}, u32[]{:S(2)}, u32[]{:S(2)}) collective-permute-start(f32[320,128]{1,0:T(8,128)S(1)} %pad_maximum_fusion.1), channel_id=1, source_target_pairs={{0,24},{1,25},{2,26},{3,27},{4,28},{5,29},{6,30},{7,31},{8,16},{9,... | collective-permute-start | bytes 491528 | tf_op jit(solution)/shard_map/ppermute | solution.py:152
  16.9 13.1 %all-to-all-start.1 = ((f32[8,10,8,128]{3,2,1,0:T(8,128)}), f32[8,10,8,128]{3,2,1,0:T(8,128)S(1)}, u32[]{:S(2)}, u32[]{:S(2)}) async-start(f32[8,10,8,128]{3,2,1,0:T(8,128)} %shard_map.67), calls=%async_computation.1 | async-start | bytes 655360 | tf_op jit(solution)/shard_map/all_to_all | solution.py:163
  23.2 9.7 %copy-start = (f32[2,8,5120]{2,1,0:T(8,128)S(1)}, f32[2,8,5120]{2,1,0:T(8,128)}, u32[]{:S(2)}) copy-start(f32[2,8,5120]{2,1,0:T(8,128)} %weight_ref.1) | copy-start | bytes 983044
  23.2 9.7 %collective-permute-start.4 = (f32[640,128]{1,0:T(8,128)S(1)}, f32[640,128]{1,0:T(8,128)S(1)}, u32[]{:S(2)}, u32[]{:S(2)}) collective-permute-start(f32[640,128]{1,0:T(8,128)S(1)} %pad_maximum_fusion), channel_id=1, source_target_pairs={{0,8},{1,5},{2,10},{3,7},{4,12},{5,1},{6,14},{7,3},{8,0},{9,13},{1... | collective-permute-start | bytes 983048 | tf_op jit(solution)/shard_map/ppermute | solution.py:152
  30.1 1.2 %collective-permute-start = (f32[8,128]{1,0:T(8,128)S(1)}, f32[8,128]{1,0:T(8,128)S(1)}, u32[]{:S(2)}, u32[]{:S(2)}) collective-permute-start(f32[8,128]{1,0:T(8,128)S(1)} %shard_map.68), channel_id=1, source_target_pairs={{0,1},{1,0},{2,3},{3,2},{4,5},{5,4},{6,7},{7,6},{8,9},{9,8},{10,11... | collective-permute-start | bytes 12296 | tf_op jit(solution)/shard_map/ppermute | solution.py:137
  31.4 3.0 %collective-permute-start.1 = (f32[8,128]{1,0:T(8,128)S(1)}, f32[8,128]{1,0:T(8,128)S(1)}, u32[]{:S(2)}, u32[]{:S(2)}) collective-permute-start(f32[8,128]{1,0:T(8,128)S(1)} %add.9), channel_id=1, source_target_pairs={{0,3},{1,2},{2,1},{3,0},{4,7},{5,6},{6,5},{7,4},{8,11},{9,10},{10,... | collective-permute-start | bytes 12296 | tf_op jit(solution)/shard_map/ppermute | solution.py:137

commit v9 on v8

--- a/solution.py
+++ b/solution.py
@@ -38,13 +38,19 @@
     return total
 
 
-def trim_kernel(trim, received_ref, trimmed_ref):
+def trim_kernel(trim, received_ref, trimmed_ref, mean_ref, done):
     count, tiles = received_ref.shape[:2]
-    for tile in range(tiles):
-        values = [received_ref[i, tile] for i in range(count)]
-        mean = middle_sum(values, trim) / (count - 2 * trim)
+    copies = []
+    for first, last in ((0, tiles // 2), (tiles // 2, tiles)):
+        for tile in range(first, last):
+            values = [received_ref[i, tile] for i in range(count)]
+            mean_ref[tile] = middle_sum(values, trim) / (count - 2 * trim)
+        part = slice(first, last)
         for i in range(count):
-            trimmed_ref[i, tile] = mean
+            copies.append(pltpu.make_async_copy(mean_ref.at[part], trimmed_ref.at[i, part], done.at[len(copies)]))
+            copies[-1].start()
+    for copy in copies:
+        copy.wait()
 
 
 def square_kernel(trimmed_ref, squares_ref):
@@ -157,14 +163,15 @@
         functools.partial(trim_kernel, count // 8),
         out_shape=f32(count, tiles, SUB, LANES),
         in_specs=[VMEM],
-        out_specs=VMEM,
+        out_specs=pl.BlockSpec(memory_space=pl.ANY),
+        scratch_shapes=[pltpu.VMEM((tiles, SUB, LANES), jnp.float32), pltpu.SemaphoreType.DMA((2 * count,))],
         compiler_params=PARAMS,
     )(received)
     trimmed = lax.all_to_all(trimmed, "rep", 0, 0, tiled=True, axis_index_groups=[order])
     squares = pl.pallas_call(
         square_kernel, out_shape=f32(SUB, LANES), in_specs=[VMEM], out_specs=VMEM, compiler_params=PARAMS
     )(trimmed)
-    for mask in [1] + [(1 << bit) + 1 for bit in range(1, (shards - 1).bit_length())]:
+    for mask in [(1 << bit) + 1 for bit in range(1, (shards - 1).bit_length())] + [1]:
         squares += swap(squares, "shard", mask)
     at = lax.axis_index(("rep", "shard")).reshape(1)
     flat = f32(weight.size // LANES, LANES)

time: 35.8 us -> 35.9 us (level)
  starting transfers between devices: 19.4 us -> 18.1 us
  waiting for transfers between devices: 12.9 us -> 14.1 us
    ppermute x2, waiting for transfers between devices: 2.1 us -> 3.53 us  [swap(): lax.ppermute(value, axis, [(i, i ^ mask) for i in range(lax.axis_size(axi...]
    ppermute x2, starting transfers between devices: 1.36 us -> 0.18 us  [swap(): lax.ppermute(value, axis, [(i, i ^ mask) for i in range(lax.axis_size(axi...]
  transfers between devices with their start and end apart: 7 -> 7, of which waited for: 6 -> 5; matrix products, arithmetic and copies ran while one was open for 0% -> 0% of each run, Pallas kernels for 4% -> 4%
where the time goes in v9:
time: 35.9 us; the launch traced here: 35.5 us
  starting transfers between devices  18.1 us (50%)
  waiting for transfers between devices  14.1 us (39%)
  Pallas kernels  2.5 us (7%)
  between operations  0.7 us (2%)
    all_to_all x1, starting transfers between devices, on_device(): lax.all_to_all(tiled.reshape(count, tiles, SUB, LANES), 'rep', 0, 0, tile...  7.96 us
    all_to_all x1, starting transfers between devices, on_device(): lax.all_to_all(trimmed, 'rep', 0, 0, tiled=True, axis_index_groups=[order])  6.27 us
    all_to_all x1, waiting for transfers between devices, on_device(): lax.all_to_all(trimmed, 'rep', 0, 0, tiled=True, axis_index_groups=[order])  6.19 us
    ppermute x3, waiting for transfers between devices, spread(): moments.append(lax.ppermute(held, ('rep', 'shard'), pairs))  4.27 us
    ppermute x3, starting transfers between devices, spread(): moments.append(lax.ppermute(held, ('rep', 'shard'), pairs))  3.72 us
    ppermute x2, waiting for transfers between devices, swap(): lax.ppermute(value, axis, [(i, i ^ mask) for i in range(lax.axis_size(axi...  3.53 us
    pallas_call x1, Pallas kernels, on_device(): pl.pallas_call(functools.partial(adam_kernel, params), out_shape=(f32(*we...  1.02 us
    pallas_call x1, Pallas kernels, on_device(): pl.pallas_call(functools.partial(trim_kernel, count // 8), out_shape=f32(...  0.87 us
  transfers between devices with their start and end apart: 7, of which 5 were waited for; matrix products, arithmetic and copies ran while one was open for 0% of the time, Pallas kernels for 4%

profile of v9, /device:TPU:0, one launch (start us, length us, event | category | flops | bytes accessed | tf_op | source)
XLA Modules:
  0.0 35.5 jit_solution(6774902632539094112)
XLA Ops:
  0.6 0.0 copy-start.1
  0.6 0.0 copy-start.2
  0.7 8.0 %all-to-all-start = ((f32[8,10,8,128]{3,2,1,0:T(8,128)}), f32[8,10,8,128]{3,2,1,0:T(8,128)S(1)}, u32[]{:S(2)}, u32[]{:S(2)}) async-start(f32[8,10,8,128]{3,2,1,0:T(8,128)} %bitcast.18), calls=%async_computation | async-start | bytes 655360 | tf_op jit(solution)/shard_map/all_to_all | solution.py:147
  8.6 0.0 copy-done.1
  8.6 0.0 copy-done.2
  8.6 1.5 %collective-permute-start.2 = (f32[160,128]{1,0:T(8,128)S(1)}, f32[160,128]{1,0:T(8,128)S(1)}, u32[]{:S(2)}, u32[]{:S(2)}) collective-permute-start(f32[160,128]{1,0:T(8,128)S(1)} %pad_maximum_fusion.2.refs_0_.own_moments_ref), channel_id=1, source_target_pairs={{0,4},{1,9},{2,6},{3,11},{4,0},{5,13},{6,2},{7,15},{8,12},{9,1},{1... | collective-permute-start | bytes 245768 | tf_op jit(solution)/shard_map/ppermute | solution.py:158
  10.2 4.3 %collective-permute-done.2.refs_1_ = f32[160,128]{1,0:T(8,128)S(1)} collective-permute-done((f32[160,128]{1,0:T(8,128)S(1)}, f32[160,128]{1,0:T(8,128)S(1)}, u32[]{:S(2)}, u32[]{:S(2)}) %collective-permute-start.2) | collective-permute-done | bytes 81952 | tf_op jit(solution)/shard_map/ppermute | solution.py:158
  14.4 1.6 %collective-permute-start.3 = (f32[320,128]{1,0:T(8,128)S(1)}, f32[320,128]{1,0:T(8,128)S(1)}, u32[]{:S(2)}, u32[]{:S(2)}) collective-permute-start(f32[320,128]{1,0:T(8,128)S(1)} %pad_maximum_fusion.1), channel_id=1, source_target_pairs={{0,24},{1,25},{2,26},{3,27},{4,28},{5,29},{6,30},{7,31},{8,16},{9,... | collective-permute-start | bytes 491528 | tf_op jit(solution)/shard_map/ppermute | solution.py:158
  16.0 0.2 all-to-all-done.received_ref
  16.1 0.9 %shard_map.67 = f32[8,10,8,128]{3,2,1,0:T(8,128)} custom-call(f32[8,10,8,128]{3,2,1,0:T(8,128)S(1)} %all-to-all-done.received_ref), custom_call_target="tpu_custom_call" | custom-call | tf_op jit(solution)/shard_map/pallas_call | solution.py:162
  17.0 6.3 %all-to-all-start.1 = ((f32[8,10,8,128]{3,2,1,0:T(8,128)}), f32[8,10,8,128]{3,2,1,0:T(8,128)S(1)}, u32[]{:S(2)}, u32[]{:S(2)}) async-start(f32[8,10,8,128]{3,2,1,0:T(8,128)} %shard_map.67), calls=%async_computation.1 | async-start | bytes 655360 | tf_op jit(solution)/shard_map/all_to_all | solution.py:170
  23.3 0.0 collective-permute-done.3.refs_2_
  23.3 0.0 copy-start
  23.3 0.6 %collective-permute-start.4 = (f32[640,128]{1,0:T(8,128)S(1)}, f32[640,128]{1,0:T(8,128)S(1)}, u32[]{:S(2)}, u32[]{:S(2)}) collective-permute-start(f32[640,128]{1,0:T(8,128)S(1)} %pad_maximum_fusion), channel_id=1, source_target_pairs={{0,8},{1,5},{2,10},{3,7},{4,12},{5,1},{6,14},{7,3},{8,0},{9,13},{1... | collective-permute-start | bytes 983048 | tf_op jit(solution)/shard_map/ppermute | solution.py:158
  24.0 6.2 %all-to-all-done.1.trimmed_ref = f32[8,10,8,128]{3,2,1,0:T(8,128)S(1)} async-done(((f32[8,10,8,128]{3,2,1,0:T(8,128)}), f32[8,10,8,128]{3,2,1,0:T(8,128)S(1)}, u32[]{:S(2)}, u32[]{:S(2)}) %all-to-all-start.1) | async-done | bytes 327712 | tf_op jit(solution)/shard_map/all_to_all | solution.py:170
  30.2 0.1 shard_map.68
  30.3 0.1 collective-permute-start
  30.3 3.0 %collective-permute-done = f32[8,128]{1,0:T(8,128)S(1)} collective-permute-done((f32[8,128]{1,0:T(8,128)S(1)}, f32[8,128]{1,0:T(8,128)S(1)}, u32[]{:S(2)}, u32[]{:S(2)}) %collective-permute-start) | collective-permute-done | bytes 4128 | tf_op jit(solution)/shard_map/ppermute | solution.py:143
  33.4 0.1 collective-permute-start.1
  33.5 0.0 collective-permute-done.4.refs_3_
  33.5 0.0 copy-done
  33.5 0.5 %shard_map.69 = (f32[640,128]{1,0:T(8,128)S(1)}, f32[640,128]{1,0:T(8,128)S(1)}, f32[640,128]{1,0:T(8,128)S(1)}, f32[640,128]{1,0:T(8,128)S(1)}, f32[640,128]{1,0:T(8,128)S(1)}, /*index=5*/f32[80,128]{1,0:T(8,128)S(1)}) custom-call(s32[1]{0:T(128)} %bitcast.3.at_ref, f32[2,8,5120]{2,1,0:T(8,128)S(1)} %copy-done, f32[640,128]{1,0:T(8,128)S(1)} %bitcast.11, ...), custom_call_target="tpu_custom_call" | custom-call | tf_op jit(solution)/shard_map/pallas_call | solution.py:178
  34.0 0.5 %collective-permute-done.1 = f32[8,128]{1,0:T(8,128)S(1)} collective-permute-done((f32[8,128]{1,0:T(8,128)S(1)}, f32[8,128]{1,0:T(8,128)S(1)}, u32[]{:S(2)}, u32[]{:S(2)}) %collective-permute-start.1) | collective-permute-done | bytes 4128 | tf_op jit(solution)/shard_map/ppermute | solution.py:143
  34.5 1.0 %shard_map.70 = (f32[2,8,5120]{2,1,0:T(8,128)}, f32[80,128]{1,0:T(8,128)}, f32[80,128]{1,0:T(8,128)}) custom-call(f32[8,128]{1,0:T(8,128)S(1)} %add.10.squares_ref, f32[640,128]{1,0:T(8,128)S(1)} %get-tuple-element.12.kept_ref, f32[640,128]{1,0:T(8,128)S(1)} %get-tuple-element.13.one_ref, f32[640,128]{1,0:T(8,128)S(1)} %get-tuple-element.14.one_slope_ref, ...), custom_call_target="tpu_custom_call" | custom-call | tf_op jit(solution)/shard_map/pallas_call | solution.py:186
  (5 shorter events, 0.0 us)
Async XLA Ops:
  0.6 8.0 %copy-start.1 = (f32[2,1,5120]{2,1,0:T(1,128)S(1)}, f32[2,1,5120]{2,1,0:T(1,128)}, u32[]{:S(2)}) copy-start(f32[2,1,5120]{2,1,0:T(1,128)} %param.7) | copy-start | bytes 122884
  0.6 8.0 %copy-start.2 = (f32[2,1,5120]{2,1,0:T(1,128)S(1)}, f32[2,1,5120]{2,1,0:T(1,128)}, u32[]{:S(2)}) copy-start(f32[2,1,5120]{2,1,0:T(1,128)} %param.6) | copy-start | bytes 122884
  0.7 15.5 %all-to-all-start = ((f32[8,10,8,128]{3,2,1,0:T(8,128)}), f32[8,10,8,128]{3,2,1,0:T(8,128)S(1)}, u32[]{:S(2)}, u32[]{:S(2)}) async-start(f32[8,10,8,128]{3,2,1,0:T(8,128)} %bitcast.18), calls=%async_computation | async-start | bytes 655360 | tf_op jit(solution)/shard_map/all_to_all | solution.py:147
  8.6 5.8 %collective-permute-start.2 = (f32[160,128]{1,0:T(8,128)S(1)}, f32[160,128]{1,0:T(8,128)S(1)}, u32[]{:S(2)}, u32[]{:S(2)}) collective-permute-start(f32[160,128]{1,0:T(8,128)S(1)} %pad_maximum_fusion.2.refs_0_.own_moments_ref), channel_id=1, source_target_pairs={{0,4},{1,9},{2,6},{3,11},{4,0},{5,13},{6,2},{7,15},{8,12},{9,1},{1... | collective-permute-start | bytes 245768 | tf_op jit(solution)/shard_map/ppermute | solution.py:158
  14.4 8.9 %collective-permute-start.3 = (f32[320,128]{1,0:T(8,128)S(1)}, f32[320,128]{1,0:T(8,128)S(1)}, u32[]{:S(2)}, u32[]{:S(2)}) collective-permute-start(f32[320,128]{1,0:T(8,128)S(1)} %pad_maximum_fusion.1), channel_id=1, source_target_pairs={{0,24},{1,25},{2,26},{3,27},{4,28},{5,29},{6,30},{7,31},{8,16},{9,... | collective-permute-start | bytes 491528 | tf_op jit(solution)/shard_map/ppermute | solution.py:158
  17.0 13.1 %all-to-all-start.1 = ((f32[8,10,8,128]{3,2,1,0:T(8,128)}), f32[8,10,8,128]{3,2,1,0:T(8,128)S(1)}, u32[]{:S(2)}, u32[]{:S(2)}) async-start(f32[8,10,8,128]{3,2,1,0:T(8,128)} %shard_map.67), calls=%async_computation.1 | async-start | bytes 655360 | tf_op jit(solution)/shard_map/all_to_all | solution.py:170
  23.3 10.1 %copy-start = (f32[2,8,5120]{2,1,0:T(8,128)S(1)}, f32[2,8,5120]{2,1,0:T(8,128)}, u32[]{:S(2)}) copy-start(f32[2,8,5120]{2,1,0:T(8,128)} %weight_ref.1) | copy-start | bytes 983044
  23.3 10.1 %collective-permute-start.4 = (f32[640,128]{1,0:T(8,128)S(1)}, f32[640,128]{1,0:T(8,128)S(1)}, u32[]{:S(2)}, u32[]{:S(2)}) collective-permute-start(f32[640,128]{1,0:T(8,128)S(1)} %pad_maximum_fusion), channel_id=1, source_target_pairs={{0,8},{1,5},{2,10},{3,7},{4,12},{5,1},{6,14},{7,3},{8,0},{9,13},{1... | collective-permute-start | bytes 983048 | tf_op jit(solution)/shard_map/ppermute | solution.py:158
  30.3 3.1 %collective-permute-start = (f32[8,128]{1,0:T(8,128)S(1)}, f32[8,128]{1,0:T(8,128)S(1)}, u32[]{:S(2)}, u32[]{:S(2)}) collective-permute-start(f32[8,128]{1,0:T(8,128)S(1)} %shard_map.68), channel_id=1, source_target_pairs={{0,3},{1,2},{2,1},{3,0},{4,7},{5,6},{6,5},{7,4},{8,11},{9,10},{10,... | collective-permute-start | bytes 12296 | tf_op jit(solution)/shard_map/ppermute | solution.py:143
  33.4 1.2 %collective-permute-start.1 = (f32[8,128]{1,0:T(8,128)S(1)}, f32[8,128]{1,0:T(8,128)S(1)}, u32[]{:S(2)}, u32[]{:S(2)}) collective-permute-start(f32[8,128]{1,0:T(8,128)S(1)} %add.9), channel_id=1, source_target_pairs={{0,1},{1,0},{2,3},{3,2},{4,5},{5,4},{6,7},{7,6},{8,9},{9,8},{10,11... | collective-permute-start | bytes 12296 | tf_op jit(solution)/shard_map/ppermute | solution.py:143

commit v10 on v8

--- a/solution.py
+++ b/solution.py
@@ -89,10 +89,10 @@
                 at += SUB
 
 
-def adam_kernel(params, squares_ref, kept_ref, one_ref, one_slope_ref, two_ref, two_slope_ref, own_ref, own_moments_ref, *refs):
+def adam_kernel(params, squares_ref, others_ref, kept_ref, one_ref, one_slope_ref, two_ref, two_slope_ref, own_ref, own_moments_ref, *refs):
     outs, stages, done = refs[:3], refs[3:6], refs[6]
     new, new_one, new_two = stages
-    total = jnp.sum(squares_ref[...], keepdims=True)
+    total = jnp.sum(squares_ref[...] + others_ref[...], keepdims=True)
     factor = jnp.minimum(1.0, 1.0 / jnp.sqrt(total / params + 1e-12))
     square = factor * factor
     run = own_ref.shape[0]
@@ -164,8 +164,9 @@
     squares = pl.pallas_call(
         square_kernel, out_shape=f32(SUB, LANES), in_specs=[VMEM], out_specs=VMEM, compiler_params=PARAMS
     )(trimmed)
+    others = jnp.zeros_like(squares)
     for mask in [1] + [(1 << bit) + 1 for bit in range(1, (shards - 1).bit_length())]:
-        squares += swap(squares, "shard", mask)
+        squares, others = squares + others, swap(squares + others, "shard", mask)
     at = lax.axis_index(("rep", "shard")).reshape(1)
     flat = f32(weight.size // LANES, LANES)
     ready = pl.pallas_call(
@@ -179,7 +180,7 @@
     new_weight, one, two = pl.pallas_call(
         functools.partial(adam_kernel, params),
         out_shape=(f32(*weight.shape), f32(run, LANES), f32(run, LANES)),
-        in_specs=[VMEM] * 8,
+        in_specs=[VMEM] * 9,
         out_specs=(pl.BlockSpec(memory_space=pl.ANY),) * 3,
         scratch_shapes=[
             pltpu.VMEM(weight.shape, jnp.float32),
@@ -188,7 +189,7 @@
             pltpu.SemaphoreType.DMA((2 + blocks * (rows // SUB) * PARTS,)),
         ],
         compiler_params=PARAMS,
-    )(squares, *ready, moments[0])
+    )(squares, others, *ready, moments[0])
     return new_weight, one.reshape(moment_one.shape), two.reshape(moment_two.shape)
 
 

time: 35.8 us -> 35.8 us (level)
  no operation moved by 1% of the time
where the time goes in v10:
time: 35.8 us; the launch traced here: 35.4 us
  starting transfers between devices  19.4 us (54%)
  waiting for transfers between devices  12.8 us (36%)
  Pallas kernels  2.43 us (7%)
  between operations  0.69 us (2%)
    all_to_all x1, starting transfers between devices, on_device(): lax.all_to_all(tiled.reshape(count, tiles, SUB, LANES), 'rep', 0, 0, tile...  7.96 us
    all_to_all x1, starting transfers between devices, on_device(): lax.all_to_all(trimmed, 'rep', 0, 0, tiled=True, axis_index_groups=[order])  6.26 us
    all_to_all x1, waiting for transfers between devices, on_device(): lax.all_to_all(trimmed, 'rep', 0, 0, tiled=True, axis_index_groups=[order])  6.08 us
    ppermute x3, waiting for transfers between devices, spread(): moments.append(lax.ppermute(held, ('rep', 'shard'), pairs))  4.52 us
    ppermute x3, starting transfers between devices, spread(): moments.append(lax.ppermute(held, ('rep', 'shard'), pairs))  3.83 us
    ppermute x2, waiting for transfers between devices, swap(): lax.ppermute(value, axis, [(i, i ^ mask) for i in range(lax.axis_size(axi...  2.09 us
    ppermute x2, starting transfers between devices, swap(): lax.ppermute(value, axis, [(i, i ^ mask) for i in range(lax.axis_size(axi...  1.36 us
    pallas_call x1, Pallas kernels, on_device(): pl.pallas_call(functools.partial(adam_kernel, params), out_shape=(f32(*we...  1.02 us
  transfers between devices with their start and end apart: 7, of which 6 were waited for; matrix products, arithmetic and copies ran while one was open for 0% of the time, Pallas kernels for 4%

profile of v10, /device:TPU:0, one launch (start us, length us, event | category | flops | bytes accessed | tf_op | source)
XLA Modules:
  0.0 35.4 jit_solution(2201015957246785221)
XLA Ops:
  0.6 0.0 copy-start.1
  0.6 0.0 copy-start.2
  0.7 8.0 %all-to-all-start = ((f32[8,10,8,128]{3,2,1,0:T(8,128)}), f32[8,10,8,128]{3,2,1,0:T(8,128)S(1)}, u32[]{:S(2)}, u32[]{:S(2)}) async-start(f32[8,10,8,128]{3,2,1,0:T(8,128)} %bitcast.18), calls=%async_computation | async-start | bytes 655360 | tf_op jit(solution)/shard_map/all_to_all | solution.py:141
  8.6 0.0 copy-done.1
  8.6 0.0 copy-done.2
  8.6 1.5 %collective-permute-start.2 = (f32[160,128]{1,0:T(8,128)S(1)}, f32[160,128]{1,0:T(8,128)S(1)}, u32[]{:S(2)}, u32[]{:S(2)}) collective-permute-start(f32[160,128]{1,0:T(8,128)S(1)} %pad_maximum_fusion.2.refs_0_.own_moments_ref), channel_id=1, source_target_pairs={{0,4},{1,9},{2,6},{3,11},{4,0},{5,13},{6,2},{7,15},{8,12},{9,1},{1... | collective-permute-start | bytes 245768 | tf_op jit(solution)/shard_map/ppermute | solution.py:152
  10.2 4.3 %collective-permute-done.2.refs_1_ = f32[160,128]{1,0:T(8,128)S(1)} collective-permute-done((f32[160,128]{1,0:T(8,128)S(1)}, f32[160,128]{1,0:T(8,128)S(1)}, u32[]{:S(2)}, u32[]{:S(2)}) %collective-permute-start.2) | collective-permute-done | bytes 81952 | tf_op jit(solution)/shard_map/ppermute | solution.py:152
  14.4 1.6 %collective-permute-start.3 = (f32[320,128]{1,0:T(8,128)S(1)}, f32[320,128]{1,0:T(8,128)S(1)}, u32[]{:S(2)}, u32[]{:S(2)}) collective-permute-start(f32[320,128]{1,0:T(8,128)S(1)} %pad_maximum_fusion.1), channel_id=1, source_target_pairs={{0,24},{1,25},{2,26},{3,27},{4,28},{5,29},{6,30},{7,31},{8,16},{9,... | collective-permute-start | bytes 491528 | tf_op jit(solution)/shard_map/ppermute | solution.py:152
  16.0 0.2 all-to-all-done.received_ref
  16.1 0.8 %shard_map.67 = f32[8,10,8,128]{3,2,1,0:T(8,128)} custom-call(f32[8,10,8,128]{3,2,1,0:T(8,128)S(1)} %all-to-all-done.received_ref), custom_call_target="tpu_custom_call" | custom-call | tf_op jit(solution)/shard_map/pallas_call | solution.py:156
  16.9 6.3 %all-to-all-start.1 = ((f32[8,10,8,128]{3,2,1,0:T(8,128)}), f32[8,10,8,128]{3,2,1,0:T(8,128)S(1)}, u32[]{:S(2)}, u32[]{:S(2)}) async-start(f32[8,10,8,128]{3,2,1,0:T(8,128)} %shard_map.67), calls=%async_computation.1 | async-start | bytes 655360 | tf_op jit(solution)/shard_map/all_to_all | solution.py:163
  23.2 0.0 collective-permute-done.3.refs_2_
  23.2 0.0 copy-start
  23.2 0.7 %collective-permute-start.4 = (f32[640,128]{1,0:T(8,128)S(1)}, f32[640,128]{1,0:T(8,128)S(1)}, u32[]{:S(2)}, u32[]{:S(2)}) collective-permute-start(f32[640,128]{1,0:T(8,128)S(1)} %pad_maximum_fusion), channel_id=1, source_target_pairs={{0,8},{1,5},{2,10},{3,7},{4,12},{5,1},{6,14},{7,3},{8,0},{9,13},{1... | collective-permute-start | bytes 983048 | tf_op jit(solution)/shard_map/ppermute | solution.py:152
  24.0 6.1 %all-to-all-done.1.trimmed_ref = f32[8,10,8,128]{3,2,1,0:T(8,128)S(1)} async-done(((f32[8,10,8,128]{3,2,1,0:T(8,128)}), f32[8,10,8,128]{3,2,1,0:T(8,128)S(1)}, u32[]{:S(2)}, u32[]{:S(2)}) %all-to-all-start.1) | async-done | bytes 327712 | tf_op jit(solution)/shard_map/all_to_all | solution.py:163
  30.1 0.1 shard_map.68
  30.1 0.1 collective-permute-start
  30.2 1.2 %collective-permute-done = f32[8,128]{1,0:T(8,128)S(1)} collective-permute-done((f32[8,128]{1,0:T(8,128)S(1)}, f32[8,128]{1,0:T(8,128)S(1)}, u32[]{:S(2)}, u32[]{:S(2)}) %collective-permute-start) | collective-permute-done | bytes 4128 | tf_op jit(solution)/shard_map/ppermute | solution.py:137
  31.4 1.3 %collective-permute-start.1 = (f32[8,128]{1,0:T(8,128)S(1)}, f32[8,128]{1,0:T(8,128)S(1)}, u32[]{:S(2)}, u32[]{:S(2)}) collective-permute-start(f32[8,128]{1,0:T(8,128)S(1)} %add.7.squares_ref), channel_id=1, source_target_pairs={{0,3},{1,2},{2,1},{3,0},{4,7},{5,6},{6,5},{7,4},{8,11},{9,10},{10,... | collective-permute-start | bytes 12296 | tf_op jit(solution)/shard_map/ppermute | solution.py:137
  32.7 0.2 collective-permute-done.4.refs_3_
  32.9 0.0 copy-done
  32.9 0.5 %shard_map.69 = (f32[640,128]{1,0:T(8,128)S(1)}, f32[640,128]{1,0:T(8,128)S(1)}, f32[640,128]{1,0:T(8,128)S(1)}, f32[640,128]{1,0:T(8,128)S(1)}, f32[640,128]{1,0:T(8,128)S(1)}, /*index=5*/f32[80,128]{1,0:T(8,128)S(1)}) custom-call(s32[1]{0:T(128)} %bitcast.3.at_ref, f32[2,8,5120]{2,1,0:T(8,128)S(1)} %copy-done, f32[640,128]{1,0:T(8,128)S(1)} %bitcast.11, ...), custom_call_target="tpu_custom_call" | custom-call | tf_op jit(solution)/shard_map/pallas_call | solution.py:172
  33.5 0.9 %collective-permute-done.1.others_ref = f32[8,128]{1,0:T(8,128)S(1)} collective-permute-done((f32[8,128]{1,0:T(8,128)S(1)}, f32[8,128]{1,0:T(8,128)S(1)}, u32[]{:S(2)}, u32[]{:S(2)}) %collective-permute-start.1) | collective-permute-done | bytes 4128 | tf_op jit(solution)/shard_map/ppermute | solution.py:137
  34.4 1.0 %shard_map.70 = (f32[2,8,5120]{2,1,0:T(8,128)}, f32[80,128]{1,0:T(8,128)}, f32[80,128]{1,0:T(8,128)}) custom-call(f32[8,128]{1,0:T(8,128)S(1)} %add.7.squares_ref, f32[8,128]{1,0:T(8,128)S(1)} %collective-permute-done.1.others_ref, f32[640,128]{1,0:T(8,128)S(1)} %get-tuple-element.12.kept_ref, f32[640,128]{1,0:T(8,128)S(1)} %get-tuple-element.13.one_ref, ...), custom_call_target="tpu_custom_call" | custom-call | tf_op jit(solution)/shard_map/pallas_call | solution.py:180
  (4 shorter events, 0.0 us)
Async XLA Ops:
  0.6 8.0 %copy-start.1 = (f32[2,1,5120]{2,1,0:T(1,128)S(1)}, f32[2,1,5120]{2,1,0:T(1,128)}, u32[]{:S(2)}) copy-start(f32[2,1,5120]{2,1,0:T(1,128)} %param.7) | copy-start | bytes 122884
  0.6 8.0 %copy-start.2 = (f32[2,1,5120]{2,1,0:T(1,128)S(1)}, f32[2,1,5120]{2,1,0:T(1,128)}, u32[]{:S(2)}) copy-start(f32[2,1,5120]{2,1,0:T(1,128)} %param.6) | copy-start | bytes 122884
  0.7 15.5 %all-to-all-start = ((f32[8,10,8,128]{3,2,1,0:T(8,128)}), f32[8,10,8,128]{3,2,1,0:T(8,128)S(1)}, u32[]{:S(2)}, u32[]{:S(2)}) async-start(f32[8,10,8,128]{3,2,1,0:T(8,128)} %bitcast.18), calls=%async_computation | async-start | bytes 655360 | tf_op jit(solution)/shard_map/all_to_all | solution.py:141
  8.6 5.8 %collective-permute-start.2 = (f32[160,128]{1,0:T(8,128)S(1)}, f32[160,128]{1,0:T(8,128)S(1)}, u32[]{:S(2)}, u32[]{:S(2)}) collective-permute-start(f32[160,128]{1,0:T(8,128)S(1)} %pad_maximum_fusion.2.refs_0_.own_moments_ref), channel_id=1, source_target_pairs={{0,4},{1,9},{2,6},{3,11},{4,0},{5,13},{6,2},{7,15},{8,12},{9,1},{1... | collective-permute-start | bytes 245768 | tf_op jit(solution)/shard_map/ppermute | solution.py:152
  14.4 8.7 %collective-permute-start.3 = (f32[320,128]{1,0:T(8,128)S(1)}, f32[320,128]{1,0:T(8,128)S(1)}, u32[]{:S(2)}, u32[]{:S(2)}) collective-permute-start(f32[320,128]{1,0:T(8,128)S(1)} %pad_maximum_fusion.1), channel_id=1, source_target_pairs={{0,24},{1,25},{2,26},{3,27},{4,28},{5,29},{6,30},{7,31},{8,16},{9,... | collective-permute-start | bytes 491528 | tf_op jit(solution)/shard_map/ppermute | solution.py:152
  16.9 13.1 %all-to-all-start.1 = ((f32[8,10,8,128]{3,2,1,0:T(8,128)}), f32[8,10,8,128]{3,2,1,0:T(8,128)S(1)}, u32[]{:S(2)}, u32[]{:S(2)}) async-start(f32[8,10,8,128]{3,2,1,0:T(8,128)} %shard_map.67), calls=%async_computation.1 | async-start | bytes 655360 | tf_op jit(solution)/shard_map/all_to_all | solution.py:163
  23.2 9.7 %copy-start = (f32[2,8,5120]{2,1,0:T(8,128)S(1)}, f32[2,8,5120]{2,1,0:T(8,128)}, u32[]{:S(2)}) copy-start(f32[2,8,5120]{2,1,0:T(8,128)} %weight_ref.1) | copy-start | bytes 983044
  23.2 9.7 %collective-permute-start.4 = (f32[640,128]{1,0:T(8,128)S(1)}, f32[640,128]{1,0:T(8,128)S(1)}, u32[]{:S(2)}, u32[]{:S(2)}) collective-permute-start(f32[640,128]{1,0:T(8,128)S(1)} %pad_maximum_fusion), channel_id=1, source_target_pairs={{0,8},{1,5},{2,10},{3,7},{4,12},{5,1},{6,14},{7,3},{8,0},{9,13},{1... | collective-permute-start | bytes 983048 | tf_op jit(solution)/shard_map/ppermute | solution.py:152
  30.1 1.2 %collective-permute-start = (f32[8,128]{1,0:T(8,128)S(1)}, f32[8,128]{1,0:T(8,128)S(1)}, u32[]{:S(2)}, u32[]{:S(2)}) collective-permute-start(f32[8,128]{1,0:T(8,128)S(1)} %shard_map.68), channel_id=1, source_target_pairs={{0,1},{1,0},{2,3},{3,2},{4,5},{5,4},{6,7},{7,6},{8,9},{9,8},{10,11... | collective-permute-start | bytes 12296 | tf_op jit(solution)/shard_map/ppermute | solution.py:137
  31.4 3.0 %collective-permute-start.1 = (f32[8,128]{1,0:T(8,128)S(1)}, f32[8,128]{1,0:T(8,128)S(1)}, u32[]{:S(2)}, u32[]{:S(2)}) collective-permute-start(f32[8,128]{1,0:T(8,128)S(1)} %add.7.squares_ref), channel_id=1, source_target_pairs={{0,3},{1,2},{2,1},{3,0},{4,7},{5,6},{6,5},{7,4},{8,11},{9,10},{10,... | collective-permute-start | bytes 12296 | tf_op jit(solution)/shard_map/ppermute | solution.py:137

commit v11 on v10

--- a/solution.py
+++ b/solution.py
@@ -10,7 +10,7 @@
 
 STEP = 100
 LANES = 128
-PARTS = 4
+PARTS = 2
 SUB = 8
 VMEM = pl.BlockSpec(memory_space=pltpu.VMEM)
 SMEM = pl.BlockSpec(memory_space=pltpu.SMEM)

time: 35.8 us -> 35.8 us (level)
  no operation moved by 1% of the time
where the time goes in v11:
time: 35.8 us; the launch traced here: 35.4 us
  starting transfers between devices  19.4 us (54%)
  waiting for transfers between devices  12.8 us (36%)
  Pallas kernels  2.41 us (7%)
  between operations  0.69 us (2%)
    all_to_all x1, starting transfers between devices, on_device(): lax.all_to_all(tiled.reshape(count, tiles, SUB, LANES), 'rep', 0, 0, tile...  7.96 us
    all_to_all x1, starting transfers between devices, on_device(): lax.all_to_all(trimmed, 'rep', 0, 0, tiled=True, axis_index_groups=[order])  6.26 us
    all_to_all x1, waiting for transfers between devices, on_device(): lax.all_to_all(trimmed, 'rep', 0, 0, tiled=True, axis_index_groups=[order])  6.08 us
    ppermute x3, waiting for transfers between devices, spread(): moments.append(lax.ppermute(held, ('rep', 'shard'), pairs))  4.52 us
    ppermute x3, starting transfers between devices, spread(): moments.append(lax.ppermute(held, ('rep', 'shard'), pairs))  3.83 us
    ppermute x2, waiting for transfers between devices, swap(): lax.ppermute(value, axis, [(i, i ^ mask) for i in range(lax.axis_size(axi...  2.09 us
    ppermute x2, starting transfers between devices, swap(): lax.ppermute(value, axis, [(i, i ^ mask) for i in range(lax.axis_size(axi...  1.36 us
    pallas_call x1, Pallas kernels, on_device(): pl.pallas_call(functools.partial(adam_kernel, params), out_shape=(f32(*we...  1 us
  transfers between devices with their start and end apart: 7, of which 6 were waited for; matrix products, arithmetic and copies ran while one was open for 0% of the time, Pallas kernels for 4%

profile of v11, /device:TPU:0, one launch (start us, length us, event | category | flops | bytes accessed | tf_op | source)
XLA Modules:
  0.0 35.4 jit_solution(16075815483901831666)
XLA Ops:
  0.6 0.0 copy-start.1
  0.6 0.0 copy-start.2
  0.7 8.0 %all-to-all-start = ((f32[8,10,8,128]{3,2,1,0:T(8,128)}), f32[8,10,8,128]{3,2,1,0:T(8,128)S(1)}, u32[]{:S(2)}, u32[]{:S(2)}) async-start(f32[8,10,8,128]{3,2,1,0:T(8,128)} %bitcast.18), calls=%async_computation | async-start | bytes 655360 | tf_op jit(solution)/shard_map/all_to_all | solution.py:141
  8.6 0.0 copy-done.1
  8.6 0.0 copy-done.2
  8.6 1.5 %collective-permute-start.2 = (f32[160,128]{1,0:T(8,128)S(1)}, f32[160,128]{1,0:T(8,128)S(1)}, u32[]{:S(2)}, u32[]{:S(2)}) collective-permute-start(f32[160,128]{1,0:T(8,128)S(1)} %pad_maximum_fusion.2.refs_0_.own_moments_ref), channel_id=1, source_target_pairs={{0,4},{1,9},{2,6},{3,11},{4,0},{5,13},{6,2},{7,15},{8,12},{9,1},{1... | collective-permute-start | bytes 245768 | tf_op jit(solution)/shard_map/ppermute | solution.py:152
  10.2 4.3 %collective-permute-done.2.refs_1_ = f32[160,128]{1,0:T(8,128)S(1)} collective-permute-done((f32[160,128]{1,0:T(8,128)S(1)}, f32[160,128]{1,0:T(8,128)S(1)}, u32[]{:S(2)}, u32[]{:S(2)}) %collective-permute-start.2) | collective-permute-done | bytes 81952 | tf_op jit(solution)/shard_map/ppermute | solution.py:152
  14.4 1.6 %collective-permute-start.3 = (f32[320,128]{1,0:T(8,128)S(1)}, f32[320,128]{1,0:T(8,128)S(1)}, u32[]{:S(2)}, u32[]{:S(2)}) collective-permute-start(f32[320,128]{1,0:T(8,128)S(1)} %pad_maximum_fusion.1), channel_id=1, source_target_pairs={{0,24},{1,25},{2,26},{3,27},{4,28},{5,29},{6,30},{7,31},{8,16},{9,... | collective-permute-start | bytes 491528 | tf_op jit(solution)/shard_map/ppermute | solution.py:152
  16.0 0.2 all-to-all-done.received_ref
  16.1 0.8 %shard_map.67 = f32[8,10,8,128]{3,2,1,0:T(8,128)} custom-call(f32[8,10,8,128]{3,2,1,0:T(8,128)S(1)} %all-to-all-done.received_ref), custom_call_target="tpu_custom_call" | custom-call | tf_op jit(solution)/shard_map/pallas_call | solution.py:156
  16.9 6.3 %all-to-all-start.1 = ((f32[8,10,8,128]{3,2,1,0:T(8,128)}), f32[8,10,8,128]{3,2,1,0:T(8,128)S(1)}, u32[]{:S(2)}, u32[]{:S(2)}) async-start(f32[8,10,8,128]{3,2,1,0:T(8,128)} %shard_map.67), calls=%async_computation.1 | async-start | bytes 655360 | tf_op jit(solution)/shard_map/all_to_all | solution.py:163
  23.2 0.0 collective-permute-done.3.refs_2_
  23.2 0.0 copy-start
  23.2 0.7 %collective-permute-start.4 = (f32[640,128]{1,0:T(8,128)S(1)}, f32[640,128]{1,0:T(8,128)S(1)}, u32[]{:S(2)}, u32[]{:S(2)}) collective-permute-start(f32[640,128]{1,0:T(8,128)S(1)} %pad_maximum_fusion), channel_id=1, source_target_pairs={{0,8},{1,5},{2,10},{3,7},{4,12},{5,1},{6,14},{7,3},{8,0},{9,13},{1... | collective-permute-start | bytes 983048 | tf_op jit(solution)/shard_map/ppermute | solution.py:152
  24.0 6.1 %all-to-all-done.1.trimmed_ref = f32[8,10,8,128]{3,2,1,0:T(8,128)S(1)} async-done(((f32[8,10,8,128]{3,2,1,0:T(8,128)}), f32[8,10,8,128]{3,2,1,0:T(8,128)S(1)}, u32[]{:S(2)}, u32[]{:S(2)}) %all-to-all-start.1) | async-done | bytes 327712 | tf_op jit(solution)/shard_map/all_to_all | solution.py:163
  30.1 0.1 shard_map.68
  30.1 0.1 collective-permute-start
  30.2 1.2 %collective-permute-done = f32[8,128]{1,0:T(8,128)S(1)} collective-permute-done((f32[8,128]{1,0:T(8,128)S(1)}, f32[8,128]{1,0:T(8,128)S(1)}, u32[]{:S(2)}, u32[]{:S(2)}) %collective-permute-start) | collective-permute-done | bytes 4128 | tf_op jit(solution)/shard_map/ppermute | solution.py:137
  31.4 1.3 %collective-permute-start.1 = (f32[8,128]{1,0:T(8,128)S(1)}, f32[8,128]{1,0:T(8,128)S(1)}, u32[]{:S(2)}, u32[]{:S(2)}) collective-permute-start(f32[8,128]{1,0:T(8,128)S(1)} %add.7.squares_ref), channel_id=1, source_target_pairs={{0,3},{1,2},{2,1},{3,0},{4,7},{5,6},{6,5},{7,4},{8,11},{9,10},{10,... | collective-permute-start | bytes 12296 | tf_op jit(solution)/shard_map/ppermute | solution.py:137
  32.7 0.2 collective-permute-done.4.refs_3_
  32.9 0.0 copy-done
  32.9 0.5 %shard_map.69 = (f32[640,128]{1,0:T(8,128)S(1)}, f32[640,128]{1,0:T(8,128)S(1)}, f32[640,128]{1,0:T(8,128)S(1)}, f32[640,128]{1,0:T(8,128)S(1)}, f32[640,128]{1,0:T(8,128)S(1)}, /*index=5*/f32[80,128]{1,0:T(8,128)S(1)}) custom-call(s32[1]{0:T(128)} %bitcast.3.at_ref, f32[2,8,5120]{2,1,0:T(8,128)S(1)} %copy-done, f32[640,128]{1,0:T(8,128)S(1)} %bitcast.11, ...), custom_call_target="tpu_custom_call" | custom-call | tf_op jit(solution)/shard_map/pallas_call | solution.py:172
  33.5 0.9 %collective-permute-done.1.others_ref = f32[8,128]{1,0:T(8,128)S(1)} collective-permute-done((f32[8,128]{1,0:T(8,128)S(1)}, f32[8,128]{1,0:T(8,128)S(1)}, u32[]{:S(2)}, u32[]{:S(2)}) %collective-permute-start.1) | collective-permute-done | bytes 4128 | tf_op jit(solution)/shard_map/ppermute | solution.py:137
  34.4 1.0 %shard_map.70 = (f32[2,8,5120]{2,1,0:T(8,128)}, f32[80,128]{1,0:T(8,128)}, f32[80,128]{1,0:T(8,128)}) custom-call(f32[8,128]{1,0:T(8,128)S(1)} %add.7.squares_ref, f32[8,128]{1,0:T(8,128)S(1)} %collective-permute-done.1.others_ref, f32[640,128]{1,0:T(8,128)S(1)} %get-tuple-element.12.kept_ref, f32[640,128]{1,0:T(8,128)S(1)} %get-tuple-element.13.one_ref, ...), custom_call_target="tpu_custom_call" | custom-call | tf_op jit(solution)/shard_map/pallas_call | solution.py:180
  (4 shorter events, 0.0 us)
Async XLA Ops:
  0.6 8.0 %copy-start.1 = (f32[2,1,5120]{2,1,0:T(1,128)S(1)}, f32[2,1,5120]{2,1,0:T(1,128)}, u32[]{:S(2)}) copy-start(f32[2,1,5120]{2,1,0:T(1,128)} %param.7) | copy-start | bytes 122884
  0.6 8.0 %copy-start.2 = (f32[2,1,5120]{2,1,0:T(1,128)S(1)}, f32[2,1,5120]{2,1,0:T(1,128)}, u32[]{:S(2)}) copy-start(f32[2,1,5120]{2,1,0:T(1,128)} %param.6) | copy-start | bytes 122884
  0.7 15.5 %all-to-all-start = ((f32[8,10,8,128]{3,2,1,0:T(8,128)}), f32[8,10,8,128]{3,2,1,0:T(8,128)S(1)}, u32[]{:S(2)}, u32[]{:S(2)}) async-start(f32[8,10,8,128]{3,2,1,0:T(8,128)} %bitcast.18), calls=%async_computation | async-start | bytes 655360 | tf_op jit(solution)/shard_map/all_to_all | solution.py:141
  8.6 5.8 %collective-permute-start.2 = (f32[160,128]{1,0:T(8,128)S(1)}, f32[160,128]{1,0:T(8,128)S(1)}, u32[]{:S(2)}, u32[]{:S(2)}) collective-permute-start(f32[160,128]{1,0:T(8,128)S(1)} %pad_maximum_fusion.2.refs_0_.own_moments_ref), channel_id=1, source_target_pairs={{0,4},{1,9},{2,6},{3,11},{4,0},{5,13},{6,2},{7,15},{8,12},{9,1},{1... | collective-permute-start | bytes 245768 | tf_op jit(solution)/shard_map/ppermute | solution.py:152
  14.4 8.7 %collective-permute-start.3 = (f32[320,128]{1,0:T(8,128)S(1)}, f32[320,128]{1,0:T(8,128)S(1)}, u32[]{:S(2)}, u32[]{:S(2)}) collective-permute-start(f32[320,128]{1,0:T(8,128)S(1)} %pad_maximum_fusion.1), channel_id=1, source_target_pairs={{0,24},{1,25},{2,26},{3,27},{4,28},{5,29},{6,30},{7,31},{8,16},{9,... | collective-permute-start | bytes 491528 | tf_op jit(solution)/shard_map/ppermute | solution.py:152
  16.9 13.1 %all-to-all-start.1 = ((f32[8,10,8,128]{3,2,1,0:T(8,128)}), f32[8,10,8,128]{3,2,1,0:T(8,128)S(1)}, u32[]{:S(2)}, u32[]{:S(2)}) async-start(f32[8,10,8,128]{3,2,1,0:T(8,128)} %shard_map.67), calls=%async_computation.1 | async-start | bytes 655360 | tf_op jit(solution)/shard_map/all_to_all | solution.py:163
  23.2 9.7 %copy-start = (f32[2,8,5120]{2,1,0:T(8,128)S(1)}, f32[2,8,5120]{2,1,0:T(8,128)}, u32[]{:S(2)}) copy-start(f32[2,8,5120]{2,1,0:T(8,128)} %weight_ref.1) | copy-start | bytes 983044
  23.2 9.7 %collective-permute-start.4 = (f32[640,128]{1,0:T(8,128)S(1)}, f32[640,128]{1,0:T(8,128)S(1)}, u32[]{:S(2)}, u32[]{:S(2)}) collective-permute-start(f32[640,128]{1,0:T(8,128)S(1)} %pad_maximum_fusion), channel_id=1, source_target_pairs={{0,8},{1,5},{2,10},{3,7},{4,12},{5,1},{6,14},{7,3},{8,0},{9,13},{1... | collective-permute-start | bytes 983048 | tf_op jit(solution)/shard_map/ppermute | solution.py:152
  30.1 1.2 %collective-permute-start = (f32[8,128]{1,0:T(8,128)S(1)}, f32[8,128]{1,0:T(8,128)S(1)}, u32[]{:S(2)}, u32[]{:S(2)}) collective-permute-start(f32[8,128]{1,0:T(8,128)S(1)} %shard_map.68), channel_id=1, source_target_pairs={{0,1},{1,0},{2,3},{3,2},{4,5},{5,4},{6,7},{7,6},{8,9},{9,8},{10,11... | collective-permute-start | bytes 12296 | tf_op jit(solution)/shard_map/ppermute | solution.py:137
  31.4 3.0 %collective-permute-start.1 = (f32[8,128]{1,0:T(8,128)S(1)}, f32[8,128]{1,0:T(8,128)S(1)}, u32[]{:S(2)}, u32[]{:S(2)}) collective-permute-start(f32[8,128]{1,0:T(8,128)S(1)} %add.7.squares_ref), channel_id=1, source_target_pairs={{0,3},{1,2},{2,1},{3,0},{4,7},{5,6},{6,5},{7,4},{8,11},{9,10},{10,... | collective-permute-start | bytes 12296 | tf_op jit(solution)/shard_map/ppermute | solution.py:137
